TPU v7x, 128 devices: a whole 4x4x4 slice. The times are simulated.
128 devices in a mesh: lat: 4 (over z_hi, core), lon: 32 (over z_lo, x, y).
Axes of the slice: x: 4, y: 4, z: 4 (z_hi: 2, z_lo: 2; z = z_hi * 2 + z_lo), core: 2. Of those that a mesh axis runs over, the one named last changes fastest.
Arguments:
- adjoint_in: float32 [3, 72, 1440, 512], P(None, None, 'lon', 'lat'), may hold values from -6 to 6
- courant_lon: float32 [72, 1440, 512], P(None, 'lon', 'lat'), may hold values from -0.2 to 0.2
- courant_lat: float32 [72, 1440, 512], P(None, 'lon', 'lat'), may hold values from -0.2 to 0.2
- vertical_mix: float32 [72, 72], replicated, may hold values from -0.375 to 0.375
- sounding_values: float32 [20, 1048576], P(None, ('lat', 'lon')), may hold values from -6 to 6
- sounding_dest: int32 [1048576, 1], P(('lat', 'lon')), may hold values from 0 to 127; in each aligned block of 8192 rows (0 to 8191, 8192 to 16383, ...) at most 128 rows name the same one
- sounding_target: int32 [1048576], P(('lat', 'lon')), may hold values from 0 to 17279
- level_index: int32 [20], replicated, may hold values from 0 to 71
Outputs:
- adjoint_out: float32 [3, 72, 1440, 512], P(None, None, 'lon', 'lat')
- flux_grad: float32 [3, 1440, 512], P(None, 'lon', 'lat')
Inputs may be any that keep to these rules, and one draw needn't show every extreme that they name: `sounding_dest`: among the rows of one device, at most 128 name the same tile, a bound that some block reaches of them.
All inputs are finite; a program needn't handle non-finite values.
Results may differ from a plain program's by a relative error of at most 0.000065.
Values sent between devices are 32-bit elements; how exact they have to be, the bound alone decides.
No kernel may reach another device: no remote copies, remote signals or barrier semaphores. Data moves between devices by JAX's collectives and lax.ppermute only.
A program may use at most 128 MiB of HBM per device.

v0:
```python
import jax
import jax.numpy as jnp
from jax import lax
from jax.sharding import PartitionSpec as P

kappa_mix = 0.05


def with_halo(value, sides, width, wrap):
    for axis, dim in sides:
        size, length = (lax.axis_size(axis), value.shape[dim])
        up = [(i, (i + 1) % size) for i in range(size if wrap else size - 1)]
        down = [(j, i) for i, j in up]
        last = lax.slice_in_dim(value, length - width, length, axis=dim)
        initial = lax.slice_in_dim(value, 0, width, axis=dim)
        before = lax.ppermute(last, axis, up)
        after = lax.ppermute(initial, axis, down)
        value = jnp.concatenate([before, value, after], axis=dim)
    return value


def shifted(value, axis, by):
    size = lax.axis_size(axis)
    return lax.ppermute(value, axis, [(i, (i + by) % size) for i in range(size)])


def passed_along(block, axis, distance):
    devices = range(lax.axis_size(axis))
    route = [(i - distance, i) for i in devices if i - distance in devices]
    return lax.ppermute(block, axis, route)


def advance(field, east_coef, west_coef, north_coef, south_coef):
    wide = with_halo(field, (("lon", 2),), 1, True)
    tall = with_halo(field, (("lat", 3),), 1, False)
    east = wide[:, :, 2:, :]
    west = wide[:, :, :-2, :]
    north = tall[..., 2:]
    south = tall[..., :-2]
    return (
        field
        + east_coef * (east - field)
        + west_coef * (field - west)
        + north_coef * (north - field)
        + south_coef * (field - south)
    )


def mixing(field, matrix):
    return jnp.einsum("lm,slxy->smxy", matrix, field, precision=lax.Precision.HIGHEST)


def on_device(
    adjoint_in,
    courant_lon,
    courant_lat,
    vertical_mix,
    sounding_values,
    sounding_dest,
    sounding_target,
    level_index,
):
    lat_size = lax.axis_size("lat")
    lon_size = lax.axis_size("lon")
    n_tiles = lat_size * lon_size
    kernel_levels, row_count = sounding_values.shape
    capacity = 2 * row_count // n_tiles
    species_count, levels_count, tile_cols, tile_rows = adjoint_in.shape
    cell_count = tile_rows * tile_cols
    destination = sounding_dest[:, 0]
    onehot = (destination[:, None] == jnp.arange(n_tiles, dtype=jnp.int32)[None, :]).astype(
        jnp.int32
    )
    earlier = jnp.cumsum(onehot, axis=0) - onehot
    slot_index = jnp.sum(earlier * onehot, axis=1)
    position = destination * capacity + slot_index
    source_row = (
        jnp.full((n_tiles * capacity,), row_count, jnp.int32)
        .at[position]
        .set(jnp.arange(row_count, dtype=jnp.int32))
    )
    send_values = jnp.take(sounding_values, source_row, axis=1, mode="fill", fill_value=0.0)
    send_target = jnp.take(sounding_target, source_row, axis=0, mode="fill", fill_value=0)
    got_values, got_target = (
        lax.all_to_all(
            send_values.reshape(kernel_levels, n_tiles, capacity),
            ("lat", "lon"),
            split_axis=1,
            concat_axis=1,
            tiled=True,
        ),
        lax.all_to_all(
            send_target.reshape(1, n_tiles, capacity),
            ("lat", "lon"),
            split_axis=1,
            concat_axis=1,
            tiled=True,
        ),
    )
    got_values = got_values.reshape(kernel_levels, n_tiles * capacity)
    got_target = got_target.reshape(n_tiles * capacity)
    cell = got_target // species_count
    tracer = got_target % species_count
    segment = tracer * cell_count + cell % tile_cols * tile_rows + cell // tile_cols
    gathered = (
        jnp.zeros((kernel_levels, species_count * cell_count), jnp.float32)
        .at[:, segment]
        .add(got_values)
    )
    level_table = (
        level_index[:, None] == jnp.arange(levels_count, dtype=jnp.int32)[None, :]
    ).astype(jnp.float32)
    forcing = jnp.einsum(
        "kl,ksc->slc",
        level_table,
        gathered.reshape(kernel_levels, species_count, cell_count),
        precision=lax.Precision.HIGHEST,
    ).reshape(species_count, levels_count, tile_cols, tile_rows)
    west_rim = shifted(courant_lon[:, -1:, :], "lon", 1)
    south_rim = passed_along(courant_lat[:, :, -1:], "lat", 1)
    west_courant = jnp.concatenate([west_rim, courant_lon[:, :-1, :]], axis=1)
    south_courant = jnp.concatenate([south_rim, courant_lat[:, :, :-1]], axis=2)
    grid_rows = tile_rows * lat_size
    lat_global = lax.axis_index("lat") * tile_rows + jnp.arange(tile_rows, dtype=jnp.int32)
    inside = (lat_global <= grid_rows - 2).astype(jnp.float32)[None, None, :]
    below = (lat_global >= 1).astype(jnp.float32)[None, None, :]
    east_coef = jnp.maximum(courant_lon, 0.0) + kappa_mix
    west_coef = jnp.minimum(west_courant, 0.0) - kappa_mix
    north_coef = (jnp.maximum(courant_lat, 0.0) + kappa_mix) * inside
    south_coef = (jnp.minimum(south_courant, 0.0) - kappa_mix) * below
    matrix = jnp.eye(levels_count, dtype=jnp.float32) + vertical_mix
    first = (
        mixing(advance(adjoint_in, east_coef, west_coef, north_coef, south_coef), matrix) + forcing
    )
    second = mixing(advance(first, east_coef, west_coef, north_coef, south_coef), matrix)
    return (second, first[:, 0] + second[:, 0])


def solution(mesh):
    return jax.shard_map(
        on_device,
        mesh=mesh,
        in_specs=(
            P(None, None, "lon", "lat"),
            P(None, "lon", "lat"),
            P(None, "lon", "lat"),
            P(),
            P(None, ("lat", "lon")),
            P(("lat", "lon"), None),
            P(("lat", "lon")),
            P(),
        ),
        out_specs=(P(None, None, "lon", "lat"), P(None, "lon", "lat")),
        check_vma=False,
    )
```

profile of v0, /device:TPU:1, one launch (start us, length us, event | category | flops | bytes accessed | tf_op | source)
XLA Modules:
  0.0 514.4 jit_solution(13371289101370548757)
XLA Ops:
  0.6 0.0 copy-start
  0.7 1.4 slice.82
  2.0 2.1 collective-permute-start.1
  4.2 1.7 fusion.82
  5.8 5.0 collective-permute-start
  10.8 1.9 slice.88
  12.7 1.2 copy.67
  13.9 6.0 %collective-permute-start.4 = (f32[72,45,1]{0,1,2:T(8,128)}, f32[72,45,1]{0,1,2:T(8,128)}, u32[]{:S(2)}, u32[]{:S(2)}) collective-permute-start(f32[72,45,1]{0,1,2:T(8,128)} %copy.67), channel_id=1, source_target_pairs={{0,32},{32,64},{64,96},{1,33},{33,65},{65,97},{2,34},{34,66},{66,9... | collective-permute-start | bytes 38888 | tf_op jit(solution)/shard_map/ppermute | solution.py:30
  20.0 0.1 copy.47
  20.1 1.1 fusion.46
  21.2 0.0 copy-start.2
  21.2 2.0 copy-done.2
  23.3 0.1 reduce-window.9
  23.4 2.6 broadcast_add_fusion
  26.0 2.4 copy.48
  28.4 2.8 fusion.45
  31.3 0.1 compare_select_fusion.1
  31.3 30.5 %scatter_custom_fusion = s32[16384]{0:T(1024)S(1)} fusion(s32[8192]{0:T(1024)S(1)} %bitcast.82, s32[8192]{0:T(1024)S(1)} %iota.35, s32[]{:T(128)} %constant.82.clone.1), kind=kCustom, calls=%fused_computation.98 | custom fusion | bytes 65540 | tf_op jit(solution)/shard_map/scatter | solution.py:80
  61.9 90.5 %gather_fusion = s32[16384]{0:T(1024)S(1)} fusion(s32[8192]{0:T(1024)S(1)} %copy-done, s32[16384]{0:T(1024)S(1)} %fusion.70), kind=kCustom, calls=%fused_computation | custom fusion | bytes 196608 | tf_op jit(solution)/shard_map/jit(_take)/gather | solution.py:83
  152.4 0.6 broadcast_select_fusion.1
  153.1 7.4 %all-to-all-start = ((s32[1,128,128]{2,0,1:T(1,128)}), s32[1,128,128]{2,0,1:T(1,128)S(1)}, u32[]{:S(2)}, u32[]{:S(2)}) async-start(s32[1,128,128]{2,0,1:T(1,128)} %bitcast.9), calls=%async_computation | async-start | bytes 131072 | tf_op jit(solution)/shard_map/all_to_all | solution.py:92
  160.4 9.2 %fusion.83 = (f32[3,72,45,1]{3,1,2,0:T(8,128)}, f32[3,72,45,1]{3,1,2,0:T(8,128)}) fusion(f32[3,72,45,128]{3,1,2,0:T(8,128)} %param.8), kind=kLoop, calls=%fused_computation.111 | loop fusion | bytes 155520 | tf_op jit(solution)/shard_map/slice | solution.py:15
  169.6 3.5 copy.68
  173.1 5.6 %collective-permute-start.5 = (f32[3,72,45,1]{1,3,2,0:T(1,128)S(1)}, f32[3,72,45,1]{1,3,2,0:T(1,128)}, u32[]{:S(2)}, u32[]{:S(2)}) collective-permute-start(f32[3,72,45,1]{1,3,2,0:T(1,128)S(1)} %copy.68), channel_id=1, source_target_pairs={{0,32},{32,64},{64,96},{1,33},{33,65},{65,97},{2,34},{34,66},{66,9... | collective-permute-start | bytes 116648 | tf_op jit(solution)/shard_map/ppermute | solution.py:16
  178.7 1.6 maximum_add_fusion
  180.4 1.4 add_multiply_fusion
  181.7 3.6 copy.49
  185.3 56.9 %gather_fusion.1 = f32[16384,20]{1,0:T(8,128)} fusion(f32[20,8192]{0,1:T(8,128)} %copy.49, s32[16384]{0:T(1024)S(1)} %fusion.70), kind=kCustom, calls=%fused_computation.1 | custom fusion | bytes 2686976 | tf_op jit(solution)/shard_map/jit(_take)/gather | solution.py:82
  242.3 6.3 %copy.50 = f32[20,128,128]{2,0,1:T(8,128)} copy(f32[20,128,128]{0,2,1:T(8,128)} %bitcast.73) | data formatting | bytes 2621440 | tf_op jit(solution)/shard_map/jit(_take)/gather | solution.py:82
  248.6 2.8 broadcast_select_fusion
  251.4 1.3 slice.83
  252.7 4.0 copy.66
  256.7 0.0 collective-permute-done.4
  256.7 1.9 collective-permute-start.3
  258.6 2.5 copy.43
  261.1 2.4 fusion.64
  263.5 0.0 collective-permute-done.1
  263.5 2.9 fusion.62
  266.4 3.8 copy.41
  270.2 0.0 collective-permute-done.5
  270.2 3.8 copy.45
  274.1 9.9 %all-to-all-start.1 = ((f32[20,128,128]{2,0,1:T(8,128)}), f32[20,128,128]{2,0,1:T(8,128)}, u32[]{:S(2)}, u32[]{:S(2)}) async-start(f32[20,128,128]{2,0,1:T(8,128)} %broadcast_select_fusion), calls=%async_computation.1 | async-start | bytes 3145728 | tf_op jit(solution)/shard_map/all_to_all | solution.py:85
  284.0 1.2 compare_select_fusion
  285.1 22.5 %all-to-all-done.1 = f32[20,128,128]{2,0,1:T(8,128)} async-done(((f32[20,128,128]{2,0,1:T(8,128)}), f32[20,128,128]{2,0,1:T(8,128)}, u32[]{:S(2)}, u32[]{:S(2)}) %all-to-all-start.1) | async-done | bytes 1310752 | tf_op jit(solution)/shard_map/all_to_all | solution.py:85
  307.7 1.7 copy.51
  309.3 0.1 pad.38
  309.5 2.1 copy.70
  311.5 6.1 %copy.52 = f32[16384,20]{1,0:T(8,128)} copy(f32[16384,20]{0,1:T(8,128)} %bitcast.75) | data formatting | bytes 2621440 | tf_op jit(solution)/shard_map/reshape | solution.py:100
  317.6 108.6 %scatter_custom_fusion.1 = f32[20,17280]{0,1:T(8,128)} fusion(s32[16384]{0:T(1024)S(1)} %bitcast.81, f32[16384,20]{1,0:T(8,128)} %copy.52, f32[]{:T(128)} %constant.74.clone.1), kind=kCustom, calls=%fused_computation.47 | custom fusion | flops 327680 | bytes 1382912 | tf_op jit(solution)/shard_map/scatter-add | solution.py:108
  426.2 0.0 copy-start.6
  426.3 11.3 %convolution_bitcast_fusion = f32[3,9,45,8,128]{4,3,2,1,0:T(8,128)} fusion(f32[20,3,5760]{0,2,1:T(8,128)} %bitcast.71, s32[20]{0:T(128)S(1)} %copy-done.7), kind=kOutput, calls=%fused_computation.65 | convolution fusion | flops 298599840 | bytes 6359120 | tf_op jit(solution)/shard_map/kl,ksc->slc/dot_general | solution.py:113
  437.6 20.9 %bitcast_add_fusion = f32[3,72,45,128]{3,1,2,0:T(8,128)} fusion(f32[3,9,45,8,128]{4,3,2,1,0:T(8,128)} %convolution_bitcast_fusion, f32[3,72,45,128]{3,1,2,0:T(8,128)} %param.8, f32[3,72,45,1]{3,1,2,0:T(8,128)} %copy.45, f32[3,72,45,1]{3,1,2,0:T(8,128)} %copy.41, f32[3,72,1,128]{3,1,2,0:T(8,128)} %collective-permute-done.2, ...), kind=kOutput, calls=%fused_computation.4 | convolution fusion | flops 1096120576 | bytes 21885120 | tf_op jit(solution)/shard_map/lm,slxy->smxy/dot_general | solution.py:50
  458.6 1.7 fusion.80
  460.2 1.5 collective-permute-start.7
  461.7 9.2 %fusion.81 = (f32[3,72,45,1]{3,1,2,0:T(8,128)}, f32[3,72,45,1]{3,1,2,0:T(8,128)}) fusion(f32[3,72,45,128]{3,1,2,0:T(8,128)} %bitcast_add_fusion), kind=kLoop, calls=%fused_computation.109 | loop fusion | bytes 155520 | tf_op jit(solution)/shard_map/slice | solution.py:15
  470.9 3.9 copy.55
  474.8 4.5 collective-permute-start.8
  479.3 4.0 copy.57
  483.3 2.8 collective-permute-start.9
  486.1 3.8 copy.56
  490.0 3.9 copy.58
  493.8 18.2 %fusion.56 = f32[3,72,45,128]{3,1,2,0:T(8,128)} fusion(f32[3,72,45,128]{3,1,2,0:T(8,128)} %bitcast_add_fusion, f32[3,72,45,1]{3,1,2,0:T(8,128)} %copy.58, f32[3,72,45,1]{3,1,2,0:T(8,128)} %copy.56, f32[3,72,1,128]{3,1,2,0:T(8,128)} %collective-permute-done.7, f32[3,72,1,128]{3,1,2,0:T(8,128)S(1)} %collective-permute-done.6, f32[72,45,128]{2,0,1:T(8,128)S(1)} %fusion.64, ...), kind=kOutput, calls=%fused_computation.64 | convolution fusion | flops 1094876416 | bytes 16908480 | tf_op jit(solution)/shard_map/lm,slxy->smxy/dot_general | solution.py:50
  512.0 1.3 slice_add_fusion
  513.3 0.6 copy.73
  (27 shorter events, 0.1 us)
Async XLA Ops:
  0.6 61.2 %copy-start = (s32[8192]{0:T(1024)S(1)}, s32[8192]{0:T(1024)}, u32[]{:S(2)}) copy-start(s32[8192]{0:T(1024)} %param.14) | copy-start | bytes 98308
  0.6 19.3 %copy-start.5 = (s32[8192,1]{0,1:T(1,128)S(1)}, s32[8192,1]{0,1:T(1,128)}, u32[]{:S(2)}) copy-start(s32[8192,1]{0,1:T(1,128)} %param.13) | copy-start | bytes 98308
  2.0 261.5 %collective-permute-start.1 = (f32[72,1,128]{2,0,1:T(8,128)}, f32[72,1,128]{2,0,1:T(8,128)}, u32[]{:S(2)}, u32[]{:S(2)}) collective-permute-start(f32[72,1,128]{2,0,1:T(8,128)} %slice.82), channel_id=1, source_target_pairs={{0,1},{1,2},{2,3},{3,4},{4,5},{5,6},{6,7},{7,8},{8,9},{9,10},{10,1... | collective-permute-start | bytes 110600 | tf_op jit(solution)/shard_map/ppermute | solution.py:24
  5.8 431.8 %collective-permute-start = (f32[3,72,1,128]{3,1,2,0:T(8,128)}, f32[3,72,1,128]{3,1,2,0:T(8,128)}, u32[]{:S(2)}, u32[]{:S(2)}) collective-permute-start(f32[3,72,1,128]{3,1,2,0:T(8,128)} %get-tuple-element.8), channel_id=1, source_target_pairs={{1,0},{2,1},{3,2},{4,3},{5,4},{6,5},{7,6},{8,7},{9,8},{10,9},{11,1... | collective-permute-start | bytes 331784 | tf_op jit(solution)/shard_map/ppermute | solution.py:17
  10.8 426.8 %collective-permute-start.2 = (f32[3,72,1,128]{3,1,2,0:T(8,128)}, f32[3,72,1,128]{3,1,2,0:T(8,128)}, u32[]{:S(2)}, u32[]{:S(2)}) collective-permute-start(f32[3,72,1,128]{3,1,2,0:T(8,128)} %get-tuple-element.9), channel_id=1, source_target_pairs={{0,1},{1,2},{2,3},{3,4},{4,5},{5,6},{6,7},{7,8},{8,9},{9,10},{10,1... | collective-permute-start | bytes 331784 | tf_op jit(solution)/shard_map/ppermute | solution.py:16
  13.9 242.7 %collective-permute-start.4 = (f32[72,45,1]{0,1,2:T(8,128)}, f32[72,45,1]{0,1,2:T(8,128)}, u32[]{:S(2)}, u32[]{:S(2)}) collective-permute-start(f32[72,45,1]{0,1,2:T(8,128)} %copy.67), channel_id=1, source_target_pairs={{0,32},{32,64},{64,96},{1,33},{33,65},{65,97},{2,34},{34,66},{66,9... | collective-permute-start | bytes 38888 | tf_op jit(solution)/shard_map/ppermute | solution.py:30
  21.2 2.0 copy-start.2
  153.1 121.0 %all-to-all-start = ((s32[1,128,128]{2,0,1:T(1,128)}), s32[1,128,128]{2,0,1:T(1,128)S(1)}, u32[]{:S(2)}, u32[]{:S(2)}) async-start(s32[1,128,128]{2,0,1:T(1,128)} %bitcast.9), calls=%async_computation | async-start | bytes 131072 | tf_op jit(solution)/shard_map/all_to_all | solution.py:92
  169.6 10.8 %copy-start.3 = (f32[72,45,128]{2,0,1:T(8,128)S(1)}, f32[72,45,128]{2,0,1:T(8,128)}, u32[]{:S(2)}) copy-start(f32[72,45,128]{2,0,1:T(8,128)} %param.10) | copy-start | bytes 4976644
  173.1 97.1 %collective-permute-start.5 = (f32[3,72,45,1]{1,3,2,0:T(1,128)S(1)}, f32[3,72,45,1]{1,3,2,0:T(1,128)}, u32[]{:S(2)}, u32[]{:S(2)}) collective-permute-start(f32[3,72,45,1]{1,3,2,0:T(1,128)S(1)} %copy.68), channel_id=1, source_target_pairs={{0,32},{32,64},{64,96},{1,33},{33,65},{65,97},{2,34},{34,66},{66,9... | collective-permute-start | bytes 116648 | tf_op jit(solution)/shard_map/ppermute | solution.py:16
  242.3 9.2 %copy-start.4 = (f32[72,45,128]{2,0,1:T(8,128)S(1)}, f32[72,45,128]{2,0,1:T(8,128)}, u32[]{:S(2)}) copy-start(f32[72,45,128]{2,0,1:T(8,128)} %param.9) | copy-start | bytes 4976644
  256.7 9.7 %collective-permute-start.3 = (f32[3,72,45,1]{1,3,2,0:T(1,128)}, f32[3,72,45,1]{1,3,2,0:T(1,128)}, u32[]{:S(2)}, u32[]{:S(2)}) collective-permute-start(f32[3,72,45,1]{1,3,2,0:T(1,128)} %copy.66), channel_id=1, source_target_pairs={{32,0},{64,32},{96,64},{33,1},{65,33},{97,65},{34,2},{66,34},{98,6... | collective-permute-start | bytes 116648 | tf_op jit(solution)/shard_map/ppermute | solution.py:17
  274.1 33.6 %all-to-all-start.1 = ((f32[20,128,128]{2,0,1:T(8,128)}), f32[20,128,128]{2,0,1:T(8,128)}, u32[]{:S(2)}, u32[]{:S(2)}) async-start(f32[20,128,128]{2,0,1:T(8,128)} %broadcast_select_fusion), calls=%async_computation.1 | async-start | bytes 3145728 | tf_op jit(solution)/shard_map/all_to_all | solution.py:85
  317.6 108.6 %copy-start.7 = (s32[20]{0:T(128)S(1)}, s32[20]{0:T(128)}, u32[]{:S(2)}) copy-start(s32[20]{0:T(128)} %param.15) | copy-start | bytes 244
  426.2 11.4 %copy-start.6 = (f32[72,72]{1,0:T(8,128)S(1)}, f32[72,72]{1,0:T(8,128)}, u32[]{:S(2)}) copy-start(f32[72,72]{1,0:T(8,128)} %param.11) | copy-start | bytes 62212
  460.2 33.6 %collective-permute-start.6 = (f32[3,72,1,128]{3,1,2,0:T(8,128)}, f32[3,72,1,128]{3,1,2,0:T(8,128)S(1)}, u32[]{:S(2)}, u32[]{:S(2)}) collective-permute-start(f32[3,72,1,128]{3,1,2,0:T(8,128)} %get-tuple-element.4), channel_id=1, source_target_pairs={{1,0},{2,1},{3,2},{4,3},{5,4},{6,5},{7,6},{8,7},{9,8},{10,9},{11,1... | collective-permute-start | bytes 331784 | tf_op jit(solution)/shard_map/ppermute | solution.py:17
  460.2 33.6 %collective-permute-start.7 = (f32[3,72,1,128]{3,1,2,0:T(8,128)}, f32[3,72,1,128]{3,1,2,0:T(8,128)}, u32[]{:S(2)}, u32[]{:S(2)}) collective-permute-start(f32[3,72,1,128]{3,1,2,0:T(8,128)} %get-tuple-element.5), channel_id=1, source_target_pairs={{0,1},{1,2},{2,3},{3,4},{4,5},{5,6},{6,7},{7,8},{8,9},{9,10},{10,1... | collective-permute-start | bytes 331784 | tf_op jit(solution)/shard_map/ppermute | solution.py:16
  474.8 11.3 %collective-permute-start.8 = (f32[3,72,45,1]{1,3,2,0:T(1,128)}, f32[3,72,45,1]{1,3,2,0:T(1,128)}, u32[]{:S(2)}, u32[]{:S(2)}) collective-permute-start(f32[3,72,45,1]{1,3,2,0:T(1,128)} %copy.55), channel_id=1, source_target_pairs={{32,0},{64,32},{96,64},{33,1},{65,33},{97,65},{34,2},{66,34},{98,6... | collective-permute-start | bytes 116648 | tf_op jit(solution)/shard_map/ppermute | solution.py:17
  483.3 6.7 %collective-permute-start.9 = (f32[3,72,45,1]{1,3,2,0:T(1,128)}, f32[3,72,45,1]{1,3,2,0:T(1,128)}, u32[]{:S(2)}, u32[]{:S(2)}) collective-permute-start(f32[3,72,45,1]{1,3,2,0:T(1,128)} %copy.57), channel_id=1, source_target_pairs={{0,32},{32,64},{64,96},{1,33},{33,65},{65,97},{2,34},{34,66},{66,9... | collective-permute-start | bytes 116648 | tf_op jit(solution)/shard_map/ppermute | solution.py:16
  493.8 20.1 %copy-start.1 = (s32[8192]{0:T(1024)S(1)}, s32[8192]{0:T(1024)}, u32[]{:S(2)}) copy-start(s32[8192]{0:T(1024)} %param.14) | copy-start | bytes 98308
where the time goes:
time: 524 us; the launch traced here: 514 us
  local copies, waits for them, and re-layouts  264 us (50%)
  other arithmetic  130 us (25%)
  matrix products  50.5 us (10%)
  starting transfers between devices  46.7 us (9%)
  waiting for transfers between devices  22.6 us (4%)
    scatter-add x1, other arithmetic, on_device(): gathered = jnp.zeros((kernel_levels, species_count * cell_count), jnp.flo...  109 us
    gather x1, local copies, waits for them, and re-layouts, on_device(): jnp.take(sounding_target, source_row, axis=0, mode='fill', fill_value=0)  90.5 us
    gather x2, local copies, waits for them, and re-layouts, on_device(): jnp.take(sounding_values, source_row, axis=1, mode='fill', fill_value=0.0)  63.3 us
    dot_general x2, matrix products, mixing(): jnp.einsum('lm,slxy->smxy', matrix, field, precision=lax.Precision.HIGHEST)  39.2 us
    scatter x1, local copies, waits for them, and re-layouts, on_device(): source_row = jnp.full((n_tiles * capacity,), row_count, jnp.int32).at[pos...  30.5 us
    slice x5, local copies, waits for them, and re-layouts, with_halo(): initial = lax.slice_in_dim(value, 0, width, axis=dim)  25.6 us
    all_to_all x1, waiting for transfers between devices, on_device(): lax.all_to_all(send_values.reshape(kernel_levels, n_tiles, capacity), ('l...  22.5 us
    unnamed x23, local copies, waits for them, and re-layouts  17.1 us
  transfers between devices with their start and end apart: 12, of which 1 were waited for; matrix products, arithmetic and copies ran while one was open for 77% of the time, Pallas kernels for 0%

commit v1 on v0

v1 whole, which is shorter than its diff:
```python
import functools

import jax
import jax.numpy as jnp
from jax import lax
from jax.experimental import pallas as pl
from jax.experimental.pallas import tpu as pltpu
from jax.sharding import PartitionSpec as P

kappa_mix = 0.05
LANES = 128
WIDE = 256
f32 = jnp.float32
bf16 = jnp.bfloat16
VMEM_LIMIT = 56 * 2**20


def call(kernel, out_shape, *args, scratch=(), smem=(), flops=0, nbytes=0):
    specs = [
        pl.BlockSpec(memory_space=pltpu.SMEM if i in smem else pltpu.VMEM) for i in range(len(args))
    ]
    return pl.pallas_call(
        kernel,
        out_shape=out_shape,
        in_specs=specs,
        out_specs=jax.tree.map(lambda _: pl.BlockSpec(memory_space=pltpu.VMEM), out_shape),
        scratch_shapes=list(scratch),
        compiler_params=pltpu.CompilerParams(vmem_limit_bytes=VMEM_LIMIT),
        cost_estimate=pl.CostEstimate(flops=flops, bytes_accessed=nbytes, transcendentals=0),
    )(*args)


def split(value):
    high = value.astype(bf16).astype(f32)
    return high, value - high


def nt_dot(a, b):
    return lax.dot_general(a, b, (((1,), (1,)), ((), ())), preferred_element_type=f32)


def onehot_product(parts, group, spot, total, count, step, together, depth):
    rows, length = parts.shape
    chunks = length // depth

    def of_group(g, carry):
        def of_chunk(c, carry):
            at = pl.ds(pl.multiple_of(c * depth, depth), depth)
            held, key = parts[:, at], group[:, at]
            left = jnp.concatenate(
                [
                    jnp.where(
                        key == ((g * together + i) * step).astype(f32).astype(bf16), held, jnp.zeros_like(held)
                    )
                    for i in range(together)
                ],
                axis=0,
            )
            product = nt_dot(left, spot[:, at])
            to = pl.ds(pl.multiple_of(g * (together * rows), together * rows), together * rows)
            if chunks == 1:
                total[to, :] = product
            else:

                @pl.when(c == 0)
                def _():
                    total[to, :] = product

                @pl.when(c > 0)
                def _():
                    total[to, :] += product

            return carry

        return lax.fori_loop(0, chunks, of_chunk, carry)

    lax.fori_loop(0, count // together, of_group, 0)


PACK = (4, 2048)
ADD = (2, 2048)


def pack_kernel(dest, values, target, out, ranked, parts, group, spot, total):
    blocks = dest.shape[0]
    n_tiles, held, _ = out.shape
    levels = values.shape[0]
    iota_t = lax.broadcasted_iota(jnp.int32, (n_tiles, WIDE), 0)
    square = (WIDE, WIDE)
    upper = (
        lax.broadcasted_iota(jnp.int32, square, 0) < lax.broadcasted_iota(jnp.int32, square, 1)
    ).astype(f32).astype(bf16)
    iota_w = lax.broadcasted_iota(jnp.int32, square, 0)

    def rank(b, base):
        d = dest[pl.ds(b, 1), :]
        hot = iota_t == d
        hot_f = jnp.where(hot, 1.0, 0.0)
        earlier = jnp.dot(hot_f.astype(bf16), upper, preferred_element_type=f32) + base
        own = jnp.sum(jnp.where(hot, earlier, 0.0), axis=0, keepdims=True).astype(jnp.int32)
        at = pl.ds(pl.multiple_of(b * WIDE, WIDE), WIDE)
        low = own + (d & 1) * LANES
        spot[:, at] = jnp.where(iota_w == low, 1.0, 0.0).astype(bf16)
        group[:, at] = jnp.broadcast_to((d >> 1).astype(f32), (2 * held, WIDE)).astype(bf16)
        row = jnp.concatenate(
            [values[:, at], target[:, at], jnp.zeros((held - levels - 1, WIDE), f32)], axis=0
        )
        parts[:, at] = jnp.concatenate(split(row), axis=0).astype(bf16)
        return base + jnp.sum(hot_f, axis=1, keepdims=True)

    lax.fori_loop(0, blocks, rank, jnp.zeros((n_tiles, 1), f32))
    onehot_product(parts, group, spot, total, n_tiles // 2, 1, *PACK)

    def put(j, carry):
        at = pl.multiple_of(j * 2 * held, 2 * held)
        both = total[pl.ds(at, held), :] + total[pl.ds(at + held, held), :]
        out[2 * j] = both[:, :LANES]
        out[2 * j + 1] = both[:, LANES:]
        return carry

    lax.fori_loop(0, n_tiles // 2, put, 0)


def pack(dest, values, target, n_tiles):
    levels, rows = values.shape
    held = -(-(levels + 1) // 8) * 8
    scratch = (
        pltpu.VMEM((8, LANES), f32),
        pltpu.VMEM((2 * held, rows), bf16),
        pltpu.VMEM((2 * held, rows), bf16),
        pltpu.VMEM((WIDE, rows), bf16),
        pltpu.VMEM((n_tiles // 2 * 2 * held, WIDE), f32),
    )
    return call(
        pack_kernel,
        jax.ShapeDtypeStruct((n_tiles, held, LANES), f32),
        dest.reshape(rows // WIDE, WIDE),
        values,
        target.reshape(1, rows),
        scratch=scratch,
        flops=2 * rows * n_tiles * LANES * 2 * held,
        nbytes=4 * (rows * 22 + n_tiles * held * LANES),
    )


def edges_kernel(field, courant_lat, up, down):
    species, cols, levels, rows = field.shape
    lane = lax.broadcasted_iota(jnp.int32, (levels, rows), 1)

    def column(x, carry):
        for s in range(species):
            v = field[s, x]
            up[s] = jnp.where(lane == x, pltpu.roll(v, x + 1, 1), up[s])
            down[s] = jnp.where(lane == x, pltpu.roll(v, x, 1), down[s])
        up[species] = jnp.where(lane == x, pltpu.roll(courant_lat[x], x + 1, 1), up[species])
        return carry

    up[...] = jnp.zeros_like(up)
    down[...] = jnp.zeros_like(down)
    lax.fori_loop(0, cols, column, 0)


def edges(field, courant_lat):
    species, cols, levels, rows = field.shape
    return call(
        edges_kernel,
        (
            jax.ShapeDtypeStruct((species + 1, levels, rows), f32),
            jax.ShapeDtypeStruct((species, levels, rows), f32),
        ),
        field,
        courant_lat,
        flops=field.size * 4,
        nbytes=field.size * 4,
    )


def mix_weights(vertical_mix):
    levels = vertical_mix.shape[0]
    matrix = (jnp.eye(levels, dtype=f32) + vertical_mix).T
    high = lax.reduce_precision(matrix, 8, 7)
    return jnp.concatenate([high, high, matrix - high], axis=1).astype(bf16)


def step_kernel(
    lat_ref, field, clon, clat, west_col, east_col, clon_col, south, north, clat_south, weights, *refs, lat_size, after
):
    species, cols, levels, rows = field.shape
    lane = lax.broadcasted_iota(jnp.int32, (levels, rows), 1)
    first, last = lane == 0, lane == rows - 1
    lat = lat_ref[0]
    below = jnp.where(jnp.logical_and(first, lat == 0), 0.0, 1.0)
    inside = jnp.where(jnp.logical_and(last, lat == lat_size - 1), 0.0, 1.0)
    w = weights[...]

    def column(x, west, east, clon_west):
        cl, cw = clon[x], clat[x]
        e = jnp.maximum(cl, 0.0) + kappa_mix
        wst = jnp.minimum(clon_west, 0.0) - kappa_mix
        n = (jnp.maximum(cw, 0.0) + kappa_mix) * inside
        cs = jnp.where(first, pltpu.roll(clat_south[...], rows - x, 1), pltpu.roll(cw, 1, 1))
        s_ = (jnp.minimum(cs, 0.0) - kappa_mix) * below
        centre = 1.0 - e + wst - n + s_
        wide = []
        for s in range(species):
            v = field[s, x]
            v_n = jnp.where(last, pltpu.roll(north[s], rows - 1 - x, 1), pltpu.roll(v, rows - 1, 1))
            v_s = jnp.where(first, pltpu.roll(south[s], rows - x, 1), pltpu.roll(v, 1, 1))
            h = centre * v + e * east(s) - wst * west(s) + n * v_n - s_ * v_s
            high, low = split(h)
            wide.append(jnp.concatenate([high, low, high], axis=0).astype(bf16))
        mixed = jnp.dot(w, jnp.concatenate(wide, axis=1), preferred_element_type=f32)
        after(x, [mixed[:, s * rows : (s + 1) * rows] for s in range(species)], refs)

    roll_fix = None
    column(0, lambda s: west_col[s], lambda s: field[s, 1], clon_col[...])

    def body(x, carry):
        column(x, lambda s: field[s, x - 1], lambda s: field[s, x + 1], clon[x - 1])
        return carry

    lax.fori_loop(1, cols - 1, body, 0)
    column(cols - 1, lambda s: field[s, cols - 2], lambda s: east_col[s], clon[cols - 2])


def after_first(x, mixed, refs):
    (out,) = refs
    for s, m in enumerate(mixed):
        out[s, x] = m


def after_second(x, mixed, refs):
    level0, out, flux = refs
    for s, m in enumerate(mixed):
        out[s, x] = m
        flux[s, pl.ds(x, 1), :] = level0[s, pl.ds(x, 1), :] + m[0:1]


def step(lat, field, clon, clat, halo, weights, lat_size, level0=None):
    species, cols, levels, rows = field.shape
    shape = jax.ShapeDtypeStruct(field.shape, f32)
    if level0 is None:
        shapes, after, more = (shape,), after_first, ()
    else:
        shapes, after, more = (shape, jax.ShapeDtypeStruct((species, cols, rows), f32)), after_second, (level0,)
    west_col, east_col, clon_col, south, north, clat_south = halo
    return call(
        functools.partial(step_kernel, lat_size=lat_size, after=after),
        shapes,
        lat,
        field,
        clon,
        clat,
        west_col,
        east_col,
        clon_col,
        south,
        north,
        clat_south,
        weights,
        *more,
        smem=(0,),
        flops=field.size * levels * 6,
        nbytes=field.size * 12,
    )


def add_kernel(got, plain, table, first, up, down, level0, parts, group, spot, total):
    sources, held, slots = got.shape
    species, cols, levels, rows = plain.shape
    akl = table.shape[1] // 4
    iota_w = lax.broadcasted_iota(jnp.int32, (WIDE, WIDE), 0)
    second = (lax.broadcasted_iota(jnp.int32, (4 * akl, WIDE), 0) >= 2 * akl).astype(f32)

    def prepare(b, carry):
        row = jnp.concatenate([got[2 * b], got[2 * b + 1]], axis=1)
        at = pl.ds(pl.multiple_of(b * WIDE, WIDE), WIDE)
        segment = row[akl : akl + 1].astype(jnp.int32)
        spot[:, at] = jnp.where(iota_w == (segment & (WIDE - 1)), 1.0, 0.0).astype(bf16)
        group[:, at] = ((segment >> 8).astype(f32) - second).astype(bf16)
        high, low = split(row[:akl])
        both = jnp.concatenate([high, low], axis=0)
        parts[:, at] = jnp.concatenate([both, both], axis=0).astype(bf16)
        return carry

    lax.fori_loop(0, sources // 2, prepare, 0)
    onehot_product(parts, group, spot, total, -(-species * cols // 4), 2, *ADD)

    lane = lax.broadcasted_iota(jnp.int32, (levels, rows), 1)
    up[...] = jnp.zeros_like(up)
    down[...] = jnp.zeros_like(down)
    t = table[...]

    def place(at, half, s, x):
        pair = total[pl.ds(at, 2 * akl), half * rows : (half + 1) * rows]
        high, low = split(pair)
        forcing = jnp.dot(t, jnp.concatenate([high, low], axis=0).astype(bf16), preferred_element_type=f32)
        v = plain[s, x] + forcing
        first[s, x] = v
        level0[s, pl.ds(x, 1), :] = v[0:1]
        up[s] = jnp.where(lane == x, pltpu.roll(v, x + 1, 1), up[s])
        down[s] = jnp.where(lane == x, pltpu.roll(v, x, 1), down[s])

    for s in range(species):

        def column(x, carry):
            sx = s * cols + x
            at = pl.multiple_of((sx >> 1) * 2 * akl, 8)

            @pl.when((sx & 1) == 0)
            def _():
                place(at, 0, s, x)

            @pl.when((sx & 1) == 1)
            def _():
                place(at, 1, s, x)

            return carry

        lax.fori_loop(0, cols, column, 0)


def add_soundings(got, plain, table):
    sources, held, slots = got.shape
    species, cols, levels, rows = plain.shape
    akl = table.shape[1] // 4
    length = sources * slots
    pairs = -(-species * cols // 4)
    edge = jax.ShapeDtypeStruct((species, levels, rows), f32)
    return call(
        add_kernel,
        (jax.ShapeDtypeStruct(plain.shape, f32), edge, edge, jax.ShapeDtypeStruct((species, cols, rows), f32)),
        got,
        plain,
        table,
        scratch=(
            pltpu.VMEM((4 * akl, length), bf16),
            pltpu.VMEM((4 * akl, length), bf16),
            pltpu.VMEM((WIDE, length), bf16),
            pltpu.VMEM((pairs * 4 * akl, WIDE), f32),
        ),
        flops=2 * pairs * 4 * akl * WIDE * length,
        nbytes=4 * (got.size + 2 * plain.size),
    )


def on_device(
    adjoint_in,
    courant_lon,
    courant_lat,
    vertical_mix,
    sounding_values,
    sounding_dest,
    sounding_target,
    level_index,
):
    lat_size, lon_size = lax.axis_size("lat"), lax.axis_size("lon")
    n_tiles = lat_size * lon_size
    species, levels, cols, rows = adjoint_in.shape
    east_way = [(i, (i + 1) % lon_size) for i in range(lon_size)]
    west_way = [(j, i) for i, j in east_way]
    north_way = [(i, i + 1) for i in range(lat_size - 1)]
    south_way = [(j, i) for i, j in north_way]

    field = adjoint_in.transpose(0, 2, 1, 3)
    clon = courant_lon.transpose(1, 0, 2)
    clat = courant_lat.transpose(1, 0, 2)
    lat = lax.axis_index("lat").reshape(1)

    cell, tracer = sounding_target // species, sounding_target % species
    segment = (tracer * cols + cell % cols) * rows + cell // cols
    sent = pack(sounding_dest, sounding_values, segment.astype(f32), n_tiles)
    got = lax.all_to_all(sent, ("lat", "lon"), split_axis=0, concat_axis=0, tiled=True)

    up, down = edges(field, clat)
    south = lax.ppermute(up, "lat", north_way)
    north = lax.ppermute(down, "lat", south_way)
    clat_south = south[species]
    west = lax.ppermute(jnp.concatenate([field[:, cols - 1], clon[None, cols - 1]], axis=0), "lon", east_way)
    east = lax.ppermute(field[:, 0], "lon", west_way)
    clon_west = west[species]

    weights = mix_weights(vertical_mix)
    table = (jnp.arange(levels, dtype=jnp.int32)[:, None] == level_index[None, :]).astype(bf16)
    table = jnp.concatenate([table] * 4, axis=1)
    (plain,) = step(lat, field, clon, clat, (west, east, clon_west, south, north, clat_south), weights, lat_size)
    first, up, down, level0 = add_soundings(got, plain, table)
    south = lax.ppermute(up, "lat", north_way)
    north = lax.ppermute(down, "lat", south_way)
    west = lax.ppermute(first[:, cols - 1], "lon", east_way)
    east = lax.ppermute(first[:, 0], "lon", west_way)
    out, flux = step(
        lat, first, clon, clat, (west, east, clon_west, south, north, clat_south), weights, lat_size, level0
    )
    return out.transpose(0, 2, 1, 3), flux


def solution(mesh):
    return jax.shard_map(
        on_device,
        mesh=mesh,
        in_specs=(
            P(None, None, "lon", "lat"),
            P(None, "lon", "lat"),
            P(None, "lon", "lat"),
            P(),
            P(None, ("lat", "lon")),
            P(("lat", "lon"), None),
            P(("lat", "lon")),
            P(),
        ),
        out_specs=(P(None, None, "lon", "lat"), P(None, "lon", "lat")),
        check_vma=False,
    )
```

time: 524 us -> 266 us (0.51); the launches traced: 514 us -> 266 us
  local copies, waits for them, and re-layouts: 264 us -> 9.62 us
  Pallas kernels: 0 us -> 206 us
  other arithmetic: 130 us -> 4.38 us
  matrix products: 50.5 us -> 0 us
  starting transfers between devices: 46.7 us -> 32.1 us
  waiting for transfers between devices: 22.6 us -> 12.4 us
    pallas_call x0 -> x5, Pallas kernels: none -> 206 us  [call(): pl.pallas_call(kernel, out_shape=out_shape, in_specs=specs, out_specs=jax...]
    gather x3 -> x0, local copies, waits for them, and re-layouts: 154 us -> none  [the longest x1 90.5 us: on_device(): jnp.take(sounding_target, source_row, axis=0, mode='fill', fill_value=0)]
    scatter-add x1 -> x0, other arithmetic: 109 us -> none  [on_device(): gathered = jnp.zeros((kernel_levels, species_count * cell_count), jnp.flo...]
    dot_general x3 -> x0, matrix products: 50.5 us -> none  [the longest x2 39.2 us: mixing(): jnp.einsum('lm,slxy->smxy', matrix, field, precision=lax.Precision.HIGHEST)]
    slice x9 -> x1, local copies, waits for them, and re-layouts: 34.2 us -> 0.77 us  [on_device(): clon[None, cols - 1]]
    scatter x1 -> x0, local copies, waits for them, and re-layouts: 30.5 us -> none  [on_device(): source_row = jnp.full((n_tiles * capacity,), row_count, jnp.int32).at[pos...]
    all_to_all x2 -> x1, waiting for transfers between devices: 22.5 us -> 0.01 us  [on_device(): lax.all_to_all(sent, ('lat', 'lon'), split_axis=0, concat_axis=0, tiled=T...]
    ppermute x5 -> x0, local copies, waits for them, and re-layouts: 17.9 us -> none  [the longest x2 7.7 us: with_halo(): before = lax.ppermute(last, axis, up)]
  transfers between devices with their start and end apart: 12 -> 9, of which waited for: 1 -> 3; matrix products, arithmetic and copies ran while one was open for 77% -> 3% of each run, Pallas kernels for 0% -> 12%
where the time goes in v1:
time: 266 us
  Pallas kernels  206 us (77%)
  starting transfers between devices  32.1 us (12%)
  waiting for transfers between devices  12.4 us (5%)
  local copies, waits for them, and re-layouts  9.62 us (4%)
  other arithmetic  4.38 us (2%)
    pallas_call x5, Pallas kernels, call(): pl.pallas_call(kernel, out_shape=out_shape, in_specs=specs, out_specs=jax...  206 us
    all_to_all x1, starting transfers between devices, on_device(): lax.all_to_all(sent, ('lat', 'lon'), split_axis=0, concat_axis=0, tiled=T...  11.5 us
    ppermute x2, starting transfers between devices, on_device(): south = lax.ppermute(up, 'lat', north_way)  8.33 us
    ppermute x1, waiting for transfers between devices, on_device(): lax.ppermute(jnp.concatenate([field[:, cols - 1], clon[None, cols - 1]],...  5.95 us
    unnamed x25, local copies, waits for them, and re-layouts  5.89 us
    ppermute x1, starting transfers between devices, on_device(): east = lax.ppermute(field[:, 0], 'lon', west_way)  5.76 us
  transfers between devices with their start and end apart: 9, of which 3 were waited for; matrix products, arithmetic and copies ran while one was open for 3% of the time, Pallas kernels for 12%

profile of v1, /device:TPU:1, one launch (start us, length us, event | category | flops | bytes accessed | tf_op | source)
XLA Modules:
  0.0 265.6 jit_solution(11450535976822620640)
XLA Ops:
  0.6 0.5 broadcast.9
  1.1 1.5 reduce.3
  2.6 0.6 reshape.15.dest
  3.2 1.4 fusion.5
  4.7 44.2 %shard_map.95 = f32[128,24,128]{2,1,0:T(8,128)} custom-call(s32[32,256]{1,0:T(8,128)} %reshape.15.dest, f32[20,8192]{1,0:T(8,128)} %values.1, f32[1,8192]{1,0:T(1,128)} %bitcast.34), custom_call_target="tpu_custom_call" | custom-call | flops 12884901888 | bytes 2293760 | tf_op jit(solution)/shard_map/pallas_call | solution.py:22
  48.9 11.5 %all-to-all-start = ((f32[128,24,128]{2,1,0:T(8,128)}), f32[128,24,128]{2,1,0:T(8,128)S(1)}, u32[]{:S(2)}, u32[]{:S(2)}) async-start(f32[128,24,128]{2,1,0:T(8,128)} %shard_map.95), calls=%async_computation | async-start | bytes 3145728 | tf_op jit(solution)/shard_map/all_to_all | solution.py:373
  60.5 9.8 %shard_map.96 = (f32[4,72,128]{2,1,0:T(8,128)}, f32[3,72,128]{2,1,0:T(8,128)}) custom-call(f32[3,45,72,128]{3,2,1,0:T(8,128)} %bitcast.25, f32[45,72,128]{2,1,0:T(8,128)} %bitcast.27), custom_call_target="tpu_custom_call" | custom-call | flops 4976640 | bytes 4976640 | tf_op jit(solution)/shard_map/pallas_call | solution.py:22
  70.2 3.0 %collective-permute-start.3 = (f32[3,72,128]{2,1,0:T(8,128)}, f32[3,72,128]{2,1,0:T(8,128)S(1)}, u32[]{:S(2)}, u32[]{:S(2)}) collective-permute-start(f32[3,72,128]{2,1,0:T(8,128)} %get-tuple-element.11), channel_id=1, source_target_pairs={{32,0},{64,32},{96,64},{33,1},{65,33},{97,65},{34,2},{66,34},{98,6... | collective-permute-start | bytes 331784 | tf_op jit(solution)/shard_map/ppermute | solution.py:377
  73.2 0.0 copy-start.9
  73.2 0.0 copy-start.10
  73.2 4.4 %collective-permute-start.2 = (f32[4,72,128]{2,1,0:T(8,128)}, f32[4,72,128]{2,1,0:T(8,128)S(1)}, u32[]{:S(2)}, u32[]{:S(2)}) collective-permute-start(f32[4,72,128]{2,1,0:T(8,128)} %get-tuple-element.10), channel_id=1, source_target_pairs={{0,32},{32,64},{64,96},{1,33},{33,65},{65,97},{2,34},{34,66},{66,9... | collective-permute-start | bytes 442376 | tf_op jit(solution)/shard_map/ppermute | solution.py:376
  77.6 2.7 %copy.20 = f32[3,72,45,128]{3,1,0,2:T(8,128)S(1)} copy(f32[3,72,45,128]{3,1,2,0:T(8,128)} %param.8) | data formatting | bytes 9953280 | tf_op args[0]
  80.4 5.8 %collective-permute-start.1 = (f32[3,72,128]{2,1,0:T(8,128)S(1)}, f32[3,72,128]{2,1,0:T(8,128)S(1)}, u32[]{:S(2)}, u32[]{:S(2)}) collective-permute-start(f32[3,72,128]{2,1,0:T(8,128)S(1)} %get-tuple-element.20), channel_id=1, source_target_pairs={{1,0},{2,1},{3,2},{4,3},{5,4},{6,5},{7,6},{8,7},{9,8},{10,9},{11,1... | collective-permute-start | bytes 331784 | tf_op jit(solution)/shard_map/ppermute | solution.py:380
  86.1 0.8 slice.29
  86.9 0.1 collective-permute-start
  87.0 0.0 copy-done.9
  87.0 0.1 copy.12
  87.1 0.0 copy-done.10
  87.1 0.7 add_convert_fusion.table
  87.8 0.7 pad_maximum_fusion.1.weights
  88.5 0.0 collective-permute-done.2.south
  88.5 0.0 copy-start.1
  88.5 0.7 slice_bitcast_fusion.4.clat_south
  89.2 6.0 %collective-permute-done.west_col = f32[4,72,128]{2,1,0:T(8,128)S(1)} collective-permute-done((f32[4,72,128]{2,1,0:T(8,128)S(1)}, f32[4,72,128]{2,1,0:T(8,128)S(1)}, u32[]{:S(2)}, u32[]{:S(2)}) %collective-permute-start) | collective-permute-done | bytes 147488 | tf_op jit(solution)/shard_map/ppermute | solution.py:379
  95.2 0.0 copy-start.2
  95.2 0.7 slice_bitcast_fusion.5.clon_col
  95.8 0.0 collective-permute-done.3.north
  95.9 0.0 copy-start.3
  95.9 0.0 collective-permute-done.1.east_col
  95.9 0.0 copy-start.4
  95.9 0.0 copy-done.1
  95.9 0.0 copy-done.2
  95.9 0.6 copy-done.3
  96.5 0.0 copy-done.4
  96.6 22.5 %shard_map.97.plain = f32[3,45,72,128]{3,2,1,0:T(8,128)} custom-call(s32[1]{0:T(128)} %bitcast.lat_ref, f32[3,45,72,128]{3,2,1,0:T(8,128)} %bitcast.26, f32[45,72,128]{2,1,0:T(8,128)} %bitcast.31, f32[45,72,128]{2,1,0:T(8,128)} %bitcast.28, f32[4,72,128]{2,1,0:T(8,128)} %copy-done.2, f32[3,72,128]{2,1,0:T(8,128)} %copy-done.4, ...), custom_call_target="tpu_custom_call" | custom-call | flops 537477120 | bytes 14929920 | tf_op jit(solution)/shard_map/pallas_call | solution.py:22
  119.0 0.0 all-to-all-done.got
  119.0 0.0 copy-start
  119.0 1.2 copy-done
  120.2 107.4 %shard_map.98 = (f32[3,45,72,128]{3,2,1,0:T(8,128)}, f32[3,72,128]{2,1,0:T(8,128)}, f32[3,72,128]{2,1,0:T(8,128)}, f32[3,45,128]{2,1,0:T(8,128)}) custom-call(f32[128,24,128]{2,1,0:T(8,128)} %copy-done, f32[3,45,72,128]{3,2,1,0:T(8,128)} %shard_map.97.plain, bf16[72,80]{1,0:T(8,128)(2,1)} %add_convert_fusion.table), custom_call_target="tpu_custom_call" | custom-call | flops 22817013760 | bytes 11526144 | tf_op jit(solution)/shard_map/pallas_call | solution.py:22
  227.6 3.9 %collective-permute-start.6 = (f32[3,72,128]{2,1,0:T(8,128)}, f32[3,72,128]{2,1,0:T(8,128)S(1)}, u32[]{:S(2)}, u32[]{:S(2)}) collective-permute-start(f32[3,72,128]{2,1,0:T(8,128)} %get-tuple-element.13), channel_id=1, source_target_pairs={{0,32},{32,64},{64,96},{1,33},{33,65},{65,97},{2,34},{34,66},{66,9... | collective-permute-start | bytes 331784 | tf_op jit(solution)/shard_map/ppermute | solution.py:388
  231.6 1.9 collective-permute-start.7
  233.5 1.0 slice_bitcast_fusion
  234.5 0.1 collective-permute-start.5
  234.6 1.5 collective-permute-start.4
  236.0 0.0 collective-permute-done.6.south
  236.0 0.0 copy-start.5
  236.0 3.3 %collective-permute-done.7.north = f32[3,72,128]{2,1,0:T(8,128)S(1)} collective-permute-done((f32[3,72,128]{2,1,0:T(8,128)}, f32[3,72,128]{2,1,0:T(8,128)S(1)}, u32[]{:S(2)}, u32[]{:S(2)}) %collective-permute-start.7) | collective-permute-done | bytes 110624 | tf_op jit(solution)/shard_map/ppermute | solution.py:389
  239.4 0.0 copy-start.6
  239.4 0.0 collective-permute-done.5.east_col
  239.4 0.0 copy-start.7
  239.4 3.1 %collective-permute-done.4.west_col = f32[3,72,128]{2,1,0:T(8,128)S(1)} collective-permute-done((f32[3,72,128]{2,1,0:T(8,128)S(1)}, f32[3,72,128]{2,1,0:T(8,128)S(1)}, u32[]{:S(2)}, u32[]{:S(2)}) %collective-permute-start.4) | collective-permute-done | bytes 110624 | tf_op jit(solution)/shard_map/ppermute | solution.py:390
  242.5 0.0 copy-start.8
  242.5 0.0 copy-done.5
  242.5 0.0 copy-done.6
  242.5 0.0 copy-done.7
  242.5 0.7 copy-done.8
  243.1 22.5 %shard_map.99 = (f32[3,45,72,128]{3,2,1,0:T(8,128)}, f32[3,45,128]{2,1,0:T(8,128)}) custom-call(s32[1]{0:T(128)} %bitcast.lat_ref, f32[3,45,72,128]{3,2,1,0:T(8,128)} %get-tuple-element.12.field, f32[45,72,128]{2,1,0:T(8,128)} %bitcast.32, f32[45,72,128]{2,1,0:T(8,128)} %bitcast.29, f32[3,72,128]{2,1,0:T(8,128)} %copy-done.8, f32[3,72,128]{2,1,0:T(8,128)} %copy-done.7, ...), custom_call_target="tpu_custom_call" | custom-call | flops 537477120 | bytes 14929920 | tf_op jit(solution)/shard_map/pallas_call | solution.py:22
  (4 shorter events, 0.1 us)
Async XLA Ops:
  48.9 70.1 %all-to-all-start = ((f32[128,24,128]{2,1,0:T(8,128)}), f32[128,24,128]{2,1,0:T(8,128)S(1)}, u32[]{:S(2)}, u32[]{:S(2)}) async-start(f32[128,24,128]{2,1,0:T(8,128)} %shard_map.95), calls=%async_computation | async-start | bytes 3145728 | tf_op jit(solution)/shard_map/all_to_all | solution.py:373
  70.2 25.6 %collective-permute-start.3 = (f32[3,72,128]{2,1,0:T(8,128)}, f32[3,72,128]{2,1,0:T(8,128)S(1)}, u32[]{:S(2)}, u32[]{:S(2)}) collective-permute-start(f32[3,72,128]{2,1,0:T(8,128)} %get-tuple-element.11), channel_id=1, source_target_pairs={{32,0},{64,32},{96,64},{33,1},{65,33},{97,65},{34,2},{66,34},{98,6... | collective-permute-start | bytes 331784 | tf_op jit(solution)/shard_map/ppermute | solution.py:377
  73.2 13.8 %copy-start.9 = (f32[72,72]{1,0:T(8,128)S(1)}, f32[72,72]{1,0:T(8,128)}, u32[]{:S(2)}) copy-start(f32[72,72]{1,0:T(8,128)} %param.11) | copy-start | bytes 62212
  73.2 13.9 %copy-start.10 = (s32[20]{0:T(128)S(1)}, s32[20]{0:T(128)}, u32[]{:S(2)}) copy-start(s32[20]{0:T(128)} %param.15) | copy-start | bytes 244
  73.2 15.3 %collective-permute-start.2 = (f32[4,72,128]{2,1,0:T(8,128)}, f32[4,72,128]{2,1,0:T(8,128)S(1)}, u32[]{:S(2)}, u32[]{:S(2)}) collective-permute-start(f32[4,72,128]{2,1,0:T(8,128)} %get-tuple-element.10), channel_id=1, source_target_pairs={{0,32},{32,64},{64,96},{1,33},{33,65},{65,97},{2,34},{34,66},{66,9... | collective-permute-start | bytes 442376 | tf_op jit(solution)/shard_map/ppermute | solution.py:376
  80.4 15.5 %collective-permute-start.1 = (f32[3,72,128]{2,1,0:T(8,128)S(1)}, f32[3,72,128]{2,1,0:T(8,128)S(1)}, u32[]{:S(2)}, u32[]{:S(2)}) collective-permute-start(f32[3,72,128]{2,1,0:T(8,128)S(1)} %get-tuple-element.20), channel_id=1, source_target_pairs={{1,0},{2,1},{3,2},{4,3},{5,4},{6,5},{7,6},{8,7},{9,8},{10,9},{11,1... | collective-permute-start | bytes 331784 | tf_op jit(solution)/shard_map/ppermute | solution.py:380
  86.9 8.3 %collective-permute-start = (f32[4,72,128]{2,1,0:T(8,128)S(1)}, f32[4,72,128]{2,1,0:T(8,128)S(1)}, u32[]{:S(2)}, u32[]{:S(2)}) collective-permute-start(f32[4,72,128]{2,1,0:T(8,128)S(1)} %pad_maximum_fusion), channel_id=1, source_target_pairs={{0,1},{1,2},{2,3},{3,4},{4,5},{5,6},{6,7},{7,8},{8,9},{9,10},{10,1... | collective-permute-start | bytes 442376 | tf_op jit(solution)/shard_map/ppermute | solution.py:379
  88.5 7.3 %copy-start.1 = (f32[4,72,128]{2,1,0:T(8,128)}, f32[4,72,128]{2,1,0:T(8,128)S(1)}, u32[]{:S(2)}) copy-start(f32[4,72,128]{2,1,0:T(8,128)S(1)} %collective-permute-done.2.south) | copy-start | bytes 442372
  95.2 0.7 copy-start.2
  95.9 0.7 copy-start.3
  95.9 0.7 copy-start.4
  119.0 1.2 copy-start
  227.6 8.4 %collective-permute-start.6 = (f32[3,72,128]{2,1,0:T(8,128)}, f32[3,72,128]{2,1,0:T(8,128)S(1)}, u32[]{:S(2)}, u32[]{:S(2)}) collective-permute-start(f32[3,72,128]{2,1,0:T(8,128)} %get-tuple-element.13), channel_id=1, source_target_pairs={{0,32},{32,64},{64,96},{1,33},{33,65},{65,97},{2,34},{34,66},{66,9... | collective-permute-start | bytes 331784 | tf_op jit(solution)/shard_map/ppermute | solution.py:388
  231.6 7.8 %collective-permute-start.7 = (f32[3,72,128]{2,1,0:T(8,128)}, f32[3,72,128]{2,1,0:T(8,128)S(1)}, u32[]{:S(2)}, u32[]{:S(2)}) collective-permute-start(f32[3,72,128]{2,1,0:T(8,128)} %get-tuple-element.14), channel_id=1, source_target_pairs={{32,0},{64,32},{96,64},{33,1},{65,33},{97,65},{34,2},{66,34},{98,6... | collective-permute-start | bytes 331784 | tf_op jit(solution)/shard_map/ppermute | solution.py:389
  234.5 4.9 %collective-permute-start.5 = (f32[3,72,128]{2,1,0:T(8,128)S(1)}, f32[3,72,128]{2,1,0:T(8,128)S(1)}, u32[]{:S(2)}, u32[]{:S(2)}) collective-permute-start(f32[3,72,128]{2,1,0:T(8,128)S(1)} %get-tuple-element.18), channel_id=1, source_target_pairs={{1,0},{2,1},{3,2},{4,3},{5,4},{6,5},{7,6},{8,7},{9,8},{10,9},{11,1... | collective-permute-start | bytes 331784 | tf_op jit(solution)/shard_map/ppermute | solution.py:391
  234.6 7.9 %collective-permute-start.4 = (f32[3,72,128]{2,1,0:T(8,128)S(1)}, f32[3,72,128]{2,1,0:T(8,128)S(1)}, u32[]{:S(2)}, u32[]{:S(2)}) collective-permute-start(f32[3,72,128]{2,1,0:T(8,128)S(1)} %get-tuple-element.19), channel_id=1, source_target_pairs={{0,1},{1,2},{2,3},{3,4},{4,5},{5,6},{6,7},{7,8},{8,9},{9,10},{10,1... | collective-permute-start | bytes 331784 | tf_op jit(solution)/shard_map/ppermute | solution.py:390
  236.0 6.4 %copy-start.5 = (f32[3,72,128]{2,1,0:T(8,128)}, f32[3,72,128]{2,1,0:T(8,128)S(1)}, u32[]{:S(2)}) copy-start(f32[3,72,128]{2,1,0:T(8,128)S(1)} %collective-permute-done.6.south) | copy-start | bytes 331780
  239.4 3.1 %copy-start.6 = (f32[3,72,128]{2,1,0:T(8,128)}, f32[3,72,128]{2,1,0:T(8,128)S(1)}, u32[]{:S(2)}) copy-start(f32[3,72,128]{2,1,0:T(8,128)S(1)} %collective-permute-done.7.north) | copy-start | bytes 331780
  239.4 3.1 %copy-start.7 = (f32[3,72,128]{2,1,0:T(8,128)}, f32[3,72,128]{2,1,0:T(8,128)S(1)}, u32[]{:S(2)}) copy-start(f32[3,72,128]{2,1,0:T(8,128)S(1)} %collective-permute-done.5.east_col) | copy-start | bytes 331780
  242.5 0.7 copy-start.8

commit v2 on v1

v2 whole, which is shorter than its diff:
```python
import functools

import jax
import jax.numpy as jnp
from jax import lax
from jax.experimental import pallas as pl
from jax.experimental.pallas import tpu as pltpu
from jax.sharding import PartitionSpec as P

kappa_mix = 0.05
LANES = 128
WIDE = 256
f32 = jnp.float32
bf16 = jnp.bfloat16
BLOCK = 9
VMEM_LIMIT = 56 * 2**20


def call(kernel, out_shape, *args, scratch=(), smem=(), flops=0, nbytes=0):
    specs = [
        pl.BlockSpec(memory_space=pltpu.SMEM if i in smem else pltpu.VMEM) for i in range(len(args))
    ]
    return pl.pallas_call(
        kernel,
        out_shape=out_shape,
        in_specs=specs,
        out_specs=jax.tree.map(lambda _: pl.BlockSpec(memory_space=pltpu.VMEM), out_shape),
        scratch_shapes=list(scratch),
        compiler_params=pltpu.CompilerParams(vmem_limit_bytes=VMEM_LIMIT),
        cost_estimate=pl.CostEstimate(flops=flops, bytes_accessed=nbytes, transcendentals=0),
    )(*args)


def split(value):
    high = value.astype(bf16).astype(f32)
    return high, value - high


def nt_dot(a, b):
    return lax.dot_general(a, b, (((1,), (1,)), ((), ())), preferred_element_type=f32)


def onehot_product(parts, group, spot, total, count, step, together, depth):
    rows, length = parts.shape
    chunks = length // depth

    def of_group(g, carry):
        def of_chunk(c, carry):
            at = pl.ds(pl.multiple_of(c * depth, depth), depth)
            held, key = parts[:, at], group[:, at]
            left = jnp.concatenate(
                [
                    jnp.where(
                        key == ((g * together + i) * step).astype(f32).astype(bf16), held, jnp.zeros_like(held)
                    )
                    for i in range(together)
                ],
                axis=0,
            )
            product = nt_dot(left, spot[:, at])
            to = pl.ds(pl.multiple_of(g * (together * rows), together * rows), together * rows)
            if chunks == 1:
                total[to, :] = product
            else:

                @pl.when(c == 0)
                def _():
                    total[to, :] = product

                @pl.when(c > 0)
                def _():
                    total[to, :] += product

            return carry

        return lax.fori_loop(0, chunks, of_chunk, carry)

    lax.fori_loop(0, count // together, of_group, 0)


PACK = (16, 8192)
ADD = (17, 4096)


def whole_part(value, divisor):
    return ((value.astype(f32) + 0.5) * (1.0 / divisor)).astype(jnp.int32)


def pack_kernel(dest, values, target, out, parts, group, spot, total, *, species, cols, rows):
    n_tiles, held, _ = out.shape
    levels, length = values.shape
    iota_t = lax.broadcasted_iota(jnp.int32, (n_tiles, WIDE), 0)
    square = (WIDE, WIDE)
    upper = (
        lax.broadcasted_iota(jnp.int32, square, 0) < lax.broadcasted_iota(jnp.int32, square, 1)
    ).astype(f32).astype(bf16)
    iota_w = lax.broadcasted_iota(jnp.int32, square, 0)

    def rank(at, base):
        d = dest[:, at]
        hot = iota_t == d
        hot_f = jnp.where(hot, 1.0, 0.0)
        earlier = jnp.dot(hot_f.astype(bf16), upper, preferred_element_type=f32) + base
        own = jnp.sum(jnp.where(hot, earlier, 0.0), axis=0, keepdims=True).astype(jnp.int32)
        low = own + (d & 1) * LANES
        spot[:, at] = jnp.where(iota_w == low, 1.0, 0.0).astype(bf16)
        group[:, at] = jnp.broadcast_to((d >> 1).astype(f32), (2 * held, WIDE)).astype(bf16)
        t = target[:, at]
        cell = whole_part(t, species)
        row_of = whole_part(cell, cols)
        segment = ((t - cell * species) * cols + cell - row_of * cols) * rows + row_of
        row = jnp.concatenate(
            [values[:, at], segment.astype(f32), jnp.zeros((held - levels - 1, WIDE), f32)], axis=0
        )
        parts[:, at] = jnp.concatenate(split(row), axis=0).astype(bf16)
        return base + jnp.sum(hot_f, axis=1, keepdims=True)

    def ranks(b, base):
        for i in range(4):
            base = rank(pl.ds(pl.multiple_of((4 * b + i) * WIDE, WIDE), WIDE), base)
        return base

    lax.fori_loop(0, length // (4 * WIDE), ranks, jnp.zeros((n_tiles, 1), f32))
    onehot_product(parts, group, spot, total, n_tiles // 2, 1, *PACK)

    def put(g, carry):
        for i in range(4):
            j = 4 * g + i
            at = pl.multiple_of(j * 2 * held, 2 * held)
            both = total[pl.ds(at, held), :] + total[pl.ds(at + held, held), :]
            out[2 * j] = both[:, :LANES]
            out[2 * j + 1] = both[:, LANES:]
        return carry

    lax.fori_loop(0, n_tiles // 8, put, 0)


def pack(dest, values, target, n_tiles, species, cols, rows):
    levels, length = values.shape
    held = -(-(levels + 1) // 8) * 8
    scratch = (
        pltpu.VMEM((2 * held, length), bf16),
        pltpu.VMEM((2 * held, length), bf16),
        pltpu.VMEM((WIDE, length), bf16),
        pltpu.VMEM((n_tiles // 2 * 2 * held, WIDE), f32),
    )
    return call(
        functools.partial(pack_kernel, species=species, cols=cols, rows=rows),
        jax.ShapeDtypeStruct((n_tiles, held, LANES), f32),
        dest.reshape(1, length),
        values,
        target.reshape(1, length),
        scratch=scratch,
        flops=2 * length * n_tiles * LANES * 2 * held,
        nbytes=4 * (length * 22 + n_tiles * held * LANES),
    )


def lane_put(kept, lane, x, value, by):
    return jnp.where(lane == x, pltpu.roll(value, by, 1), kept)


def edges_kernel(field, clat, up, down):
    species, block, levels, rows = field.shape
    lane = lax.broadcasted_iota(jnp.int32, (levels, rows), 1)
    first = pl.program_id(0) * block

    @pl.when(first == 0)
    def _():
        up[...] = jnp.zeros_like(up)
        down[...] = jnp.zeros_like(down)

    for s in range(species + 1):
        u = up[s]
        for i in range(block):
            x = first + i
            u = lane_put(u, lane, x, field[s, i] if s < species else clat[i], x + 1)
        up[s] = u
        if s < species:
            d = down[s]
            for i in range(block):
                x = first + i
                d = lane_put(d, lane, x, field[s, i], x)
            down[s] = d


def edges(field, clat):
    species, cols, levels, rows = field.shape
    up, down = (species + 1, levels, rows), (species, levels, rows)
    return pl.pallas_call(
        edges_kernel,
        out_shape=(jax.ShapeDtypeStruct(up, f32), jax.ShapeDtypeStruct(down, f32)),
        grid=(cols // BLOCK,),
        in_specs=[
            pl.BlockSpec((species, BLOCK, levels, rows), lambda i: (0, i, 0, 0)),
            pl.BlockSpec((BLOCK, levels, rows), lambda i: (i, 0, 0)),
        ],
        out_specs=(pl.BlockSpec(up, lambda i: (0, 0, 0)), pl.BlockSpec(down, lambda i: (0, 0, 0))),
        compiler_params=pltpu.CompilerParams(vmem_limit_bytes=VMEM_LIMIT),
        cost_estimate=pl.CostEstimate(flops=field.size * 4, bytes_accessed=field.size * 5, transcendentals=0),
    )(field, clat)


def mix_weights(vertical_mix):
    levels = vertical_mix.shape[0]
    matrix = (jnp.eye(levels, dtype=f32) + vertical_mix).T
    high = lax.reduce_precision(matrix, 8, 7)
    return jnp.concatenate([high, high, matrix - high], axis=1).astype(bf16)


def step_kernel(
    lat_ref,
    field,
    field_west,
    field_east,
    clon,
    clon_before,
    clat,
    west_col,
    east_col,
    clon_col,
    south,
    north,
    clat_south,
    weights,
    *refs,
    lat_size,
):
    species, block, levels, rows = field.shape
    lane = lax.broadcasted_iota(jnp.int32, (levels, rows), 1)
    first, last = lane == 0, lane == rows - 1
    lat = lat_ref[0]
    below = jnp.where(jnp.logical_and(first, lat == 0), 0.0, 1.0)
    inside = jnp.where(jnp.logical_and(last, lat == lat_size - 1), 0.0, 1.0)
    w = weights[...]
    here = pl.program_id(0)
    at_start, at_end = here == 0, here == pl.num_programs(0) - 1
    waiting = []

    def mix(ready):
        mixed = jnp.dot(
            w, jnp.concatenate([r for _, _, r in ready], axis=1), preferred_element_type=f32
        )
        for k, (s, i, _) in enumerate(ready):
            m = mixed[:, k * rows : (k + 1) * rows]
            if len(refs) == 1:
                refs[0][s, i] = m
            else:
                level0, out, flux = refs
                x = here * block + i
                out[s, i] = m
                flux[s, pl.ds(x, 1), :] = level0[s, pl.ds(x, 1), :] + m[0:1]

    for i in range(block):
        x = here * block + i
        cl, cw = clon[i], clat[i]
        cl_west = clon[i - 1] if i else jnp.where(at_start, clon_col[0], clon_before[0])
        e = jnp.maximum(cl, 0.0) + kappa_mix
        w_ = kappa_mix - jnp.minimum(cl_west, 0.0)
        n = (jnp.maximum(cw, 0.0) + kappa_mix) * inside
        cs = jnp.where(first, pltpu.roll(clat_south[0], lax.rem(rows - x, rows), 1), pltpu.roll(cw, 1, 1))
        s_ = (kappa_mix - jnp.minimum(cs, 0.0)) * below
        centre = 1.0 - (e + w_ + n + s_)
        for s in range(species):
            v = field[s, i]
            v_w = field[s, i - 1] if i else jnp.where(at_start, west_col[s], field_west[s, 0])
            v_e = field[s, i + 1] if i < block - 1 else jnp.where(at_end, east_col[s], field_east[s, 0])
            v_n = jnp.where(last, pltpu.roll(north[s], rows - 1 - x, 1), pltpu.roll(v, rows - 1, 1))
            v_s = jnp.where(first, pltpu.roll(south[s], lax.rem(rows - x, rows), 1), pltpu.roll(v, 1, 1))
            h = centre * v + e * v_e + w_ * v_w + n * v_n + s_ * v_s
            high, low = split(h)
            waiting.append((s, i, jnp.concatenate([high, low, high], axis=0).astype(bf16)))
            if len(waiting) == 2:
                mix(waiting)
                waiting.clear()
    if waiting:
        mix(waiting)


def step(lat, field, clon, clat, halo, weights, lat_size, level0=None):
    species, cols, levels, rows = field.shape
    shapes = [jax.ShapeDtypeStruct(field.shape, f32)]
    columns = pl.BlockSpec((species, BLOCK, levels, rows), lambda i: (0, i, 0, 0))
    courant = pl.BlockSpec((BLOCK, levels, rows), lambda i: (i, 0, 0))
    out_specs = [columns]
    whole = lambda shape: pl.BlockSpec(shape, lambda i: (0,) * len(shape))
    part = lambda at: pl.BlockSpec((1, levels, rows), lambda i: (at, 0, 0))
    more = ()
    if level0 is not None:
        more = (level0,)
        shapes.append(jax.ShapeDtypeStruct(level0.shape, f32))
        out_specs.append(whole(level0.shape))
    west, east, clon_west, south, north, clat_south = halo
    three = whole((species, levels, rows))
    return pl.pallas_call(
        functools.partial(step_kernel, lat_size=lat_size),
        out_shape=shapes,
        grid=(cols // BLOCK,),
        in_specs=[
            pl.BlockSpec(memory_space=pltpu.SMEM),
            columns,
            pl.BlockSpec((species, 1, levels, rows), lambda i: (0, jnp.maximum(i * BLOCK - 1, 0), 0, 0)),
            pl.BlockSpec((species, 1, levels, rows), lambda i: (0, jnp.minimum(i * BLOCK + BLOCK, cols - 1), 0, 0)),
            courant,
            pl.BlockSpec((1, levels, rows), lambda i: (jnp.maximum(i * BLOCK - 1, 0), 0, 0)),
            courant,
            three,
            three,
            part(species),
            three,
            three,
            part(species),
            whole(weights.shape),
            *[whole(m.shape) for m in more],
        ],
        out_specs=out_specs,
        compiler_params=pltpu.CompilerParams(vmem_limit_bytes=VMEM_LIMIT),
        cost_estimate=pl.CostEstimate(
            flops=field.size * levels * 6, bytes_accessed=field.size * 12, transcendentals=0
        ),
    )(
        lat,
        field,
        field,
        field,
        clon,
        clon,
        clat,
        west,
        east,
        clon_west,
        south,
        north,
        clat_south,
        weights,
        *more,
    )


def add_kernel(
    got, plain, table, first, up, down, west, east, level0, parts, group, spot, total, held_field, sem_in, sem_out
):
    sources, held, slots = got.shape
    species, cols, levels, rows = plain.shape
    akl = table.shape[1] // 4
    fetch = pltpu.make_async_copy(plain, held_field, sem_in)
    fetch.start()
    iota_w = lax.broadcasted_iota(jnp.int32, (WIDE, WIDE), 0)
    second = (lax.broadcasted_iota(jnp.int32, (4 * akl, WIDE), 0) >= 2 * akl).astype(f32)

    def prepare(g, carry):
        for i in range(2):
            b = 2 * g + i
            row = jnp.concatenate([got[2 * b], got[2 * b + 1]], axis=1)
            at = pl.ds(pl.multiple_of(b * WIDE, WIDE), WIDE)
            segment = row[akl : akl + 1].astype(jnp.int32)
            spot[:, at] = jnp.where(iota_w == (segment & (WIDE - 1)), 1.0, 0.0).astype(bf16)
            group[:, at] = ((segment >> 8).astype(f32) - second).astype(bf16)
            high, low = split(row[:akl])
            both = jnp.concatenate([high, low], axis=0)
            parts[:, at] = jnp.concatenate([both, both], axis=0).astype(bf16)
        return carry

    lax.fori_loop(0, sources // 4, prepare, 0)
    onehot_product(parts, group, spot, total, -(-species * cols // 4), 2, *ADD)

    lane = lax.broadcasted_iota(jnp.int32, (levels, rows), 1)
    up[...] = jnp.zeros_like(up)
    down[...] = jnp.zeros_like(down)
    t = table[...]
    fetch.wait()
    blocks = cols // BLOCK

    def leave(s, b):
        at = pl.ds(b * BLOCK, BLOCK)
        return pltpu.make_async_copy(held_field.at[s, at], first.at[s, at], sem_out.at[s, b])

    for s in range(species):

        def columns(b, carry):
            u, d = up[s], down[s]
            for i in range(BLOCK):
                x = b * BLOCK + i
                sx = s * cols + x
                pair = total[
                    pl.ds(pl.multiple_of((sx >> 1) * 2 * akl, 8), 2 * akl),
                    pl.ds(pl.multiple_of((sx & 1) * rows, rows), rows),
                ]
                high, low = split(pair)
                forcing = jnp.dot(
                    t, jnp.concatenate([high, low], axis=0).astype(bf16), preferred_element_type=f32
                )
                v = held_field[s, x] + forcing
                held_field[s, x] = v
                level0[s, pl.ds(x, 1), :] = v[0:1]
                u = lane_put(u, lane, x, v, x + 1)
                d = lane_put(d, lane, x, v, x)
            up[s] = u
            down[s] = d
            leave(s, b).start()
            return carry

        lax.fori_loop(0, blocks, columns, 0)
        east[s] = held_field[s, 0]
        west[s] = held_field[s, cols - 1]
    for s in range(species):
        for b in range(blocks):
            leave(s, b).wait()


def add_soundings(got, plain, table):
    sources, held, slots = got.shape
    species, cols, levels, rows = plain.shape
    akl = table.shape[1] // 4
    length = sources * slots
    pairs = -(-species * cols // 4)
    edge = jax.ShapeDtypeStruct((species, levels, rows), f32)
    vmem, hbm = pl.BlockSpec(memory_space=pltpu.VMEM), pl.BlockSpec(memory_space=pl.ANY)
    return pl.pallas_call(
        add_kernel,
        out_shape=(
            jax.ShapeDtypeStruct(plain.shape, f32),
            edge,
            edge,
            edge,
            edge,
            jax.ShapeDtypeStruct((species, cols, rows), f32),
        ),
        in_specs=[vmem, hbm, vmem],
        out_specs=(hbm, vmem, vmem, vmem, vmem, vmem),
        scratch_shapes=(
            pltpu.VMEM((4 * akl, length), bf16),
            pltpu.VMEM((4 * akl, length), bf16),
            pltpu.VMEM((WIDE, length), bf16),
            pltpu.VMEM((pairs * 4 * akl, WIDE), f32),
            pltpu.VMEM(plain.shape, f32),
            pltpu.SemaphoreType.DMA,
            pltpu.SemaphoreType.DMA((species, cols // BLOCK)),
        ),
        compiler_params=pltpu.CompilerParams(vmem_limit_bytes=VMEM_LIMIT),
        cost_estimate=pl.CostEstimate(
            flops=2 * pairs * 4 * akl * WIDE * length,
            bytes_accessed=4 * (got.size + 2 * plain.size),
            transcendentals=0,
        ),
    )(got, plain, table)


def on_device(
    adjoint_in,
    courant_lon,
    courant_lat,
    vertical_mix,
    sounding_values,
    sounding_dest,
    sounding_target,
    level_index,
):
    lat_size, lon_size = lax.axis_size("lat"), lax.axis_size("lon")
    n_tiles = lat_size * lon_size
    species, levels, cols, rows = adjoint_in.shape
    east_way = [(i, (i + 1) % lon_size) for i in range(lon_size)]
    west_way = [(j, i) for i, j in east_way]
    north_way = [(i, i + 1) for i in range(lat_size - 1)]
    south_way = [(j, i) for i, j in north_way]

    field = adjoint_in.transpose(0, 2, 1, 3)
    clon = courant_lon.transpose(1, 0, 2)
    clat = courant_lat.transpose(1, 0, 2)
    lat = lax.axis_index("lat").reshape(1)

    sent = pack(sounding_dest, sounding_values, sounding_target, n_tiles, species, cols, rows)
    got = lax.all_to_all(sent, ("lat", "lon"), split_axis=0, concat_axis=0, tiled=True)

    up, down = edges(field, clat)
    clat_south = south = lax.ppermute(up, "lat", north_way)
    north = lax.ppermute(down, "lat", south_way)
    clon_west = west = lax.ppermute(
        jnp.concatenate([field[:, cols - 1], clon[None, cols - 1]], axis=0), "lon", east_way
    )
    east = lax.ppermute(field[:, 0], "lon", west_way)

    weights = mix_weights(vertical_mix)
    table = (jnp.arange(levels, dtype=jnp.int32)[:, None] == level_index[None, :]).astype(bf16)
    table = jnp.concatenate([table] * 4, axis=1)
    (plain,) = step(lat, field, clon, clat, (west, east, clon_west, south, north, clat_south), weights, lat_size)
    first, up, down, west, east, level0 = add_soundings(got, plain, table)
    south = lax.ppermute(up, "lat", north_way)
    north = lax.ppermute(down, "lat", south_way)
    west = lax.ppermute(west, "lon", east_way)
    east = lax.ppermute(east, "lon", west_way)
    out, flux = step(
        lat, first, clon, clat, (west, east, clon_west, south, north, clat_south), weights, lat_size, level0
    )
    return out.transpose(0, 2, 1, 3), flux


def solution(mesh):
    return jax.shard_map(
        on_device,
        mesh=mesh,
        in_specs=(
            P(None, None, "lon", "lat"),
            P(None, "lon", "lat"),
            P(None, "lon", "lat"),
            P(),
            P(None, ("lat", "lon")),
            P(("lat", "lon"), None),
            P(("lat", "lon")),
            P(),
        ),
        out_specs=(P(None, None, "lon", "lat"), P(None, "lon", "lat")),
        check_vma=False,
    )
```

time: 266 us -> 144 us (0.54)
  Pallas kernels: 206 us -> 85.7 us
  starting transfers between devices: 32.1 us -> 36.8 us
  local copies, waits for them, and re-layouts: 9.62 us -> 6.11 us
  other arithmetic: 4.38 us -> 1.45 us
    pallas_call x5 -> x1, Pallas kernels: 206 us -> 20.3 us  [call(): pl.pallas_call(kernel, out_shape=out_shape, in_specs=specs, out_specs=jax...]
    pallas_call x0 -> x4, Pallas kernels: none -> 65.4 us  [the longest x1 37 us: add_soundings(): pl.pallas_call(add_kernel, out_shape=(jax.ShapeDtypeStruct(plain.shape, f...]
    ppermute x2 -> x3, starting transfers between devices: 1.53 us -> 10.1 us  [the longest x1 5.67 us: on_device(): east = lax.ppermute(east, 'lon', west_way)]
    ppermute x2 -> x1, starting transfers between devices: 8.33 us -> 4.49 us  [on_device(): south = lax.ppermute(up, 'lat', north_way)]
    ppermute x2 -> x3, waiting for transfers between devices: 3.09 us -> 0.01 us  [the longest x1 0.01 us: on_device(): east = lax.ppermute(east, 'lon', west_way)]
    unnamed x25 -> x24, local copies, waits for them, and re-layouts: 5.89 us -> 5.32 us
  transfers between devices with their start and end apart: 9 -> 9, of which waited for: 3 -> 3; matrix products, arithmetic and copies ran while one was open for 3% -> 4% of each run, Pallas kernels for 12% -> 12%
where the time goes in v2:
time: 144 us; the launch traced here: 143 us
  Pallas kernels  85.7 us (60%)
  starting transfers between devices  36.8 us (26%)
  waiting for transfers between devices  12.4 us (9%)
  local copies, waits for them, and re-layouts  6.11 us (4%)
  other arithmetic  1.45 us (1%)
    pallas_call x1, Pallas kernels, add_soundings(): pl.pallas_call(add_kernel, out_shape=(jax.ShapeDtypeStruct(plain.shape, f...  37 us
    pallas_call x2, Pallas kernels, step(): pl.pallas_call(functools.partial(step_kernel, lat_size=lat_size), out_sha...  21.8 us
    pallas_call x1, Pallas kernels, call(): pl.pallas_call(kernel, out_shape=out_shape, in_specs=specs, out_specs=jax...  20.3 us
    all_to_all x1, starting transfers between devices, on_device(): lax.all_to_all(sent, ('lat', 'lon'), split_axis=0, concat_axis=0, tiled=T...  11.5 us
    pallas_call x1, Pallas kernels, edges(): pl.pallas_call(edges_kernel, out_shape=(jax.ShapeDtypeStruct(up, f32), ja...  6.6 us
    ppermute x1, waiting for transfers between devices, on_device(): lax.ppermute(jnp.concatenate([field[:, cols - 1], clon[None, cols - 1]],...  6.6 us
    ppermute x1, starting transfers between devices, on_device(): east = lax.ppermute(field[:, 0], 'lon', west_way)  5.76 us
    ppermute x2, waiting for transfers between devices, on_device(): north = lax.ppermute(down, 'lat', south_way)  5.73 us
  transfers between devices with their start and end apart: 9, of which 3 were waited for; matrix products, arithmetic and copies ran while one was open for 4% of the time, Pallas kernels for 12%

profile of v2, /device:TPU:1, one launch (start us, length us, event | category | flops | bytes accessed | tf_op | source)
XLA Modules:
  0.0 143.4 jit_solution(1024689944371538365)
XLA Ops:
  0.6 20.3 %shard_map.95 = f32[128,24,128]{2,1,0:T(8,128)} custom-call(s32[1,8192]{1,0:T(1,128)} %bitcast.31, f32[20,8192]{1,0:T(8,128)} %values.1, s32[1,8192]{1,0:T(1,128)} %bitcast.32), custom_call_target="tpu_custom_call" | custom-call | flops 12884901888 | bytes 2293760 | tf_op jit(solution)/shard_map/pallas_call | solution.py:23
  21.0 11.5 %all-to-all-start = ((f32[128,24,128]{2,1,0:T(8,128)}), f32[128,24,128]{2,1,0:T(8,128)S(1)}, u32[]{:S(2)}, u32[]{:S(2)}) async-start(f32[128,24,128]{2,1,0:T(8,128)} %shard_map.95), calls=%async_computation | async-start | bytes 3145728 | tf_op jit(solution)/shard_map/all_to_all | solution.py:473
  32.5 6.6 %shard_map.96 = (f32[4,72,128]{2,1,0:T(8,128)}, f32[3,72,128]{2,1,0:T(8,128)}) custom-call(f32[3,45,72,128]{3,2,1,0:T(8,128)} %bitcast.17, f32[45,72,128]{2,1,0:T(8,128)} %bitcast.26), custom_call_target="tpu_custom_call" | custom-call | flops 4976640 | bytes 6220800 | tf_op jit(solution)/shard_map/pallas_call | solution.py:190
  39.1 3.0 %collective-permute-start.3 = (f32[3,72,128]{2,1,0:T(8,128)}, f32[3,72,128]{2,1,0:T(8,128)S(1)}, u32[]{:S(2)}, u32[]{:S(2)}) collective-permute-start(f32[3,72,128]{2,1,0:T(8,128)} %get-tuple-element.13), channel_id=1, source_target_pairs={{32,0},{64,32},{96,64},{33,1},{65,33},{97,65},{34,2},{66,34},{98,6... | collective-permute-start | bytes 331784 | tf_op jit(solution)/shard_map/ppermute | solution.py:477
  42.0 0.0 copy-start.9
  42.1 0.0 copy-start.10
  42.1 4.4 %collective-permute-start.2 = (f32[4,72,128]{2,1,0:T(8,128)}, f32[4,72,128]{2,1,0:T(8,128)S(1)}, u32[]{:S(2)}, u32[]{:S(2)}) collective-permute-start(f32[4,72,128]{2,1,0:T(8,128)} %get-tuple-element.12), channel_id=1, source_target_pairs={{0,32},{32,64},{64,96},{1,33},{33,65},{65,97},{2,34},{34,66},{66,9... | collective-permute-start | bytes 442376 | tf_op jit(solution)/shard_map/ppermute | solution.py:476
  46.5 2.7 %copy.18 = f32[3,72,45,128]{3,1,0,2:T(8,128)S(1)} copy(f32[3,72,45,128]{3,1,2,0:T(8,128)} %param.8) | data formatting | bytes 9953280 | tf_op args[0]
  49.2 5.8 %collective-permute-start.1 = (f32[3,72,128]{2,1,0:T(8,128)S(1)}, f32[3,72,128]{2,1,0:T(8,128)S(1)}, u32[]{:S(2)}, u32[]{:S(2)}) collective-permute-start(f32[3,72,128]{2,1,0:T(8,128)S(1)} %get-tuple-element.22), channel_id=1, source_target_pairs={{1,0},{2,1},{3,2},{4,3},{5,4},{6,5},{7,6},{8,7},{9,8},{10,9},{11,1... | collective-permute-start | bytes 331784 | tf_op jit(solution)/shard_map/ppermute | solution.py:481
  55.0 0.8 slice.13
  55.8 0.1 collective-permute-start
  55.8 0.0 copy-done.9
  55.9 0.1 copy.12
  55.9 0.0 copy-done.10
  56.0 0.7 pad_maximum_fusion.1.weights
  56.7 0.7 add_convert_fusion.table
  57.4 0.0 collective-permute-done.3.north
  57.4 0.0 copy-start.7
  57.4 0.0 collective-permute-done.1.east_col
  57.4 0.0 copy-start.8
  57.4 0.0 collective-permute-done.2.south.clat_south
  57.4 0.0 copy-start.1
  57.4 6.6 %collective-permute-done.west_col.clon_col = f32[4,72,128]{2,1,0:T(8,128)S(1)} collective-permute-done((f32[4,72,128]{2,1,0:T(8,128)S(1)}, f32[4,72,128]{2,1,0:T(8,128)S(1)}, u32[]{:S(2)}, u32[]{:S(2)}) %collective-permute-start) | collective-permute-done | bytes 147488 | tf_op jit(solution)/shard_map/ppermute | solution.py:478
  64.0 0.0 copy-start.2
  64.0 0.0 copy-done.7
  64.0 0.0 copy-done.8
  64.0 0.0 copy-done.1
  64.1 0.6 copy-done.2
  64.7 10.8 %shard_map.97.plain = f32[3,45,72,128]{3,2,1,0:T(8,128)} custom-call(s32[1]{0:T(128)} %bitcast.lat_ref, f32[3,45,72,128]{3,2,1,0:T(8,128)} %bitcast.18, f32[3,45,72,128]{3,2,1,0:T(8,128)} %bitcast.19, f32[3,45,72,128]{3,2,1,0:T(8,128)} %bitcast.20, f32[45,72,128]{2,1,0:T(8,128)} %bitcast.22, f32[45,72,128]{2,1,0:T(8,128)} %bitcast.23, ...), custom_call_target="tpu_custom_call" | custom-call | flops 537477120 | bytes 14929920 | tf_op jit(solution)/shard_map/pallas_call | solution.py:295
  75.5 0.0 all-to-all-done.got
  75.5 0.0 copy-start
  75.6 1.2 copy-done
  76.8 37.0 %shard_map.98 = (f32[3,45,72,128]{3,2,1,0:T(8,128)}, f32[3,72,128]{2,1,0:T(8,128)}, f32[3,72,128]{2,1,0:T(8,128)}, f32[3,72,128]{2,1,0:T(8,128)}, f32[3,72,128]{2,1,0:T(8,128)}, /*index=5*/f32[3,45,128]{2,1,0:T(8,128)}) custom-call(f32[128,24,128]{2,1,0:T(8,128)} %copy-done, f32[3,45,72,128]{3,2,1,0:T(8,128)} %shard_map.97.plain, ...), custom_call_target="tpu_custom_call" | custom-call | flops 22817013760 | bytes 11526144 | tf_op jit(solution)/shard_map/pallas_call | solution.py:419
  113.8 0.1 collective-permute-start.4
  113.9 5.7 %collective-permute-start.5 = (f32[3,72,128]{2,1,0:T(8,128)}, f32[3,72,128]{2,1,0:T(8,128)S(1)}, u32[]{:S(2)}, u32[]{:S(2)}) collective-permute-start(f32[3,72,128]{2,1,0:T(8,128)} %get-tuple-element.16), channel_id=1, source_target_pairs={{1,0},{2,1},{3,2},{4,3},{5,4},{6,5},{7,6},{8,7},{9,8},{10,9},{11,1... | collective-permute-start | bytes 331784 | tf_op jit(solution)/shard_map/ppermute | solution.py:491
  119.5 4.5 %collective-permute-start.6 = (f32[3,72,128]{2,1,0:T(8,128)}, f32[3,72,128]{2,1,0:T(8,128)S(1)}, u32[]{:S(2)}, u32[]{:S(2)}) collective-permute-start(f32[3,72,128]{2,1,0:T(8,128)} %get-tuple-element.17), channel_id=1, source_target_pairs={{0,32},{32,64},{64,96},{1,33},{33,65},{65,97},{2,34},{34,66},{66,9... | collective-permute-start | bytes 331784 | tf_op jit(solution)/shard_map/ppermute | solution.py:488
  124.0 1.9 %collective-permute-start.7 = (f32[3,72,128]{2,1,0:T(8,128)}, f32[3,72,128]{2,1,0:T(8,128)S(1)}, u32[]{:S(2)}, u32[]{:S(2)}) collective-permute-start(f32[3,72,128]{2,1,0:T(8,128)} %get-tuple-element.18), channel_id=1, source_target_pairs={{32,0},{64,32},{96,64},{33,1},{65,33},{97,65},{34,2},{66,34},{98,6... | collective-permute-start | bytes 331784 | tf_op jit(solution)/shard_map/ppermute | solution.py:489
  126.0 0.0 collective-permute-done.4.west_col
  126.0 0.0 copy-start.3
  126.0 0.0 collective-permute-done.5.east_col
  126.0 0.0 copy-start.4
  126.0 0.1 collective-permute-done.6.south
  126.1 0.0 copy-start.5
  126.1 5.7 %collective-permute-done.7.north = f32[3,72,128]{2,1,0:T(8,128)S(1)} collective-permute-done((f32[3,72,128]{2,1,0:T(8,128)}, f32[3,72,128]{2,1,0:T(8,128)S(1)}, u32[]{:S(2)}, u32[]{:S(2)}) %collective-permute-start.7) | collective-permute-done | bytes 110624 | tf_op jit(solution)/shard_map/ppermute | solution.py:489
  131.8 0.0 copy-start.6
  131.8 0.0 copy-done.3
  131.8 0.0 copy-done.4
  131.8 0.0 copy-done.5
  131.8 0.6 copy-done.6
  132.5 10.9 %shard_map.99 = (f32[3,45,72,128]{3,2,1,0:T(8,128)}, f32[3,45,128]{2,1,0:T(8,128)}) custom-call(s32[1]{0:T(128)} %bitcast.lat_ref, f32[3,45,72,128]{3,2,1,0:T(8,128)} %get-tuple-element.14.field.field_west.field_east, f32[3,45,72,128]{3,2,1,0:T(8,128)} %get-tuple-element.14.field.field_west.field_east, ...), custom_call_target="tpu_custom_call" | custom-call | flops 537477120 | bytes 14929920 | tf_op jit(solution)/shard_map/pallas_call | solution.py:295
  (4 shorter events, 0.1 us)
Async XLA Ops:
  21.0 54.6 %all-to-all-start = ((f32[128,24,128]{2,1,0:T(8,128)}), f32[128,24,128]{2,1,0:T(8,128)S(1)}, u32[]{:S(2)}, u32[]{:S(2)}) async-start(f32[128,24,128]{2,1,0:T(8,128)} %shard_map.95), calls=%async_computation | async-start | bytes 3145728 | tf_op jit(solution)/shard_map/all_to_all | solution.py:473
  39.1 18.3 %collective-permute-start.3 = (f32[3,72,128]{2,1,0:T(8,128)}, f32[3,72,128]{2,1,0:T(8,128)S(1)}, u32[]{:S(2)}, u32[]{:S(2)}) collective-permute-start(f32[3,72,128]{2,1,0:T(8,128)} %get-tuple-element.13), channel_id=1, source_target_pairs={{32,0},{64,32},{96,64},{33,1},{65,33},{97,65},{34,2},{66,34},{98,6... | collective-permute-start | bytes 331784 | tf_op jit(solution)/shard_map/ppermute | solution.py:477
  42.0 13.8 %copy-start.9 = (f32[72,72]{1,0:T(8,128)S(1)}, f32[72,72]{1,0:T(8,128)}, u32[]{:S(2)}) copy-start(f32[72,72]{1,0:T(8,128)} %param.11) | copy-start | bytes 62212
  42.1 13.9 %copy-start.10 = (s32[20]{0:T(128)S(1)}, s32[20]{0:T(128)}, u32[]{:S(2)}) copy-start(s32[20]{0:T(128)} %param.15) | copy-start | bytes 244
  42.1 15.4 %collective-permute-start.2 = (f32[4,72,128]{2,1,0:T(8,128)}, f32[4,72,128]{2,1,0:T(8,128)S(1)}, u32[]{:S(2)}, u32[]{:S(2)}) collective-permute-start(f32[4,72,128]{2,1,0:T(8,128)} %get-tuple-element.12), channel_id=1, source_target_pairs={{0,32},{32,64},{64,96},{1,33},{33,65},{65,97},{2,34},{34,66},{66,9... | collective-permute-start | bytes 442376 | tf_op jit(solution)/shard_map/ppermute | solution.py:476
  49.2 8.2 %collective-permute-start.1 = (f32[3,72,128]{2,1,0:T(8,128)S(1)}, f32[3,72,128]{2,1,0:T(8,128)S(1)}, u32[]{:S(2)}, u32[]{:S(2)}) collective-permute-start(f32[3,72,128]{2,1,0:T(8,128)S(1)} %get-tuple-element.22), channel_id=1, source_target_pairs={{1,0},{2,1},{3,2},{4,3},{5,4},{6,5},{7,6},{8,7},{9,8},{10,9},{11,1... | collective-permute-start | bytes 331784 | tf_op jit(solution)/shard_map/ppermute | solution.py:481
  55.8 8.3 %collective-permute-start = (f32[4,72,128]{2,1,0:T(8,128)S(1)}, f32[4,72,128]{2,1,0:T(8,128)S(1)}, u32[]{:S(2)}, u32[]{:S(2)}) collective-permute-start(f32[4,72,128]{2,1,0:T(8,128)S(1)} %pad_maximum_fusion), channel_id=1, source_target_pairs={{0,1},{1,2},{2,3},{3,4},{4,5},{5,6},{6,7},{7,8},{8,9},{9,10},{10,1... | collective-permute-start | bytes 442376 | tf_op jit(solution)/shard_map/ppermute | solution.py:478
  57.4 6.6 %copy-start.7 = (f32[3,72,128]{2,1,0:T(8,128)}, f32[3,72,128]{2,1,0:T(8,128)S(1)}, u32[]{:S(2)}) copy-start(f32[3,72,128]{2,1,0:T(8,128)S(1)} %collective-permute-done.3.north) | copy-start | bytes 331780
  57.4 6.6 %copy-start.8 = (f32[3,72,128]{2,1,0:T(8,128)}, f32[3,72,128]{2,1,0:T(8,128)S(1)}, u32[]{:S(2)}) copy-start(f32[3,72,128]{2,1,0:T(8,128)S(1)} %collective-permute-done.1.east_col) | copy-start | bytes 331780
  57.4 6.6 %copy-start.1 = (f32[4,72,128]{2,1,0:T(8,128)}, f32[4,72,128]{2,1,0:T(8,128)S(1)}, u32[]{:S(2)}) copy-start(f32[4,72,128]{2,1,0:T(8,128)S(1)} %collective-permute-done.2.south.clat_south) | copy-start | bytes 442372
  64.0 0.7 copy-start.2
  75.5 1.2 copy-start
  113.8 12.2 %collective-permute-start.4 = (f32[3,72,128]{2,1,0:T(8,128)}, f32[3,72,128]{2,1,0:T(8,128)S(1)}, u32[]{:S(2)}, u32[]{:S(2)}) collective-permute-start(f32[3,72,128]{2,1,0:T(8,128)} %get-tuple-element.15), channel_id=1, source_target_pairs={{0,1},{1,2},{2,3},{3,4},{4,5},{5,6},{6,7},{7,8},{8,9},{9,10},{10,1... | collective-permute-start | bytes 331784 | tf_op jit(solution)/shard_map/ppermute | solution.py:490
  113.9 12.1 %collective-permute-start.5 = (f32[3,72,128]{2,1,0:T(8,128)}, f32[3,72,128]{2,1,0:T(8,128)S(1)}, u32[]{:S(2)}, u32[]{:S(2)}) collective-permute-start(f32[3,72,128]{2,1,0:T(8,128)} %get-tuple-element.16), channel_id=1, source_target_pairs={{1,0},{2,1},{3,2},{4,3},{5,4},{6,5},{7,6},{8,7},{9,8},{10,9},{11,1... | collective-permute-start | bytes 331784 | tf_op jit(solution)/shard_map/ppermute | solution.py:491
  119.5 6.5 %collective-permute-start.6 = (f32[3,72,128]{2,1,0:T(8,128)}, f32[3,72,128]{2,1,0:T(8,128)S(1)}, u32[]{:S(2)}, u32[]{:S(2)}) collective-permute-start(f32[3,72,128]{2,1,0:T(8,128)} %get-tuple-element.17), channel_id=1, source_target_pairs={{0,32},{32,64},{64,96},{1,33},{33,65},{65,97},{2,34},{34,66},{66,9... | collective-permute-start | bytes 331784 | tf_op jit(solution)/shard_map/ppermute | solution.py:488
  124.0 7.8 %collective-permute-start.7 = (f32[3,72,128]{2,1,0:T(8,128)}, f32[3,72,128]{2,1,0:T(8,128)S(1)}, u32[]{:S(2)}, u32[]{:S(2)}) collective-permute-start(f32[3,72,128]{2,1,0:T(8,128)} %get-tuple-element.18), channel_id=1, source_target_pairs={{32,0},{64,32},{96,64},{33,1},{65,33},{97,65},{34,2},{66,34},{98,6... | collective-permute-start | bytes 331784 | tf_op jit(solution)/shard_map/ppermute | solution.py:489
  126.0 5.8 %copy-start.3 = (f32[3,72,128]{2,1,0:T(8,128)}, f32[3,72,128]{2,1,0:T(8,128)S(1)}, u32[]{:S(2)}) copy-start(f32[3,72,128]{2,1,0:T(8,128)S(1)} %collective-permute-done.4.west_col) | copy-start | bytes 331780
  126.0 5.8 %copy-start.4 = (f32[3,72,128]{2,1,0:T(8,128)}, f32[3,72,128]{2,1,0:T(8,128)S(1)}, u32[]{:S(2)}) copy-start(f32[3,72,128]{2,1,0:T(8,128)S(1)} %collective-permute-done.5.east_col) | copy-start | bytes 331780
  126.1 5.7 %copy-start.5 = (f32[3,72,128]{2,1,0:T(8,128)}, f32[3,72,128]{2,1,0:T(8,128)S(1)}, u32[]{:S(2)}) copy-start(f32[3,72,128]{2,1,0:T(8,128)S(1)} %collective-permute-done.6.south) | copy-start | bytes 331780
  131.8 0.6 copy-start.6

commit v3 on v2

--- a/solution.py
+++ b/solution.py
@@ -12,8 +12,9 @@
 WIDE = 256
 f32 = jnp.float32
 bf16 = jnp.bfloat16
-BLOCK = 9
-VMEM_LIMIT = 56 * 2**20
+BLOCK = 15
+VMEM_LIMIT = 52 * 2**20
+ADD_LIMIT = 46 * 2**20
 
 
 def call(kernel, out_shape, *args, scratch=(), smem=(), flops=0, nbytes=0):
@@ -156,49 +157,57 @@
     )
 
 
-def lane_put(kept, lane, x, value, by):
-    return jnp.where(lane == x, pltpu.roll(value, by, 1), kept)
-
-
-def edges_kernel(field, clat, up, down):
+def edge_lanes(columns, kept, first, by):
+    lane = lax.broadcasted_iota(jnp.int32, kept.shape, 1)
+    own = kept
+    for i, v in enumerate(columns):
+        own = jnp.where(lane == i, pltpu.roll(v, i + by, 1), own)
+    inside = jnp.logical_and(lane >= first, lane < first + len(columns))
+    return jnp.where(inside, pltpu.roll(own, first, 1), kept)
+
+
+def edges_kernel(field, clat, clon_last, up, down, west, east):
     species, block, levels, rows = field.shape
-    lane = lax.broadcasted_iota(jnp.int32, (levels, rows), 1)
-    first = pl.program_id(0) * block
-
-    @pl.when(first == 0)
+    here = pl.program_id(0)
+    first = here * block
+
+    @pl.when(here == 0)
     def _():
         up[...] = jnp.zeros_like(up)
         down[...] = jnp.zeros_like(down)
+        for s in range(species):
+            east[s] = field[s, 0]
+
+    @pl.when(here == pl.num_programs(0) - 1)
+    def _():
+        for s in range(species):
+            west[s] = field[s, block - 1]
+        west[species] = clon_last[0]
 
     for s in range(species + 1):
-        u = up[s]
-        for i in range(block):
-            x = first + i
-            u = lane_put(u, lane, x, field[s, i] if s < species else clat[i], x + 1)
-        up[s] = u
+        columns = [field[s, i] if s < species else clat[i] for i in range(block)]
+        up[s] = edge_lanes(columns, up[s], first, 1)
         if s < species:
-            d = down[s]
-            for i in range(block):
-                x = first + i
-                d = lane_put(d, lane, x, field[s, i], x)
-            down[s] = d
-
-
-def edges(field, clat):
+            down[s] = edge_lanes(columns, down[s], first, 0)
+
+
+def edges(field, clat, clon):
     species, cols, levels, rows = field.shape
-    up, down = (species + 1, levels, rows), (species, levels, rows)
+    four, three = (species + 1, levels, rows), (species, levels, rows)
+    shapes = (four, three, four, three)
     return pl.pallas_call(
         edges_kernel,
-        out_shape=(jax.ShapeDtypeStruct(up, f32), jax.ShapeDtypeStruct(down, f32)),
+        out_shape=tuple(jax.ShapeDtypeStruct(shape, f32) for shape in shapes),
         grid=(cols // BLOCK,),
         in_specs=[
             pl.BlockSpec((species, BLOCK, levels, rows), lambda i: (0, i, 0, 0)),
             pl.BlockSpec((BLOCK, levels, rows), lambda i: (i, 0, 0)),
+            pl.BlockSpec((1, levels, rows), lambda i: (cols - 1, 0, 0)),
         ],
-        out_specs=(pl.BlockSpec(up, lambda i: (0, 0, 0)), pl.BlockSpec(down, lambda i: (0, 0, 0))),
+        out_specs=tuple(pl.BlockSpec(shape, lambda i: (0, 0, 0)) for shape in shapes),
         compiler_params=pltpu.CompilerParams(vmem_limit_bytes=VMEM_LIMIT),
         cost_estimate=pl.CostEstimate(flops=field.size * 4, bytes_accessed=field.size * 5, transcendentals=0),
-    )(field, clat)
+    )(field, clat, clon)
 
 
 def mix_weights(vertical_mix):
@@ -235,7 +244,16 @@
     w = weights[...]
     here = pl.program_id(0)
     at_start, at_end = here == 0, here == pl.num_programs(0) - 1
+    start = here * block
+    south_on = lax.rem(rows - start, rows)
+    north_on = rows - 1 - start
+    souths = [pltpu.roll(south[s], south_on, 1) for s in range(species)]
+    norths = [pltpu.roll(north[s], north_on, 1) for s in range(species)]
+    courant_south = pltpu.roll(clat_south[0], south_on, 1)
     waiting = []
+
+    def back(v, i):
+        return pltpu.roll(v, rows - i, 1) if i else v
 
     def mix(ready):
         mixed = jnp.dot(
@@ -252,21 +270,20 @@
                 flux[s, pl.ds(x, 1), :] = level0[s, pl.ds(x, 1), :] + m[0:1]
 
     for i in range(block):
-        x = here * block + i
         cl, cw = clon[i], clat[i]
         cl_west = clon[i - 1] if i else jnp.where(at_start, clon_col[0], clon_before[0])
         e = jnp.maximum(cl, 0.0) + kappa_mix
         w_ = kappa_mix - jnp.minimum(cl_west, 0.0)
         n = (jnp.maximum(cw, 0.0) + kappa_mix) * inside
-        cs = jnp.where(first, pltpu.roll(clat_south[0], lax.rem(rows - x, rows), 1), pltpu.roll(cw, 1, 1))
+        cs = jnp.where(first, back(courant_south, i), pltpu.roll(cw, 1, 1))
         s_ = (kappa_mix - jnp.minimum(cs, 0.0)) * below
         centre = 1.0 - (e + w_ + n + s_)
         for s in range(species):
             v = field[s, i]
             v_w = field[s, i - 1] if i else jnp.where(at_start, west_col[s], field_west[s, 0])
             v_e = field[s, i + 1] if i < block - 1 else jnp.where(at_end, east_col[s], field_east[s, 0])
-            v_n = jnp.where(last, pltpu.roll(north[s], rows - 1 - x, 1), pltpu.roll(v, rows - 1, 1))
-            v_s = jnp.where(first, pltpu.roll(south[s], lax.rem(rows - x, rows), 1), pltpu.roll(v, 1, 1))
+            v_n = jnp.where(last, back(norths[s], i), pltpu.roll(v, rows - 1, 1))
+            v_s = jnp.where(first, back(souths[s], i), pltpu.roll(v, 1, 1))
             h = centre * v + e * v_e + w_ * v_w + n * v_n + s_ * v_s
             high, low = split(h)
             waiting.append((s, i, jnp.concatenate([high, low, high], axis=0).astype(bf16)))
@@ -338,11 +355,36 @@
 
 
 def add_kernel(
-    got, plain, table, first, up, down, west, east, level0, parts, group, spot, total, held_field, sem_in, sem_out
+    got_at,
+    plain,
+    table,
+    first,
+    up,
+    down,
+    west,
+    east,
+    level0,
+    got,
+    parts,
+    group,
+    spot,
+    total,
+    held_field,
+    sem_in,
+    sem_got,
+    sem_out,
 ):
-    sources, held, slots = got.shape
+    sources, held, slots = got_at.shape
     species, cols, levels, rows = plain.shape
     akl = table.shape[1] // 4
+    quarters = sem_got.shape[0]
+    quarter = sources // quarters
+    came = [
+        pltpu.make_async_copy(got_at.at[pl.ds(q * quarter, quarter)], got.at[pl.ds(q * quarter, quarter)], sem_got.at[q])
+        for q in range(quarters)
+    ]
+    for copy in came:
+        copy.start()
     fetch = pltpu.make_async_copy(plain, held_field, sem_in)
     fetch.start()
     iota_w = lax.broadcasted_iota(jnp.int32, (WIDE, WIDE), 0)
@@ -361,10 +403,11 @@
             parts[:, at] = jnp.concatenate([both, both], axis=0).astype(bf16)
         return carry
 
-    lax.fori_loop(0, sources // 4, prepare, 0)
+    for q, copy in enumerate(came):
+        copy.wait()
+        lax.fori_loop(q * quarter // 4, (q + 1) * quarter // 4, prepare, 0)
     onehot_product(parts, group, spot, total, -(-species * cols // 4), 2, *ADD)
 
-    lane = lax.broadcasted_iota(jnp.int32, (levels, rows), 1)
     up[...] = jnp.zeros_like(up)
     down[...] = jnp.zeros_like(down)
     t = table[...]
@@ -378,7 +421,7 @@
     for s in range(species):
 
         def columns(b, carry):
-            u, d = up[s], down[s]
+            done = []
             for i in range(BLOCK):
                 x = b * BLOCK + i
                 sx = s * cols + x
@@ -393,10 +436,9 @@
                 v = held_field[s, x] + forcing
                 held_field[s, x] = v
                 level0[s, pl.ds(x, 1), :] = v[0:1]
-                u = lane_put(u, lane, x, v, x + 1)
-                d = lane_put(d, lane, x, v, x)
-            up[s] = u
-            down[s] = d
+                done.append(v)
+            up[s] = edge_lanes(done, up[s], b * BLOCK, 1)
+            down[s] = edge_lanes(done, down[s], b * BLOCK, 0)
             leave(s, b).start()
             return carry
 
@@ -426,18 +468,20 @@
             edge,
             jax.ShapeDtypeStruct((species, cols, rows), f32),
         ),
-        in_specs=[vmem, hbm, vmem],
+        in_specs=[hbm, hbm, vmem],
         out_specs=(hbm, vmem, vmem, vmem, vmem, vmem),
         scratch_shapes=(
+            pltpu.VMEM(got.shape, f32),
             pltpu.VMEM((4 * akl, length), bf16),
             pltpu.VMEM((4 * akl, length), bf16),
             pltpu.VMEM((WIDE, length), bf16),
             pltpu.VMEM((pairs * 4 * akl, WIDE), f32),
             pltpu.VMEM(plain.shape, f32),
             pltpu.SemaphoreType.DMA,
+            pltpu.SemaphoreType.DMA((4,)),
             pltpu.SemaphoreType.DMA((species, cols // BLOCK)),
         ),
-        compiler_params=pltpu.CompilerParams(vmem_limit_bytes=VMEM_LIMIT),
+        compiler_params=pltpu.CompilerParams(vmem_limit_bytes=ADD_LIMIT),
         cost_estimate=pl.CostEstimate(
             flops=2 * pairs * 4 * akl * WIDE * length,
             bytes_accessed=4 * (got.size + 2 * plain.size),
@@ -469,16 +513,15 @@
     clat = courant_lat.transpose(1, 0, 2)
     lat = lax.axis_index("lat").reshape(1)
 
+    up, down, west, east = edges(field, clat, clon)
+    south = lax.ppermute(up, "lat", north_way)
+    north = lax.ppermute(down, "lat", south_way)
+    west = lax.ppermute(west, "lon", east_way)
+    east = lax.ppermute(east, "lon", west_way)
     sent = pack(sounding_dest, sounding_values, sounding_target, n_tiles, species, cols, rows)
+    sent, south, north, west, east = lax.optimization_barrier((sent, south, north, west, east))
+    clat_south, clon_west = south, west
     got = lax.all_to_all(sent, ("lat", "lon"), split_axis=0, concat_axis=0, tiled=True)
-
-    up, down = edges(field, clat)
-    clat_south = south = lax.ppermute(up, "lat", north_way)
-    north = lax.ppermute(down, "lat", south_way)
-    clon_west = west = lax.ppermute(
-        jnp.concatenate([field[:, cols - 1], clon[None, cols - 1]], axis=0), "lon", east_way
-    )
-    east = lax.ppermute(field[:, 0], "lon", west_way)
 
     weights = mix_weights(vertical_mix)
     table = (jnp.arange(levels, dtype=jnp.int32)[:, None] == level_index[None, :]).astype(bf16)

time: 144 us -> 139 us (0.965)
  waiting for transfers between devices: 12.4 us -> 18.7 us
  local copies, waits for them, and re-layouts: 6.11 us -> 2.31 us
  Pallas kernels: 85.7 us -> 82.2 us
  starting transfers between devices: 36.8 us -> 34.3 us
    all_to_all x1, waiting for transfers between devices: 0.01 us -> 13.1 us  [on_device(): lax.all_to_all(sent, ('lat', 'lon'), split_axis=0, concat_axis=0, tiled=T...]
    ppermute x3 -> x0, starting transfers between devices: 10.2 us -> none  [the longest x1 5.76 us: on_device(): east = lax.ppermute(field[:, 0], 'lon', west_way)]
    ppermute x3 -> x0, waiting for transfers between devices: 6.61 us -> none  [the longest x1 6.6 us: on_device(): lax.ppermute(jnp.concatenate([field[:, cols - 1], clon[None, cols - 1]],...]
    ppermute x1 -> x2, starting transfers between devices: 5.67 us -> 11.3 us  [on_device(): east = lax.ppermute(east, 'lon', west_way)]
    ppermute x1 -> x2, starting transfers between devices: 4.49 us -> 9.96 us  [on_device(): south = lax.ppermute(up, 'lat', north_way)]
    all_to_all x1, starting transfers between devices: 11.5 us -> 6.92 us  [on_device(): lax.all_to_all(sent, ('lat', 'lon'), split_axis=0, concat_axis=0, tiled=T...]
    unnamed x24 -> x13, local copies, waits for them, and re-layouts: 5.32 us -> 2.31 us
  transfers between devices with their start and end apart: 9 -> 9, of which waited for: 3 -> 2; matrix products, arithmetic and copies ran while one was open for 4% -> 0% of each run, Pallas kernels for 12% -> 21%
where the time goes in v3:
time: 139 us
  Pallas kernels  82.2 us (59%)
  starting transfers between devices  34.3 us (25%)
  waiting for transfers between devices  18.7 us (13%)
  local copies, waits for them, and re-layouts  2.31 us (2%)
    pallas_call x1, Pallas kernels, add_soundings(): pl.pallas_call(add_kernel, out_shape=(jax.ShapeDtypeStruct(plain.shape, f...  35.6 us
    pallas_call x2, Pallas kernels, step(): pl.pallas_call(functools.partial(step_kernel, lat_size=lat_size), out_sha...  21.1 us
    pallas_call x1, Pallas kernels, call(): pl.pallas_call(kernel, out_shape=out_shape, in_specs=specs, out_specs=jax...  19.2 us
    all_to_all x1, waiting for transfers between devices, on_device(): lax.all_to_all(sent, ('lat', 'lon'), split_axis=0, concat_axis=0, tiled=T...  13.1 us
    ppermute x2, starting transfers between devices, on_device(): east = lax.ppermute(east, 'lon', west_way)  11.3 us
    ppermute x2, starting transfers between devices, on_device(): south = lax.ppermute(up, 'lat', north_way)  9.96 us
    all_to_all x1, starting transfers between devices, on_device(): lax.all_to_all(sent, ('lat', 'lon'), split_axis=0, concat_axis=0, tiled=T...  6.92 us
    pallas_call x1, Pallas kernels, edges(): pl.pallas_call(edges_kernel, out_shape=tuple((jax.ShapeDtypeStruct(shape,...  6.3 us
  transfers between devices with their start and end apart: 9, of which 2 were waited for; matrix products, arithmetic and copies ran while one was open for 0% of the time, Pallas kernels for 21%

profile of v3, /device:TPU:1, one launch (start us, length us, event | category | flops | bytes accessed | tf_op | source)
XLA Modules:
  0.0 138.6 jit_solution(5935597587332577925)
XLA Ops:
  0.6 0.0 copy-start.3
  0.6 0.0 copy-start.2
  0.7 0.0 copy-start.1
  0.7 6.3 %shard_map.96 = (f32[4,72,128]{2,1,0:T(8,128)S(1)}, f32[3,72,128]{2,1,0:T(8,128)S(1)}, f32[4,72,128]{2,1,0:T(8,128)S(1)}, f32[3,72,128]{2,1,0:T(8,128)S(1)}) custom-call(f32[3,45,72,128]{3,2,1,0:T(8,128)} %bitcast.12, f32[45,72,128]{2,1,0:T(8,128)} %bitcast.21, f32[45,72,128]{2,1,0:T(8,128)} %bitcast.16), custom_call_target="tpu_custom_call" | custom-call | flops 4976640 | bytes 6220800 | tf_op jit(solution)/shard_map/pallas_call | solution.py:198
  7.0 3.3 %collective-permute-start.1 = (f32[3,72,128]{2,1,0:T(8,128)S(1)}, f32[3,72,128]{2,1,0:T(8,128)S(1)}, u32[]{:S(2)}, u32[]{:S(2)}) collective-permute-start(f32[3,72,128]{2,1,0:T(8,128)S(1)} %get-tuple-element.20), channel_id=1, source_target_pairs={{32,0},{64,32},{96,64},{33,1},{65,33},{97,65},{34,2},{66,34},{98,6... | collective-permute-start | bytes 331784 | tf_op jit(solution)/shard_map/ppermute | solution.py:518
  10.3 6.4 %collective-permute-start.3 = (f32[3,72,128]{2,1,0:T(8,128)S(1)}, f32[3,72,128]{2,1,0:T(8,128)S(1)}, u32[]{:S(2)}, u32[]{:S(2)}) collective-permute-start(f32[3,72,128]{2,1,0:T(8,128)S(1)} %get-tuple-element.22), channel_id=1, source_target_pairs={{1,0},{2,1},{3,2},{4,3},{5,4},{6,5},{7,6},{8,7},{9,8},{10,9},{11,1... | collective-permute-start | bytes 331784 | tf_op jit(solution)/shard_map/ppermute | solution.py:520
  16.7 5.4 %collective-permute-start = (f32[4,72,128]{2,1,0:T(8,128)S(1)}, f32[4,72,128]{2,1,0:T(8,128)S(1)}, u32[]{:S(2)}, u32[]{:S(2)}) collective-permute-start(f32[4,72,128]{2,1,0:T(8,128)S(1)} %get-tuple-element.19), channel_id=1, source_target_pairs={{0,32},{32,64},{64,96},{1,33},{33,65},{65,97},{2,34},{34,66},{66,9... | collective-permute-start | bytes 442376 | tf_op jit(solution)/shard_map/ppermute | solution.py:517
  22.1 0.1 collective-permute-start.2
  22.2 0.0 copy-done.3
  22.2 0.0 copy-done.2
  22.2 0.0 copy-done.1
  22.2 0.0 copy-start.4
  22.2 0.0 copy-start.5
  22.3 19.2 %shard_map.95 = f32[128,24,128]{2,1,0:T(8,128)} custom-call(s32[1,8192]{1,0:T(1,128)S(1)} %bitcast.10, f32[20,8192]{1,0:T(8,128)S(1)} %copy-done.1, s32[1,8192]{1,0:T(1,128)S(1)} %bitcast.11), custom_call_target="tpu_custom_call" | custom-call | flops 12884901888 | bytes 2293760 | tf_op jit(solution)/shard_map/pallas_call | solution.py:24
  41.5 0.0 collective-permute-done.1.north
  41.5 0.0 collective-permute-done.3.east_col
  41.5 0.0 collective-permute-done.south.clat_south
  41.5 0.0 collective-permute-done.2.west_col.clon_col
  41.5 6.9 %all-to-all-start = ((f32[128,24,128]{2,1,0:T(8,128)}), f32[128,24,128]{2,1,0:T(8,128)S(1)}, u32[]{:S(2)}, u32[]{:S(2)}) async-start(f32[128,24,128]{2,1,0:T(8,128)} %shard_map.95), calls=%async_computation | async-start | bytes 3145728 | tf_op jit(solution)/shard_map/all_to_all | solution.py:524
  48.4 0.0 copy-done.4
  48.4 0.1 copy.10
  48.5 0.0 copy-done.5
  48.5 0.1 add_convert_fusion.table
  48.7 0.1 pad_maximum_fusion.weights
  48.8 10.6 %shard_map.97.plain = f32[3,45,72,128]{3,2,1,0:T(8,128)} custom-call(s32[1]{0:T(128)} %bitcast.lat_ref, f32[3,45,72,128]{3,2,1,0:T(8,128)} %bitcast.13, f32[3,45,72,128]{3,2,1,0:T(8,128)} %bitcast.14, f32[3,45,72,128]{3,2,1,0:T(8,128)} %bitcast.15, f32[45,72,128]{2,1,0:T(8,128)} %bitcast.17, f32[45,72,128]{2,1,0:T(8,128)} %bitcast.18, ...), custom_call_target="tpu_custom_call" | custom-call | flops 537477120 | bytes 14929920 | tf_op jit(solution)/shard_map/pallas_call | solution.py:312
  59.4 13.1 %all-to-all-done.got_at = f32[128,24,128]{2,1,0:T(8,128)S(1)} async-done(((f32[128,24,128]{2,1,0:T(8,128)}), f32[128,24,128]{2,1,0:T(8,128)S(1)}, u32[]{:S(2)}, u32[]{:S(2)}) %all-to-all-start) | async-done | bytes 1572896 | tf_op jit(solution)/shard_map/all_to_all | solution.py:524
  72.4 35.6 %shard_map.98 = (f32[3,45,72,128]{3,2,1,0:T(8,128)S(1)}, f32[3,72,128]{2,1,0:T(8,128)S(1)}, f32[3,72,128]{2,1,0:T(8,128)S(1)}, f32[3,72,128]{2,1,0:T(8,128)S(1)}...) custom-call(f32[128,24,128]{2,1,0:T(8,128)S(1)} %all-to-all-done.got_at, f32[3,45,72,128]{3,2,1,0:T(8,128)} %shard_map.97.plain, ...), custom_call_target="tpu_custom_call" | custom-call | flops 22817013760 | bytes 11526144 | tf_op jit(solution)/shard_map/pallas_call | solution.py:461
  108.0 0.0 copy-start
  108.0 2.2 %copy-done = f32[3,45,72,128]{3,2,1,0:T(8,128)} copy-done((f32[3,45,72,128]{3,2,1,0:T(8,128)}, f32[3,45,72,128]{3,2,1,0:T(8,128)S(1)}, u32[]{:S(2)}) %copy-start) | copy-done | bytes 4976664
  110.2 0.8 collective-permute-start.4
  111.0 4.9 %collective-permute-start.5 = (f32[3,72,128]{2,1,0:T(8,128)S(1)}, f32[3,72,128]{2,1,0:T(8,128)S(1)}, u32[]{:S(2)}, u32[]{:S(2)}) collective-permute-start(f32[3,72,128]{2,1,0:T(8,128)S(1)} %get-tuple-element.30), channel_id=1, source_target_pairs={{1,0},{2,1},{3,2},{4,3},{5,4},{6,5},{7,6},{8,7},{9,8},{10,9},{11,1... | collective-permute-start | bytes 331784 | tf_op jit(solution)/shard_map/ppermute | solution.py:534
  115.9 4.6 %collective-permute-start.6 = (f32[3,72,128]{2,1,0:T(8,128)S(1)}, f32[3,72,128]{2,1,0:T(8,128)S(1)}, u32[]{:S(2)}, u32[]{:S(2)}) collective-permute-start(f32[3,72,128]{2,1,0:T(8,128)S(1)} %get-tuple-element.31), channel_id=1, source_target_pairs={{0,32},{32,64},{64,96},{1,33},{33,65},{65,97},{2,34},{34,66},{66,9... | collective-permute-start | bytes 331784 | tf_op jit(solution)/shard_map/ppermute | solution.py:531
  120.5 1.9 %collective-permute-start.7 = (f32[3,72,128]{2,1,0:T(8,128)S(1)}, f32[3,72,128]{2,1,0:T(8,128)S(1)}, u32[]{:S(2)}, u32[]{:S(2)}) collective-permute-start(f32[3,72,128]{2,1,0:T(8,128)S(1)} %get-tuple-element.32), channel_id=1, source_target_pairs={{32,0},{64,32},{96,64},{33,1},{65,33},{97,65},{34,2},{66,34},{98,6... | collective-permute-start | bytes 331784 | tf_op jit(solution)/shard_map/ppermute | solution.py:532
  122.4 0.0 collective-permute-done.4.west_col
  122.4 0.0 collective-permute-done.5.east_col
  122.4 0.0 collective-permute-done.6.south
  122.5 5.6 %collective-permute-done.7.north = f32[3,72,128]{2,1,0:T(8,128)S(1)} collective-permute-done((f32[3,72,128]{2,1,0:T(8,128)S(1)}, f32[3,72,128]{2,1,0:T(8,128)S(1)}, u32[]{:S(2)}, u32[]{:S(2)}) %collective-permute-start.7) | collective-permute-done | bytes 110624 | tf_op jit(solution)/shard_map/ppermute | solution.py:532
  128.1 10.5 %shard_map.99 = (f32[3,45,72,128]{3,2,1,0:T(8,128)}, f32[3,45,128]{2,1,0:T(8,128)}) custom-call(s32[1]{0:T(128)} %bitcast.lat_ref, f32[3,45,72,128]{3,2,1,0:T(8,128)} %copy-done, f32[3,45,72,128]{3,2,1,0:T(8,128)} %copy-done, f32[3,45,72,128]{3,2,1,0:T(8,128)} %copy-done, f32[45,72,128]{2,1,0:T(8,128)} %bitcast.19, f32[45,72,128]{2,1,0:T(8,128)} %bitcast.20, ...), custom_call_target="tpu_custom_call" | custom-call | flops 537477120 | bytes 14929920 | tf_op jit(solution)/shard_map/pallas_call | solution.py:312
  (2 shorter events, 0.0 us)
Async XLA Ops:
  0.6 21.6 %copy-start.3 = (s32[8192]{0:T(1024)S(1)}, s32[8192]{0:T(1024)}, u32[]{:S(2)}) copy-start(s32[8192]{0:T(1024)} %param.14) | copy-start | bytes 98308
  0.6 21.6 %copy-start.2 = (s32[8192,1]{0,1:T(1,128)S(1)}, s32[8192,1]{0,1:T(1,128)}, u32[]{:S(2)}) copy-start(s32[8192,1]{0,1:T(1,128)} %param.13) | copy-start | bytes 98308
  0.7 21.6 %copy-start.1 = (f32[20,8192]{1,0:T(8,128)S(1)}, f32[20,8192]{1,0:T(8,128)}, u32[]{:S(2)}) copy-start(f32[20,8192]{1,0:T(8,128)} %values.1) | copy-start | bytes 1966084
  7.0 34.5 %collective-permute-start.1 = (f32[3,72,128]{2,1,0:T(8,128)S(1)}, f32[3,72,128]{2,1,0:T(8,128)S(1)}, u32[]{:S(2)}, u32[]{:S(2)}) collective-permute-start(f32[3,72,128]{2,1,0:T(8,128)S(1)} %get-tuple-element.20), channel_id=1, source_target_pairs={{32,0},{64,32},{96,64},{33,1},{65,33},{97,65},{34,2},{66,34},{98,6... | collective-permute-start | bytes 331784 | tf_op jit(solution)/shard_map/ppermute | solution.py:518
  10.3 31.2 %collective-permute-start.3 = (f32[3,72,128]{2,1,0:T(8,128)S(1)}, f32[3,72,128]{2,1,0:T(8,128)S(1)}, u32[]{:S(2)}, u32[]{:S(2)}) collective-permute-start(f32[3,72,128]{2,1,0:T(8,128)S(1)} %get-tuple-element.22), channel_id=1, source_target_pairs={{1,0},{2,1},{3,2},{4,3},{5,4},{6,5},{7,6},{8,7},{9,8},{10,9},{11,1... | collective-permute-start | bytes 331784 | tf_op jit(solution)/shard_map/ppermute | solution.py:520
  16.7 24.7 %collective-permute-start = (f32[4,72,128]{2,1,0:T(8,128)S(1)}, f32[4,72,128]{2,1,0:T(8,128)S(1)}, u32[]{:S(2)}, u32[]{:S(2)}) collective-permute-start(f32[4,72,128]{2,1,0:T(8,128)S(1)} %get-tuple-element.19), channel_id=1, source_target_pairs={{0,32},{32,64},{64,96},{1,33},{33,65},{65,97},{2,34},{34,66},{66,9... | collective-permute-start | bytes 442376 | tf_op jit(solution)/shard_map/ppermute | solution.py:517
  22.1 19.4 %collective-permute-start.2 = (f32[4,72,128]{2,1,0:T(8,128)S(1)}, f32[4,72,128]{2,1,0:T(8,128)S(1)}, u32[]{:S(2)}, u32[]{:S(2)}) collective-permute-start(f32[4,72,128]{2,1,0:T(8,128)S(1)} %get-tuple-element.21), channel_id=1, source_target_pairs={{0,1},{1,2},{2,3},{3,4},{4,5},{5,6},{6,7},{7,8},{8,9},{9,10},{10,1... | collective-permute-start | bytes 442376 | tf_op jit(solution)/shard_map/ppermute | solution.py:519
  22.2 26.2 %copy-start.4 = (f32[72,72]{1,0:T(8,128)S(1)}, f32[72,72]{1,0:T(8,128)}, u32[]{:S(2)}) copy-start(f32[72,72]{1,0:T(8,128)} %param.11) | copy-start | bytes 62212
  22.2 26.3 %copy-start.5 = (s32[20]{0:T(128)S(1)}, s32[20]{0:T(128)}, u32[]{:S(2)}) copy-start(s32[20]{0:T(128)} %param.15) | copy-start | bytes 244
  41.5 30.9 %all-to-all-start = ((f32[128,24,128]{2,1,0:T(8,128)}), f32[128,24,128]{2,1,0:T(8,128)S(1)}, u32[]{:S(2)}, u32[]{:S(2)}) async-start(f32[128,24,128]{2,1,0:T(8,128)} %shard_map.95), calls=%async_computation | async-start | bytes 3145728 | tf_op jit(solution)/shard_map/all_to_all | solution.py:524
  108.0 2.2 %copy-start = (f32[3,45,72,128]{3,2,1,0:T(8,128)}, f32[3,45,72,128]{3,2,1,0:T(8,128)S(1)}, u32[]{:S(2)}) copy-start(f32[3,45,72,128]{3,2,1,0:T(8,128)S(1)} %get-tuple-element.28.field.field_west.field_east) | copy-start | bytes 14929924
  110.2 12.2 %collective-permute-start.4 = (f32[3,72,128]{2,1,0:T(8,128)S(1)}, f32[3,72,128]{2,1,0:T(8,128)S(1)}, u32[]{:S(2)}, u32[]{:S(2)}) collective-permute-start(f32[3,72,128]{2,1,0:T(8,128)S(1)} %get-tuple-element.29), channel_id=1, source_target_pairs={{0,1},{1,2},{2,3},{3,4},{4,5},{5,6},{6,7},{7,8},{8,9},{9,10},{10,1... | collective-permute-start | bytes 331784 | tf_op jit(solution)/shard_map/ppermute | solution.py:533
  111.0 11.4 %collective-permute-start.5 = (f32[3,72,128]{2,1,0:T(8,128)S(1)}, f32[3,72,128]{2,1,0:T(8,128)S(1)}, u32[]{:S(2)}, u32[]{:S(2)}) collective-permute-start(f32[3,72,128]{2,1,0:T(8,128)S(1)} %get-tuple-element.30), channel_id=1, source_target_pairs={{1,0},{2,1},{3,2},{4,3},{5,4},{6,5},{7,6},{8,7},{9,8},{10,9},{11,1... | collective-permute-start | bytes 331784 | tf_op jit(solution)/shard_map/ppermute | solution.py:534
  115.9 6.5 %collective-permute-start.6 = (f32[3,72,128]{2,1,0:T(8,128)S(1)}, f32[3,72,128]{2,1,0:T(8,128)S(1)}, u32[]{:S(2)}, u32[]{:S(2)}) collective-permute-start(f32[3,72,128]{2,1,0:T(8,128)S(1)} %get-tuple-element.31), channel_id=1, source_target_pairs={{0,32},{32,64},{64,96},{1,33},{33,65},{65,97},{2,34},{34,66},{66,9... | collective-permute-start | bytes 331784 | tf_op jit(solution)/shard_map/ppermute | solution.py:531
  120.5 7.6 %collective-permute-start.7 = (f32[3,72,128]{2,1,0:T(8,128)S(1)}, f32[3,72,128]{2,1,0:T(8,128)S(1)}, u32[]{:S(2)}, u32[]{:S(2)}) collective-permute-start(f32[3,72,128]{2,1,0:T(8,128)S(1)} %get-tuple-element.32), channel_id=1, source_target_pairs={{32,0},{64,32},{96,64},{33,1},{65,33},{97,65},{34,2},{66,34},{98,6... | collective-permute-start | bytes 331784 | tf_op jit(solution)/shard_map/ppermute | solution.py:532

commit v4 on v3

--- a/solution.py
+++ b/solution.py
@@ -14,7 +14,7 @@
 bf16 = jnp.bfloat16
 BLOCK = 15
 VMEM_LIMIT = 52 * 2**20
-ADD_LIMIT = 46 * 2**20
+ADD_LIMIT = 49 * 2**20
 
 
 def call(kernel, out_shape, *args, scratch=(), smem=(), flops=0, nbytes=0):
@@ -296,7 +296,7 @@
 
 def step(lat, field, clon, clat, halo, weights, lat_size, level0=None):
     species, cols, levels, rows = field.shape
-    shapes = [jax.ShapeDtypeStruct(field.shape, f32)]
+    shapes = [pltpu.HBM(field.shape, f32)]
     columns = pl.BlockSpec((species, BLOCK, levels, rows), lambda i: (0, i, 0, 0))
     courant = pl.BlockSpec((BLOCK, levels, rows), lambda i: (i, 0, 0))
     out_specs = [columns]
@@ -461,14 +461,14 @@
     return pl.pallas_call(
         add_kernel,
         out_shape=(
-            jax.ShapeDtypeStruct(plain.shape, f32),
+            pltpu.HBM(plain.shape, f32),
             edge,
             edge,
             edge,
             edge,
             jax.ShapeDtypeStruct((species, cols, rows), f32),
         ),
-        in_specs=[hbm, hbm, vmem],
+        in_specs=[hbm, pl.BlockSpec(memory_space=pltpu.HBM), vmem],
         out_specs=(hbm, vmem, vmem, vmem, vmem, vmem),
         scratch_shapes=(
             pltpu.VMEM(got.shape, f32),
@@ -505,7 +505,7 @@
     species, levels, cols, rows = adjoint_in.shape
     east_way = [(i, (i + 1) % lon_size) for i in range(lon_size)]
     west_way = [(j, i) for i, j in east_way]
-    north_way = [(i, i + 1) for i in range(lat_size - 1)]
+    north_way = [(i, (i + 1) % lat_size) for i in range(lat_size)]
     south_way = [(j, i) for i, j in north_way]
 
     field = adjoint_in.transpose(0, 2, 1, 3)

time: 139 us -> 131 us (0.942)
  starting transfers between devices: 34.3 us -> 28.7 us
  local copies, waits for them, and re-layouts: 2.31 us -> 0.1 us
    ppermute x2, starting transfers between devices: 5.25 us -> 1.49 us  [on_device(): north = lax.ppermute(down, 'lat', south_way)]
    ppermute x2, starting transfers between devices: 9.96 us -> 6.24 us  [on_device(): south = lax.ppermute(up, 'lat', north_way)]
    unnamed x13 -> x11, local copies, waits for them, and re-layouts: 2.31 us -> 0.1 us
    all_to_all x1, starting transfers between devices: 6.92 us -> 8.81 us  [on_device(): lax.all_to_all(sent, ('lat', 'lon'), split_axis=0, concat_axis=0, tiled=T...]
    ppermute x2, waiting for transfers between devices: 0.01 us -> 1.75 us  [on_device(): south = lax.ppermute(up, 'lat', north_way)]
    ppermute x2, waiting for transfers between devices: 5.61 us -> 3.92 us  [on_device(): north = lax.ppermute(down, 'lat', south_way)]
  transfers between devices with their start and end apart: 9 -> 9, of which waited for: 2 -> 3; matrix products, arithmetic and copies ran while one was open for 0% -> 0% of each run, Pallas kernels for 21% -> 23%
where the time goes in v4:
time: 131 us
  Pallas kernels  82.1 us (63%)
  starting transfers between devices  28.7 us (22%)
  waiting for transfers between devices  18.7 us (14%)
    pallas_call x1, Pallas kernels, add_soundings(): pl.pallas_call(add_kernel, out_shape=(pltpu.HBM(plain.shape, f32), edge,...  35.6 us
    pallas_call x2, Pallas kernels, step(): pl.pallas_call(functools.partial(step_kernel, lat_size=lat_size), out_sha...  21.1 us
    pallas_call x1, Pallas kernels, call(): pl.pallas_call(kernel, out_shape=out_shape, in_specs=specs, out_specs=jax...  19.2 us
    all_to_all x1, waiting for transfers between devices, on_device(): lax.all_to_all(sent, ('lat', 'lon'), split_axis=0, concat_axis=0, tiled=T...  13.1 us
    ppermute x2, starting transfers between devices, on_device(): east = lax.ppermute(east, 'lon', west_way)  11.3 us
    all_to_all x1, starting transfers between devices, on_device(): lax.all_to_all(sent, ('lat', 'lon'), split_axis=0, concat_axis=0, tiled=T...  8.81 us
    pallas_call x1, Pallas kernels, edges(): pl.pallas_call(edges_kernel, out_shape=tuple((jax.ShapeDtypeStruct(shape,...  6.3 us
    ppermute x2, starting transfers between devices, on_device(): south = lax.ppermute(up, 'lat', north_way)  6.24 us
  transfers between devices with their start and end apart: 9, of which 3 were waited for; matrix products, arithmetic and copies ran while one was open for 0% of the time, Pallas kernels for 23%

profile of v4, /device:TPU:1, one launch (start us, length us, event | category | flops | bytes accessed | tf_op | source)
XLA Modules:
  0.0 130.6 jit_solution(7308115249802288900)
XLA Ops:
  0.6 0.0 copy-start.2
  0.6 0.0 copy-start.1
  0.7 0.0 copy-start
  0.7 6.3 %shard_map.96 = (f32[4,72,128]{2,1,0:T(8,128)S(1)}, f32[3,72,128]{2,1,0:T(8,128)S(1)}, f32[4,72,128]{2,1,0:T(8,128)S(1)}, f32[3,72,128]{2,1,0:T(8,128)S(1)}) custom-call(f32[3,45,72,128]{3,2,1,0:T(8,128)} %bitcast.12, f32[45,72,128]{2,1,0:T(8,128)} %bitcast.21, f32[45,72,128]{2,1,0:T(8,128)} %bitcast.16), custom_call_target="tpu_custom_call" | custom-call | flops 4976640 | bytes 6220800 | tf_op jit(solution)/shard_map/pallas_call | solution.py:198
  7.0 1.5 %collective-permute-start.1 = (f32[3,72,128]{2,1,0:T(8,128)S(1)}, f32[3,72,128]{2,1,0:T(8,128)S(1)}, u32[]{:S(2)}, u32[]{:S(2)}) collective-permute-start(f32[3,72,128]{2,1,0:T(8,128)S(1)} %get-tuple-element.20), channel_id=1, source_target_pairs={{32,0},{64,32},{96,64},{0,96},{33,1},{65,33},{97,65},{1,97},{34,2}... | collective-permute-start | bytes 331784 | tf_op jit(solution)/shard_map/ppermute | solution.py:518
  8.5 6.4 %collective-permute-start.3 = (f32[3,72,128]{2,1,0:T(8,128)S(1)}, f32[3,72,128]{2,1,0:T(8,128)S(1)}, u32[]{:S(2)}, u32[]{:S(2)}) collective-permute-start(f32[3,72,128]{2,1,0:T(8,128)S(1)} %get-tuple-element.22), channel_id=1, source_target_pairs={{1,0},{2,1},{3,2},{4,3},{5,4},{6,5},{7,6},{8,7},{9,8},{10,9},{11,1... | collective-permute-start | bytes 331784 | tf_op jit(solution)/shard_map/ppermute | solution.py:520
  14.8 3.5 %collective-permute-start = (f32[4,72,128]{2,1,0:T(8,128)S(1)}, f32[4,72,128]{2,1,0:T(8,128)S(1)}, u32[]{:S(2)}, u32[]{:S(2)}) collective-permute-start(f32[4,72,128]{2,1,0:T(8,128)S(1)} %get-tuple-element.19), channel_id=1, source_target_pairs={{0,32},{32,64},{64,96},{96,0},{1,33},{33,65},{65,97},{97,1},{2,34}... | collective-permute-start | bytes 442376 | tf_op jit(solution)/shard_map/ppermute | solution.py:517
  18.4 0.0 collective-permute-start.2
  18.4 0.0 copy-done.2
  18.4 0.0 copy-done.1
  18.4 0.0 copy-done
  18.4 0.0 copy-start.3
  18.4 0.0 copy-start.4
  18.4 19.2 %shard_map.95 = f32[128,24,128]{2,1,0:T(8,128)} custom-call(s32[1,8192]{1,0:T(1,128)S(1)} %bitcast.10, f32[20,8192]{1,0:T(8,128)S(1)} %copy-done, s32[1,8192]{1,0:T(1,128)S(1)} %bitcast.11), custom_call_target="tpu_custom_call" | custom-call | flops 12884901888 | bytes 2293760 | tf_op jit(solution)/shard_map/pallas_call | solution.py:24
  37.6 0.0 collective-permute-done.1.north
  37.6 0.0 collective-permute-done.3.east_col
  37.6 0.0 collective-permute-done.south.clat_south
  37.6 0.0 collective-permute-done.2.west_col.clon_col
  37.6 8.8 %all-to-all-start = ((f32[128,24,128]{2,1,0:T(8,128)}), f32[128,24,128]{2,1,0:T(8,128)S(1)}, u32[]{:S(2)}, u32[]{:S(2)}) async-start(f32[128,24,128]{2,1,0:T(8,128)} %shard_map.95), calls=%async_computation | async-start | bytes 3145728 | tf_op jit(solution)/shard_map/all_to_all | solution.py:524
  46.5 0.0 copy-done.3
  46.5 0.1 copy.10
  46.6 0.0 copy-done.4
  46.6 0.1 add_convert_fusion.table
  46.7 0.1 pad_maximum_fusion.weights
  46.8 10.6 %shard_map.97.plain = f32[3,45,72,128]{3,2,1,0:T(8,128)} custom-call(s32[1]{0:T(128)} %bitcast.lat_ref, f32[3,45,72,128]{3,2,1,0:T(8,128)} %bitcast.13, f32[3,45,72,128]{3,2,1,0:T(8,128)} %bitcast.14, f32[3,45,72,128]{3,2,1,0:T(8,128)} %bitcast.15, f32[45,72,128]{2,1,0:T(8,128)} %bitcast.17, f32[45,72,128]{2,1,0:T(8,128)} %bitcast.18, ...), custom_call_target="tpu_custom_call" | custom-call | flops 537477120 | bytes 14929920 | tf_op jit(solution)/shard_map/pallas_call | solution.py:312
  57.4 13.1 %all-to-all-done.got_at = f32[128,24,128]{2,1,0:T(8,128)S(1)} async-done(((f32[128,24,128]{2,1,0:T(8,128)}), f32[128,24,128]{2,1,0:T(8,128)S(1)}, u32[]{:S(2)}, u32[]{:S(2)}) %all-to-all-start) | async-done | bytes 1572896 | tf_op jit(solution)/shard_map/all_to_all | solution.py:524
  70.4 35.6 %shard_map.98 = (f32[3,45,72,128]{3,2,1,0:T(8,128)}, f32[3,72,128]{2,1,0:T(8,128)S(1)}, f32[3,72,128]{2,1,0:T(8,128)S(1)}, f32[3,72,128]{2,1,0:T(8,128)S(1)}, f3...) custom-call(f32[128,24,128]{2,1,0:T(8,128)S(1)} %all-to-all-done.got_at, f32[3,45,72,128]{3,2,1,0:T(8,128)} %shard_map.97.plain, ...), custom_call_target="tpu_custom_call" | custom-call | flops 22817013760 | bytes 11526144 | tf_op jit(solution)/shard_map/pallas_call | solution.py:461
  106.0 0.8 collective-permute-start.4
  106.9 4.9 %collective-permute-start.5 = (f32[3,72,128]{2,1,0:T(8,128)S(1)}, f32[3,72,128]{2,1,0:T(8,128)S(1)}, u32[]{:S(2)}, u32[]{:S(2)}) collective-permute-start(f32[3,72,128]{2,1,0:T(8,128)S(1)} %get-tuple-element.30), channel_id=1, source_target_pairs={{1,0},{2,1},{3,2},{4,3},{5,4},{6,5},{7,6},{8,7},{9,8},{10,9},{11,1... | collective-permute-start | bytes 331784 | tf_op jit(solution)/shard_map/ppermute | solution.py:534
  111.8 2.7 %collective-permute-start.6 = (f32[3,72,128]{2,1,0:T(8,128)S(1)}, f32[3,72,128]{2,1,0:T(8,128)S(1)}, u32[]{:S(2)}, u32[]{:S(2)}) collective-permute-start(f32[3,72,128]{2,1,0:T(8,128)S(1)} %get-tuple-element.31), channel_id=1, source_target_pairs={{0,32},{32,64},{64,96},{96,0},{1,33},{33,65},{65,97},{97,1},{2,34}... | collective-permute-start | bytes 331784 | tf_op jit(solution)/shard_map/ppermute | solution.py:531
  114.5 0.0 collective-permute-start.7
  114.5 0.0 collective-permute-done.4.west_col
  114.5 0.0 collective-permute-done.5.east_col
  114.5 1.7 %collective-permute-done.6.south = f32[3,72,128]{2,1,0:T(8,128)S(1)} collective-permute-done((f32[3,72,128]{2,1,0:T(8,128)S(1)}, f32[3,72,128]{2,1,0:T(8,128)S(1)}, u32[]{:S(2)}, u32[]{:S(2)}) %collective-permute-start.6) | collective-permute-done | bytes 110624 | tf_op jit(solution)/shard_map/ppermute | solution.py:531
  116.2 3.9 %collective-permute-done.7.north = f32[3,72,128]{2,1,0:T(8,128)S(1)} collective-permute-done((f32[3,72,128]{2,1,0:T(8,128)S(1)}, f32[3,72,128]{2,1,0:T(8,128)S(1)}, u32[]{:S(2)}, u32[]{:S(2)}) %collective-permute-start.7) | collective-permute-done | bytes 110624 | tf_op jit(solution)/shard_map/ppermute | solution.py:532
  120.1 10.5 %shard_map.99 = (f32[3,45,72,128]{3,2,1,0:T(8,128)}, f32[3,45,128]{2,1,0:T(8,128)}) custom-call(s32[1]{0:T(128)} %bitcast.lat_ref, f32[3,45,72,128]{3,2,1,0:T(8,128)} %get-tuple-element.28.field.field_west.field_east, f32[3,45,72,128]{3,2,1,0:T(8,128)} %get-tuple-element.28.field.field_west.field_east, ...), custom_call_target="tpu_custom_call" | custom-call | flops 537477120 | bytes 14929920 | tf_op jit(solution)/shard_map/pallas_call | solution.py:312
  (2 shorter events, 0.0 us)
Async XLA Ops:
  0.6 17.7 %copy-start.2 = (s32[8192]{0:T(1024)S(1)}, s32[8192]{0:T(1024)}, u32[]{:S(2)}) copy-start(s32[8192]{0:T(1024)} %param.14) | copy-start | bytes 98308
  0.6 17.7 %copy-start.1 = (s32[8192,1]{0,1:T(1,128)S(1)}, s32[8192,1]{0,1:T(1,128)}, u32[]{:S(2)}) copy-start(s32[8192,1]{0,1:T(1,128)} %param.13) | copy-start | bytes 98308
  0.7 17.7 %copy-start = (f32[20,8192]{1,0:T(8,128)S(1)}, f32[20,8192]{1,0:T(8,128)}, u32[]{:S(2)}) copy-start(f32[20,8192]{1,0:T(8,128)} %values.1) | copy-start | bytes 1966084
  7.0 30.7 %collective-permute-start.1 = (f32[3,72,128]{2,1,0:T(8,128)S(1)}, f32[3,72,128]{2,1,0:T(8,128)S(1)}, u32[]{:S(2)}, u32[]{:S(2)}) collective-permute-start(f32[3,72,128]{2,1,0:T(8,128)S(1)} %get-tuple-element.20), channel_id=1, source_target_pairs={{32,0},{64,32},{96,64},{0,96},{33,1},{65,33},{97,65},{1,97},{34,2}... | collective-permute-start | bytes 331784 | tf_op jit(solution)/shard_map/ppermute | solution.py:518
  8.5 29.2 %collective-permute-start.3 = (f32[3,72,128]{2,1,0:T(8,128)S(1)}, f32[3,72,128]{2,1,0:T(8,128)S(1)}, u32[]{:S(2)}, u32[]{:S(2)}) collective-permute-start(f32[3,72,128]{2,1,0:T(8,128)S(1)} %get-tuple-element.22), channel_id=1, source_target_pairs={{1,0},{2,1},{3,2},{4,3},{5,4},{6,5},{7,6},{8,7},{9,8},{10,9},{11,1... | collective-permute-start | bytes 331784 | tf_op jit(solution)/shard_map/ppermute | solution.py:520
  14.8 22.8 %collective-permute-start = (f32[4,72,128]{2,1,0:T(8,128)S(1)}, f32[4,72,128]{2,1,0:T(8,128)S(1)}, u32[]{:S(2)}, u32[]{:S(2)}) collective-permute-start(f32[4,72,128]{2,1,0:T(8,128)S(1)} %get-tuple-element.19), channel_id=1, source_target_pairs={{0,32},{32,64},{64,96},{96,0},{1,33},{33,65},{65,97},{97,1},{2,34}... | collective-permute-start | bytes 442376 | tf_op jit(solution)/shard_map/ppermute | solution.py:517
  18.4 19.3 %collective-permute-start.2 = (f32[4,72,128]{2,1,0:T(8,128)S(1)}, f32[4,72,128]{2,1,0:T(8,128)S(1)}, u32[]{:S(2)}, u32[]{:S(2)}) collective-permute-start(f32[4,72,128]{2,1,0:T(8,128)S(1)} %get-tuple-element.21), channel_id=1, source_target_pairs={{0,1},{1,2},{2,3},{3,4},{4,5},{5,6},{6,7},{7,8},{8,9},{9,10},{10,1... | collective-permute-start | bytes 442376 | tf_op jit(solution)/shard_map/ppermute | solution.py:519
  18.4 28.1 %copy-start.3 = (f32[72,72]{1,0:T(8,128)S(1)}, f32[72,72]{1,0:T(8,128)}, u32[]{:S(2)}) copy-start(f32[72,72]{1,0:T(8,128)} %param.11) | copy-start | bytes 62212
  18.4 28.1 %copy-start.4 = (s32[20]{0:T(128)S(1)}, s32[20]{0:T(128)}, u32[]{:S(2)}) copy-start(s32[20]{0:T(128)} %param.15) | copy-start | bytes 244
  37.6 32.8 %all-to-all-start = ((f32[128,24,128]{2,1,0:T(8,128)}), f32[128,24,128]{2,1,0:T(8,128)S(1)}, u32[]{:S(2)}, u32[]{:S(2)}) async-start(f32[128,24,128]{2,1,0:T(8,128)} %shard_map.95), calls=%async_computation | async-start | bytes 3145728 | tf_op jit(solution)/shard_map/all_to_all | solution.py:524
  106.0 8.4 %collective-permute-start.4 = (f32[3,72,128]{2,1,0:T(8,128)S(1)}, f32[3,72,128]{2,1,0:T(8,128)S(1)}, u32[]{:S(2)}, u32[]{:S(2)}) collective-permute-start(f32[3,72,128]{2,1,0:T(8,128)S(1)} %get-tuple-element.29), channel_id=1, source_target_pairs={{0,1},{1,2},{2,3},{3,4},{4,5},{5,6},{6,7},{7,8},{8,9},{9,10},{10,1... | collective-permute-start | bytes 331784 | tf_op jit(solution)/shard_map/ppermute | solution.py:533
  106.9 7.6 %collective-permute-start.5 = (f32[3,72,128]{2,1,0:T(8,128)S(1)}, f32[3,72,128]{2,1,0:T(8,128)S(1)}, u32[]{:S(2)}, u32[]{:S(2)}) collective-permute-start(f32[3,72,128]{2,1,0:T(8,128)S(1)} %get-tuple-element.30), channel_id=1, source_target_pairs={{1,0},{2,1},{3,2},{4,3},{5,4},{6,5},{7,6},{8,7},{9,8},{10,9},{11,1... | collective-permute-start | bytes 331784 | tf_op jit(solution)/shard_map/ppermute | solution.py:534
  111.8 4.4 %collective-permute-start.6 = (f32[3,72,128]{2,1,0:T(8,128)S(1)}, f32[3,72,128]{2,1,0:T(8,128)S(1)}, u32[]{:S(2)}, u32[]{:S(2)}) collective-permute-start(f32[3,72,128]{2,1,0:T(8,128)S(1)} %get-tuple-element.31), channel_id=1, source_target_pairs={{0,32},{32,64},{64,96},{96,0},{1,33},{33,65},{65,97},{97,1},{2,34}... | collective-permute-start | bytes 331784 | tf_op jit(solution)/shard_map/ppermute | solution.py:531
  114.5 5.7 %collective-permute-start.7 = (f32[3,72,128]{2,1,0:T(8,128)S(1)}, f32[3,72,128]{2,1,0:T(8,128)S(1)}, u32[]{:S(2)}, u32[]{:S(2)}) collective-permute-start(f32[3,72,128]{2,1,0:T(8,128)S(1)} %get-tuple-element.32), channel_id=1, source_target_pairs={{32,0},{64,32},{96,64},{0,96},{33,1},{65,33},{97,65},{1,97},{34,2}... | collective-permute-start | bytes 331784 | tf_op jit(solution)/shard_map/ppermute | solution.py:532

commit v5 on v4

v5 whole, which is shorter than its diff:
```python
import functools

import jax
import jax.numpy as jnp
from jax import lax
from jax.experimental import pallas as pl
from jax.experimental.pallas import tpu as pltpu
from jax.sharding import PartitionSpec as P

kappa_mix = 0.05
LANES = 128
WIDE = 256
f32 = jnp.float32
bf16 = jnp.bfloat16
BLOCK = 15
VMEM_LIMIT = 52 * 2**20
PACK_LIMIT = 58 * 2**20
ADD_LIMIT = 49 * 2**20


def split(value):
    high = value.astype(bf16).astype(f32)
    return high, value - high


def nt_dot(a, b):
    return lax.dot_general(a, b, (((1,), (1,)), ((), ())), preferred_element_type=f32)


def onehot_product(parts, group, spot, total, count, step, together, depth, beside=None):
    rows, length = parts.shape
    chunks = length // depth

    def chunk(g, c):
        at = pl.ds(pl.multiple_of(c * depth, depth), depth)
        held, key = parts[:, at], group[:, at]
        left = jnp.concatenate(
            [
                jnp.where(key == ((g * together + i) * step).astype(f32).astype(bf16), held, jnp.zeros_like(held))
                for i in range(together)
            ],
            axis=0,
        )
        return nt_dot(left, spot[:, at])

    def of_group(g, carry):
        to = pl.ds(pl.multiple_of(g * (together * rows), together * rows), together * rows)
        if beside is not None:
            beside(g)
        if chunks == 1:
            total[to, :] = chunk(g, 0)
            return carry

        def of_chunk(c, carry):
            product = chunk(g, c)

            @pl.when(c == 0)
            def _():
                total[to, :] = product

            @pl.when(c > 0)
            def _():
                total[to, :] += product

            return carry

        return lax.fori_loop(0, chunks, of_chunk, carry)

    lax.fori_loop(0, count // together, of_group, 0)


def edge_lanes(columns, kept, first, up, share=None):
    rows = kept.shape[1]
    lane = lax.broadcasted_iota(jnp.int32, kept.shape, 1)
    own = jnp.zeros_like(kept)
    for i, v in enumerate(columns):
        if up:
            own = jnp.where(lane == 2 * i, pltpu.roll(v, 2 * i + 1, 1), own)
        else:
            own = jnp.where(lane == 2 * i + 1, pltpu.roll(v, 2 * i + 1, 1), own)
    if share is not None:
        own = own * share
    turn = 2 * first if up else lax.rem(2 * first + rows - 2, rows)
    return kept + pltpu.roll(own, turn, 1)


PACK = (16, 8192)
ADD = (17, 4096)


def whole_part(value, divisor):
    return ((value.astype(f32) + 0.5) * (1.0 / divisor)).astype(jnp.int32)


def pack_kernel(
    dest,
    values,
    target,
    field_at,
    clon_at,
    clat_at,
    out,
    up,
    down,
    west,
    east,
    parts,
    group,
    spot,
    total,
    field,
    clat,
    sems,
):
    n_tiles, held, _ = out.shape
    species, cols, _, rows = field.shape
    copies = [(field_at, field), (clat_at, clat), (clon_at.at[cols - 1], west.at[species])]
    for s in range(species):
        copies += [(field_at.at[s, cols - 1], west.at[s]), (field_at.at[s, 0], east.at[s])]
    copies = [pltpu.make_async_copy(*pair, sems.at[i]) for i, pair in enumerate(copies)]
    for copy in copies:
        copy.start()
    up[...] = jnp.zeros_like(up)
    down[...] = jnp.zeros_like(down)
    levels, length = values.shape
    iota_t = lax.broadcasted_iota(jnp.int32, (n_tiles, WIDE), 0)
    square = (WIDE, WIDE)
    upper = (
        lax.broadcasted_iota(jnp.int32, square, 0) < lax.broadcasted_iota(jnp.int32, square, 1)
    ).astype(f32).astype(bf16)
    iota_w = lax.broadcasted_iota(jnp.int32, square, 0)

    def rank(at, base):
        d = dest[:, at]
        hot = iota_t == d
        hot_f = jnp.where(hot, 1.0, 0.0)
        earlier = jnp.dot(hot_f.astype(bf16), upper, preferred_element_type=f32) + base
        own = jnp.sum(jnp.where(hot, earlier, 0.0), axis=0, keepdims=True).astype(jnp.int32)
        low = own + (d & 1) * LANES
        spot[:, at] = jnp.where(iota_w == low, 1.0, 0.0).astype(bf16)
        group[:, at] = jnp.broadcast_to((d >> 1).astype(f32), (2 * held, WIDE)).astype(bf16)
        t = target[:, at]
        cell = whole_part(t, species)
        row_of = whole_part(cell, cols)
        segment = ((t - cell * species) * cols + cell - row_of * cols) * rows + row_of
        row = jnp.concatenate(
            [values[:, at], segment.astype(f32), jnp.zeros((held - levels - 1, WIDE), f32)], axis=0
        )
        parts[:, at] = jnp.concatenate(split(row), axis=0).astype(bf16)
        return base + jnp.sum(hot_f, axis=1, keepdims=True)

    def ranks(b, base):
        for i in range(4):
            base = rank(pl.ds(pl.multiple_of((4 * b + i) * WIDE, WIDE), WIDE), base)
        return base

    lax.fori_loop(0, length // (4 * WIDE), ranks, jnp.zeros((n_tiles, 1), f32))
    for copy in copies:
        copy.wait()
    blocks = cols // BLOCK

    def take_edges(g):
        first = jnp.minimum(g, blocks - 1) * BLOCK
        new = (g < blocks).astype(f32)
        for s in range(species + 1):
            columns = [field[s, first + i] if s < species else clat[first + i] for i in range(BLOCK)]
            up[s] = edge_lanes(columns, up[s], first, True, new)
            if s < species:
                down[s] = edge_lanes(columns, down[s], first, False, new)

    onehot_product(parts, group, spot, total, n_tiles // 2, 1, *PACK, beside=take_edges)

    def put(g, carry):
        for i in range(4):
            j = 4 * g + i
            at = pl.multiple_of(j * 2 * held, 2 * held)
            both = total[pl.ds(at, held), :] + total[pl.ds(at + held, held), :]
            out[2 * j] = both[:, :LANES]
            out[2 * j + 1] = both[:, LANES:]
        return carry

    lax.fori_loop(0, n_tiles // 8, put, 0)


def pack(dest, values, target, field, clon, clat, n_tiles):
    levels, length = values.shape
    species, cols, depth, rows = field.shape
    held = -(-(levels + 1) // 8) * 8
    four, three = (species + 1, depth, rows), (species, depth, rows)
    vmem, hbm = pl.BlockSpec(memory_space=pltpu.VMEM), pl.BlockSpec(memory_space=pl.ANY)
    return pl.pallas_call(
        pack_kernel,
        out_shape=tuple(
            jax.ShapeDtypeStruct(shape, f32) for shape in ((n_tiles, held, LANES), four, three, four, three)
        ),
        in_specs=[vmem, vmem, vmem, hbm, hbm, hbm],
        out_specs=(vmem,) * 5,
        scratch_shapes=(
            pltpu.VMEM((2 * held, length), bf16),
            pltpu.VMEM((2 * held, length), bf16),
            pltpu.VMEM((WIDE, length), bf16),
            pltpu.VMEM((n_tiles // 2 * 2 * held, WIDE), f32),
            pltpu.VMEM(field.shape, f32),
            pltpu.VMEM(clat.shape, f32),
            pltpu.SemaphoreType.DMA((3 + 2 * species,)),
        ),
        compiler_params=pltpu.CompilerParams(vmem_limit_bytes=PACK_LIMIT),
        cost_estimate=pl.CostEstimate(
            flops=2 * length * n_tiles * LANES * 2 * held,
            bytes_accessed=4 * (length * 22 + n_tiles * held * LANES + field.size),
            transcendentals=0,
        ),
    )(dest.reshape(1, length), values, target.reshape(1, length), field, clon, clat)


def mix_weights(vertical_mix):
    levels = vertical_mix.shape[0]
    matrix = (jnp.eye(levels, dtype=f32) + vertical_mix).T
    high = lax.reduce_precision(matrix, 8, 7)
    return jnp.concatenate([high, high, matrix - high], axis=1).astype(bf16)


def step_kernel(
    lat_ref,
    field,
    field_west,
    field_east,
    clon,
    clon_before,
    clat,
    west_col,
    east_col,
    clon_col,
    south,
    north,
    clat_south,
    weights,
    *refs,
    lat_size,
    second,
):
    species, block, levels, rows = field.shape
    lane = lax.broadcasted_iota(jnp.int32, (levels, rows), 1)
    first, last = lane == 0, lane == rows - 1
    lat = lat_ref[0]
    below = jnp.where(jnp.logical_and(first, lat == 0), 0.0, 1.0)
    inside = jnp.where(jnp.logical_and(last, lat == lat_size - 1), 0.0, 1.0)
    w = weights[...]
    here = pl.program_id(0)
    at_start, at_end = here == 0, here == pl.num_programs(0) - 1
    start = here * block
    turn = lax.rem(rows - 2 * start, rows)
    even = lane % 2 == 0

    def turned(a, b):
        return pltpu.roll(jnp.where(even, a, b), turn, 1)

    halos = [turned(south[s], north[s]) for s in range(species)]
    courant_south = pltpu.roll(clat_south[0], turn, 1)
    waiting = []

    def back(v, i):
        return pltpu.roll(v, rows - 2 * i, 1) if i else v

    if second:
        total, table, out, flux = refs
        t = table[...]
        akl = t.shape[1] // 4
        wanted = []
        made = {}

        def make(ready):
            forcing = jnp.dot(t, jnp.concatenate([p for _, _, p in ready], axis=1), preferred_element_type=f32)
            for k, (key, v, _) in enumerate(ready):
                made[key] = v + forcing[:, k * rows : (k + 1) * rows]

        def want(s, i, v, x):
            wanted.append(((s, i), v, spread(total, s * cols + x, rows, akl)))
            if len(wanted) == 2:
                make(wanted)
                wanted.clear()

        cols = pl.num_programs(0) * block
        for i in range(-1, block + 1):
            for s in range(species):
                if i < 0:
                    want(s, i, field_west[s, 0], jnp.maximum(start - 1, 0))
                elif i == block:
                    want(s, i, field_east[s, 0], jnp.minimum(start + block, cols - 1))
                else:
                    want(s, i, field[s, i], start + i)
        if wanted:
            make(wanted)

        def at_column(s, i):
            return made[s, i]
    else:
        out, up, down, west, east = refs
        finished = [[None] * block for _ in range(species)]

        def at_column(s, i):
            return field_west[s, 0] if i < 0 else field_east[s, 0] if i == block else field[s, i]

    def mix(ready):
        mixed = jnp.dot(
            w, jnp.concatenate([r for _, _, r in ready], axis=1), preferred_element_type=f32
        )
        for k, (s, i, _) in enumerate(ready):
            m = mixed[:, k * rows : (k + 1) * rows]
            out[s, i] = m
            if second:
                flux[s, pl.ds(start + i, 1), :] = at_column(s, i)[0:1] + m[0:1]
            else:
                finished[s][i] = m

    for i in range(block):
        cl, cw = clon[i], clat[i]
        cl_west = clon[i - 1] if i else jnp.where(at_start, clon_col[0], clon_before[0])
        e = jnp.maximum(cl, 0.0) + kappa_mix
        w_ = kappa_mix - jnp.minimum(cl_west, 0.0)
        n = (jnp.maximum(cw, 0.0) + kappa_mix) * inside
        cs = jnp.where(first, back(courant_south, i), pltpu.roll(cw, 1, 1))
        s_ = (kappa_mix - jnp.minimum(cs, 0.0)) * below
        centre = 1.0 - (e + w_ + n + s_)
        for s in range(species):
            v, v_w, v_e = at_column(s, i), at_column(s, i - 1), at_column(s, i + 1)
            if i == 0:
                v_w = jnp.where(at_start, west_col[s], v_w)
            if i == block - 1:
                v_e = jnp.where(at_end, east_col[s], v_e)
            halo = back(halos[s], i)
            v_n = jnp.where(last, halo, pltpu.roll(v, rows - 1, 1))
            v_s = jnp.where(first, halo, pltpu.roll(v, 1, 1))
            h = centre * v + e * v_e + w_ * v_w + n * v_n + s_ * v_s
            high, low = split(h)
            waiting.append((s, i, jnp.concatenate([high, low, high], axis=0).astype(bf16)))
            if len(waiting) == 2:
                mix(waiting)
                waiting.clear()
    if waiting:
        mix(waiting)
    if not second:

        @pl.when(at_start)
        def _():
            up[...] = jnp.zeros_like(up)
            down[...] = jnp.zeros_like(down)
            for s in range(species):
                east[s] = out[s, 0]

        @pl.when(at_end)
        def _():
            for s in range(species):
                west[s] = out[s, block - 1]

        for s in range(species):
            up[s] = edge_lanes(finished[s], up[s], start, True)
            down[s] = edge_lanes(finished[s], down[s], start, False)


def spread(total, sx, rows, akl):
    pair = total[
        pl.ds(pl.multiple_of((sx >> 1) * 2 * akl, 8), 2 * akl),
        pl.ds(pl.multiple_of((sx & 1) * rows, rows), rows),
    ]
    return jnp.concatenate(split(pair), axis=0).astype(bf16)


def step(lat, field, clon, clat, halo, weights, lat_size, total=None, table=None):
    species, cols, levels, rows = field.shape
    columns = pl.BlockSpec((species, BLOCK, levels, rows), lambda i: (0, i, 0, 0))
    courant = pl.BlockSpec((BLOCK, levels, rows), lambda i: (i, 0, 0))
    whole = lambda shape: pl.BlockSpec(shape, lambda i: (0,) * len(shape))
    part = lambda at: pl.BlockSpec((1, levels, rows), lambda i: (at, 0, 0))
    west, east, clon_west, south, north, clat_south = halo
    three = whole((species, levels, rows))
    second = total is not None
    more = (total, table) if second else ()
    shapes = [(species, cols, rows)] if second else [(species, levels, rows)] * 4
    return pl.pallas_call(
        functools.partial(step_kernel, lat_size=lat_size, second=second),
        out_shape=[pltpu.HBM(field.shape, f32)] + [jax.ShapeDtypeStruct(shape, f32) for shape in shapes],
        grid=(cols // BLOCK,),
        in_specs=[
            pl.BlockSpec(memory_space=pltpu.SMEM),
            columns,
            pl.BlockSpec((species, 1, levels, rows), lambda i: (0, jnp.maximum(i * BLOCK - 1, 0), 0, 0)),
            pl.BlockSpec((species, 1, levels, rows), lambda i: (0, jnp.minimum(i * BLOCK + BLOCK, cols - 1), 0, 0)),
            courant,
            pl.BlockSpec((1, levels, rows), lambda i: (jnp.maximum(i * BLOCK - 1, 0), 0, 0)),
            courant,
            three,
            three,
            part(species),
            three,
            three,
            part(species),
            whole(weights.shape),
            *[whole(m.shape) for m in more],
        ],
        out_specs=[columns] + [whole(shape) for shape in shapes],
        compiler_params=pltpu.CompilerParams(vmem_limit_bytes=VMEM_LIMIT),
        cost_estimate=pl.CostEstimate(
            flops=field.size * levels * 6, bytes_accessed=field.size * 12, transcendentals=0
        ),
    )(
        lat,
        field,
        field,
        field,
        clon,
        clon,
        clat,
        west,
        east,
        clon_west,
        south,
        north,
        clat_south,
        weights,
        *more,
    )


def add_kernel(
    got_at,
    plain_up,
    plain_down,
    plain_west,
    plain_east,
    table,
    total,
    up,
    down,
    west,
    east,
    got,
    parts,
    group,
    spot,
    sem_got,
    *,
    cols,
):
    sources, held, slots = got_at.shape
    species, levels, rows = plain_up.shape
    akl = table.shape[1] // 4
    quarters = sem_got.shape[0]
    quarter = sources // quarters
    came = [
        pltpu.make_async_copy(got_at.at[pl.ds(q * quarter, quarter)], got.at[pl.ds(q * quarter, quarter)], sem_got.at[q])
        for q in range(quarters)
    ]
    for copy in came:
        copy.start()
    iota_w = lax.broadcasted_iota(jnp.int32, (WIDE, WIDE), 0)
    second = (lax.broadcasted_iota(jnp.int32, (4 * akl, WIDE), 0) >= 2 * akl).astype(f32)

    def prepare(g, carry):
        for i in range(2):
            b = 2 * g + i
            row = jnp.concatenate([got[2 * b], got[2 * b + 1]], axis=1)
            at = pl.ds(pl.multiple_of(b * WIDE, WIDE), WIDE)
            segment = row[akl : akl + 1].astype(jnp.int32)
            spot[:, at] = jnp.where(iota_w == (segment & (WIDE - 1)), 1.0, 0.0).astype(bf16)
            group[:, at] = ((segment >> 8).astype(f32) - second).astype(bf16)
            high, low = split(row[:akl])
            both = jnp.concatenate([high, low], axis=0)
            parts[:, at] = jnp.concatenate([both, both], axis=0).astype(bf16)
        return carry

    for q, copy in enumerate(came):
        copy.wait()
        lax.fori_loop(q * quarter // 4, (q + 1) * quarter // 4, prepare, 0)
    onehot_product(parts, group, spot, total, total.shape[0] // (4 * akl), 2, *ADD)

    t = table[...]

    def forced(parts_of, before):
        return before + jnp.dot(t, parts_of, preferred_element_type=f32)

    for s in range(species):
        east[s] = forced(spread(total, s * cols, rows, akl), plain_east[s])
        west[s] = forced(spread(total, s * cols + cols - 1, rows, akl), plain_west[s])

        def of_block(b, carry):
            columns = []
            for i in range(BLOCK):
                sx = s * cols + b * BLOCK + i
                columns.append(
                    total[
                        pl.ds(pl.multiple_of((sx >> 1) * 2 * akl, 8), 2 * akl),
                        pl.ds(pl.multiple_of((sx & 1) * rows, rows), rows),
                    ]
                )
            return tuple(edge_lanes(columns, kept, b * BLOCK, k == 0) for k, kept in enumerate(carry))

        none = jnp.zeros((2 * akl, rows), f32)
        ends = lax.fori_loop(0, cols // BLOCK, of_block, (none, none))
        for end, before, after in zip(ends, (plain_up, plain_down), (up, down)):
            after[s] = forced(jnp.concatenate(split(end), axis=0).astype(bf16), before[s])


def add_soundings(got, edges, table, cols):
    sources, held, slots = got.shape
    species, levels, rows = edges[0].shape
    akl = table.shape[1] // 4
    length = sources * slots
    pairs = -(-species * cols // 4)
    edge = jax.ShapeDtypeStruct((species, levels, rows), f32)
    vmem, hbm = pl.BlockSpec(memory_space=pltpu.VMEM), pl.BlockSpec(memory_space=pl.ANY)
    return pl.pallas_call(
        functools.partial(add_kernel, cols=cols),
        out_shape=(jax.ShapeDtypeStruct((pairs * 4 * akl, WIDE), f32), edge, edge, edge, edge),
        in_specs=[hbm] + [vmem] * 5,
        out_specs=(vmem,) * 5,
        scratch_shapes=(
            pltpu.VMEM(got.shape, f32),
            pltpu.VMEM((4 * akl, length), bf16),
            pltpu.VMEM((4 * akl, length), bf16),
            pltpu.VMEM((WIDE, length), bf16),
            pltpu.SemaphoreType.DMA((4,)),
        ),
        compiler_params=pltpu.CompilerParams(vmem_limit_bytes=ADD_LIMIT),
        cost_estimate=pl.CostEstimate(
            flops=2 * pairs * 4 * akl * WIDE * length,
            bytes_accessed=4 * got.size,
            transcendentals=0,
        ),
    )(got, *edges, table)


def on_device(
    adjoint_in,
    courant_lon,
    courant_lat,
    vertical_mix,
    sounding_values,
    sounding_dest,
    sounding_target,
    level_index,
):
    lat_size, lon_size = lax.axis_size("lat"), lax.axis_size("lon")
    n_tiles = lat_size * lon_size
    species, levels, cols, rows = adjoint_in.shape
    east_way = [(i, (i + 1) % lon_size) for i in range(lon_size)]
    west_way = [(j, i) for i, j in east_way]
    north_way = [(i, (i + 1) % lat_size) for i in range(lat_size)]
    south_way = [(j, i) for i, j in north_way]

    field = adjoint_in.transpose(0, 2, 1, 3)
    clon = courant_lon.transpose(1, 0, 2)
    clat = courant_lat.transpose(1, 0, 2)
    lat = lax.axis_index("lat").reshape(1)

    sent, up, down, west, east = pack(sounding_dest, sounding_values, sounding_target, field, clon, clat, n_tiles)
    south = lax.ppermute(up, "lat", north_way)
    north = lax.ppermute(down, "lat", south_way)
    west = lax.ppermute(west, "lon", east_way)
    east = lax.ppermute(east, "lon", west_way)
    sent, south, north, west, east = lax.optimization_barrier((sent, south, north, west, east))
    clat_south, clon_west = south, west
    got = lax.all_to_all(sent, ("lat", "lon"), split_axis=0, concat_axis=0, tiled=True)

    weights = mix_weights(vertical_mix)
    table = (jnp.arange(levels, dtype=jnp.int32)[:, None] == level_index[None, :]).astype(bf16)
    table = jnp.concatenate([table] * 4, axis=1)
    plain, *own_edges = step(lat, field, clon, clat, (west, east, clon_west, south, north, clat_south), weights, lat_size)
    total, up, down, west, east = add_soundings(got, own_edges, table, cols)
    south = lax.ppermute(up, "lat", north_way)
    north = lax.ppermute(down, "lat", south_way)
    west = lax.ppermute(west, "lon", east_way)
    east = lax.ppermute(east, "lon", west_way)
    halo = (west, east, clon_west, south, north, clat_south)
    out, flux = step(lat, plain, clon, clat, halo, weights, lat_size, total, table)
    return out.transpose(0, 2, 1, 3), flux


def solution(mesh):
    return jax.shard_map(
        on_device,
        mesh=mesh,
        in_specs=(
            P(None, None, "lon", "lat"),
            P(None, "lon", "lat"),
            P(None, "lon", "lat"),
            P(),
            P(None, ("lat", "lon")),
            P(("lat", "lon"), None),
            P(("lat", "lon")),
            P(),
        ),
        out_specs=(P(None, None, "lon", "lat"), P(None, "lon", "lat")),
        check_vma=False,
    )
```

time: 131 us -> 127 us (0.969)
  Pallas kernels: 82.1 us -> 76 us
  waiting for transfers between devices: 18.7 us -> 22.2 us
    pallas_call x5 -> x4, Pallas kernels: 82.1 us -> 76 us  [the longest x1 32.7 us: add_soundings(): pl.pallas_call(functools.partial(add_kernel, cols=cols), out_shape=(jax.S...]
    ppermute x2, waiting for transfers between devices: 3.92 us -> 8.59 us  [on_device(): north = lax.ppermute(down, 'lat', south_way)]
    ppermute x2, starting transfers between devices: 11.3 us -> 9.29 us  [on_device(): east = lax.ppermute(east, 'lon', west_way)]
    ppermute x2, starting transfers between devices: 6.24 us -> 7.74 us  [on_device(): south = lax.ppermute(up, 'lat', north_way)]
    ppermute x2, starting transfers between devices: 1.49 us -> 0.01 us  [on_device(): north = lax.ppermute(down, 'lat', south_way)]
  transfers between devices with their start and end apart: 9 -> 9, of which waited for: 3 -> 4; matrix products, arithmetic and copies ran while one was open for 0% -> 0% of each run, Pallas kernels for 23% -> 9%
where the time goes in v5:
time: 127 us
  Pallas kernels  76 us (60%)
  starting transfers between devices  27.6 us (22%)
  waiting for transfers between devices  22.2 us (17%)
    pallas_call x1, Pallas kernels, add_soundings(): pl.pallas_call(functools.partial(add_kernel, cols=cols), out_shape=(jax.S...  32.7 us
    pallas_call x2, Pallas kernels, step(): pl.pallas_call(functools.partial(step_kernel, lat_size=lat_size, second=s...  22.2 us
    pallas_call x1, Pallas kernels, pack(): pl.pallas_call(pack_kernel, out_shape=tuple((jax.ShapeDtypeStruct(shape,...  21.1 us
    all_to_all x1, waiting for transfers between devices, on_device(): lax.all_to_all(sent, ('lat', 'lon'), split_axis=0, concat_axis=0, tiled=T...  11.9 us
    ppermute x2, starting transfers between devices, on_device(): east = lax.ppermute(east, 'lon', west_way)  9.29 us
    ppermute x2, waiting for transfers between devices, on_device(): north = lax.ppermute(down, 'lat', south_way)  8.59 us
    all_to_all x1, starting transfers between devices, on_device(): lax.all_to_all(sent, ('lat', 'lon'), split_axis=0, concat_axis=0, tiled=T...  8.44 us
    ppermute x2, starting transfers between devices, on_device(): south = lax.ppermute(up, 'lat', north_way)  7.74 us
  transfers between devices with their start and end apart: 9, of which 4 were waited for; matrix products, arithmetic and copies ran while one was open for 0% of the time, Pallas kernels for 9%

profile of v5, /device:TPU:1, one launch (start us, length us, event | category | flops | bytes accessed | tf_op | source)
XLA Modules:
  0.0 126.9 jit_solution(7508299621147648664)
XLA Ops:
  0.6 21.1 %shard_map.95 = (f32[128,24,128]{2,1,0:T(8,128)}, f32[4,72,128]{2,1,0:T(8,128)}, f32[3,72,128]{2,1,0:T(8,128)}, f32[4,72,128]{2,1,0:T(8,128)}, f32[3,72,128]{2,1,0:T(8,128)}) custom-call(s32[1,8192]{1,0:T(1,128)} %bitcast.23, f32[20,8192]{1,0:T(8,128)} %values.1, s32[1,8192]{1,0:T(1,128)} %bitcast.24, f32[3,45,72,128]{3,2,1,0:T(8,128)} %bitcast.10, ...), custom_call_target="tpu_custom_call" | custom-call | flops 12884901888 | bytes 7270400 | tf_op jit(solution)/shard_map/pallas_call | solution.py:191
  21.7 0.0 copy-start
  21.7 0.0 copy-start.1
  21.7 5.0 %collective-permute-start = (f32[4,72,128]{2,1,0:T(8,128)}, f32[4,72,128]{2,1,0:T(8,128)S(1)}, u32[]{:S(2)}, u32[]{:S(2)}) collective-permute-start(f32[4,72,128]{2,1,0:T(8,128)} %get-tuple-element.25), channel_id=1, source_target_pairs={{0,32},{32,64},{64,96},{96,0},{1,33},{33,65},{65,97},{97,1},{2,34}... | collective-permute-start | bytes 442376 | tf_op jit(solution)/shard_map/ppermute | solution.py:557
  26.8 1.3 %collective-permute-start.2 = (f32[4,72,128]{2,1,0:T(8,128)}, f32[4,72,128]{2,1,0:T(8,128)S(1)}, u32[]{:S(2)}, u32[]{:S(2)}) collective-permute-start(f32[4,72,128]{2,1,0:T(8,128)} %get-tuple-element.27), channel_id=1, source_target_pairs={{0,1},{1,2},{2,3},{3,4},{4,5},{5,6},{6,7},{7,8},{8,9},{9,10},{10,1... | collective-permute-start | bytes 442376 | tf_op jit(solution)/shard_map/ppermute | solution.py:559
  28.1 0.0 collective-permute-start.1
  28.1 4.4 %collective-permute-start.3 = (f32[3,72,128]{2,1,0:T(8,128)}, f32[3,72,128]{2,1,0:T(8,128)S(1)}, u32[]{:S(2)}, u32[]{:S(2)}) collective-permute-start(f32[3,72,128]{2,1,0:T(8,128)} %get-tuple-element.28), channel_id=1, source_target_pairs={{1,0},{2,1},{3,2},{4,3},{5,4},{6,5},{7,6},{8,7},{9,8},{10,9},{11,1... | collective-permute-start | bytes 331784 | tf_op jit(solution)/shard_map/ppermute | solution.py:560
  32.5 4.7 %collective-permute-done.1.north = f32[3,72,128]{2,1,0:T(8,128)S(1)} collective-permute-done((f32[3,72,128]{2,1,0:T(8,128)}, f32[3,72,128]{2,1,0:T(8,128)S(1)}, u32[]{:S(2)}, u32[]{:S(2)}) %collective-permute-start.1) | collective-permute-done | bytes 110624 | tf_op jit(solution)/shard_map/ppermute | solution.py:558
  37.1 0.0 collective-permute-done.3.east_col
  37.1 0.0 collective-permute-done.south.clat_south
  37.2 0.0 collective-permute-done.2.west_col.clon_col
  37.2 8.4 %all-to-all-start = ((f32[128,24,128]{2,1,0:T(8,128)}), f32[128,24,128]{2,1,0:T(8,128)S(1)}, u32[]{:S(2)}, u32[]{:S(2)}) async-start(f32[128,24,128]{2,1,0:T(8,128)} %get-tuple-element.34), calls=%async_computation | async-start | bytes 3145728 | tf_op jit(solution)/shard_map/all_to_all | solution.py:563
  45.6 0.0 copy-done
  45.6 0.1 copy.10
  45.7 0.0 copy-done.1
  45.7 0.1 add_convert_fusion.table.refs_1_
  45.9 0.1 pad_maximum_fusion.weights
  46.0 11.7 %shard_map.96 = (f32[3,45,72,128]{3,2,1,0:T(8,128)}, f32[3,72,128]{2,1,0:T(8,128)S(1)}, f32[3,72,128]{2,1,0:T(8,128)S(1)}, f32[3,72,128]{2,1,0:T(8,128)S(1)}, f32[3,72,128]{2,1,0:T(8,128)S(1)}) custom-call(s32[1]{0:T(128)} %bitcast.lat_ref, f32[3,45,72,128]{3,2,1,0:T(8,128)} %bitcast.11, f32[3,45,72,128]{3,2,1,0:T(8,128)} %bitcast.12, ...), custom_call_target="tpu_custom_call" | custom-call | flops 537477120 | bytes 14929920 | tf_op jit(solution)/shard_map/pallas_call | solution.py:380
  57.7 11.9 %all-to-all-done.got_at = f32[128,24,128]{2,1,0:T(8,128)S(1)} async-done(((f32[128,24,128]{2,1,0:T(8,128)}), f32[128,24,128]{2,1,0:T(8,128)S(1)}, u32[]{:S(2)}, u32[]{:S(2)}) %all-to-all-start) | async-done | bytes 1572896 | tf_op jit(solution)/shard_map/all_to_all | solution.py:563
  69.6 32.7 %shard_map.97 = (f32[2720,256]{1,0:T(8,128)}, f32[3,72,128]{2,1,0:T(8,128)S(1)}, f32[3,72,128]{2,1,0:T(8,128)S(1)}, f32[3,72,128]{2,1,0:T(8,128)S(1)}, f32[3,72,128]{2,1,0:T(8,128)S(1)}) custom-call(f32[128,24,128]{2,1,0:T(8,128)S(1)} %all-to-all-done.got_at, f32[3,72,128]{2,1,0:T(8,128)S(1)} %get-tuple-element.35.plain_up, ...), custom_call_target="tpu_custom_call" | custom-call | flops 22817013760 | bytes 1572864 | tf_op jit(solution)/shard_map/pallas_call | solution.py:512
  102.3 0.8 collective-permute-start.4
  103.1 4.9 %collective-permute-start.5 = (f32[3,72,128]{2,1,0:T(8,128)S(1)}, f32[3,72,128]{2,1,0:T(8,128)S(1)}, u32[]{:S(2)}, u32[]{:S(2)}) collective-permute-start(f32[3,72,128]{2,1,0:T(8,128)S(1)} %get-tuple-element.40), channel_id=1, source_target_pairs={{1,0},{2,1},{3,2},{4,3},{5,4},{6,5},{7,6},{8,7},{9,8},{10,9},{11,1... | collective-permute-start | bytes 331784 | tf_op jit(solution)/shard_map/ppermute | solution.py:573
  108.0 2.7 %collective-permute-start.6 = (f32[3,72,128]{2,1,0:T(8,128)S(1)}, f32[3,72,128]{2,1,0:T(8,128)S(1)}, u32[]{:S(2)}, u32[]{:S(2)}) collective-permute-start(f32[3,72,128]{2,1,0:T(8,128)S(1)} %get-tuple-element.41), channel_id=1, source_target_pairs={{0,32},{32,64},{64,96},{96,0},{1,33},{33,65},{65,97},{97,1},{2,34}... | collective-permute-start | bytes 331784 | tf_op jit(solution)/shard_map/ppermute | solution.py:570
  110.7 0.0 collective-permute-start.7
  110.7 0.0 collective-permute-done.4.west_col
  110.8 0.0 collective-permute-done.5.east_col
  110.8 1.7 %collective-permute-done.6.south = f32[3,72,128]{2,1,0:T(8,128)S(1)} collective-permute-done((f32[3,72,128]{2,1,0:T(8,128)S(1)}, f32[3,72,128]{2,1,0:T(8,128)S(1)}, u32[]{:S(2)}, u32[]{:S(2)}) %collective-permute-start.6) | collective-permute-done | bytes 110624 | tf_op jit(solution)/shard_map/ppermute | solution.py:570
  112.5 3.9 %collective-permute-done.7.north = f32[3,72,128]{2,1,0:T(8,128)S(1)} collective-permute-done((f32[3,72,128]{2,1,0:T(8,128)S(1)}, f32[3,72,128]{2,1,0:T(8,128)S(1)}, u32[]{:S(2)}, u32[]{:S(2)}) %collective-permute-start.7) | collective-permute-done | bytes 110624 | tf_op jit(solution)/shard_map/ppermute | solution.py:571
  116.4 10.5 %shard_map.98 = (f32[3,45,72,128]{3,2,1,0:T(8,128)}, f32[3,45,128]{2,1,0:T(8,128)}) custom-call(s32[1]{0:T(128)} %bitcast.lat_ref, f32[3,45,72,128]{3,2,1,0:T(8,128)} %get-tuple-element.33.field.field_west.field_east, f32[3,45,72,128]{3,2,1,0:T(8,128)} %get-tuple-element.33.field.field_west.field_east, ...), custom_call_target="tpu_custom_call" | custom-call | flops 537477120 | bytes 14929920 | tf_op jit(solution)/shard_map/pallas_call | solution.py:380
  (2 shorter events, 0.0 us)
Async XLA Ops:
  21.7 23.9 %copy-start = (f32[72,72]{1,0:T(8,128)S(1)}, f32[72,72]{1,0:T(8,128)}, u32[]{:S(2)}) copy-start(f32[72,72]{1,0:T(8,128)} %param.11) | copy-start | bytes 62212
  21.7 24.0 %copy-start.1 = (s32[20]{0:T(128)S(1)}, s32[20]{0:T(128)}, u32[]{:S(2)}) copy-start(s32[20]{0:T(128)} %param.15) | copy-start | bytes 244
  21.7 15.4 %collective-permute-start = (f32[4,72,128]{2,1,0:T(8,128)}, f32[4,72,128]{2,1,0:T(8,128)S(1)}, u32[]{:S(2)}, u32[]{:S(2)}) collective-permute-start(f32[4,72,128]{2,1,0:T(8,128)} %get-tuple-element.25), channel_id=1, source_target_pairs={{0,32},{32,64},{64,96},{96,0},{1,33},{33,65},{65,97},{97,1},{2,34}... | collective-permute-start | bytes 442376 | tf_op jit(solution)/shard_map/ppermute | solution.py:557
  26.8 10.4 %collective-permute-start.2 = (f32[4,72,128]{2,1,0:T(8,128)}, f32[4,72,128]{2,1,0:T(8,128)S(1)}, u32[]{:S(2)}, u32[]{:S(2)}) collective-permute-start(f32[4,72,128]{2,1,0:T(8,128)} %get-tuple-element.27), channel_id=1, source_target_pairs={{0,1},{1,2},{2,3},{3,4},{4,5},{5,6},{6,7},{7,8},{8,9},{9,10},{10,1... | collective-permute-start | bytes 442376 | tf_op jit(solution)/shard_map/ppermute | solution.py:559
  28.1 9.0 %collective-permute-start.1 = (f32[3,72,128]{2,1,0:T(8,128)}, f32[3,72,128]{2,1,0:T(8,128)S(1)}, u32[]{:S(2)}, u32[]{:S(2)}) collective-permute-start(f32[3,72,128]{2,1,0:T(8,128)} %get-tuple-element.26), channel_id=1, source_target_pairs={{32,0},{64,32},{96,64},{0,96},{33,1},{65,33},{97,65},{1,97},{34,2}... | collective-permute-start | bytes 331784 | tf_op jit(solution)/shard_map/ppermute | solution.py:558
  28.1 9.0 %collective-permute-start.3 = (f32[3,72,128]{2,1,0:T(8,128)}, f32[3,72,128]{2,1,0:T(8,128)S(1)}, u32[]{:S(2)}, u32[]{:S(2)}) collective-permute-start(f32[3,72,128]{2,1,0:T(8,128)} %get-tuple-element.28), channel_id=1, source_target_pairs={{1,0},{2,1},{3,2},{4,3},{5,4},{6,5},{7,6},{8,7},{9,8},{10,9},{11,1... | collective-permute-start | bytes 331784 | tf_op jit(solution)/shard_map/ppermute | solution.py:560
  37.2 32.4 %all-to-all-start = ((f32[128,24,128]{2,1,0:T(8,128)}), f32[128,24,128]{2,1,0:T(8,128)S(1)}, u32[]{:S(2)}, u32[]{:S(2)}) async-start(f32[128,24,128]{2,1,0:T(8,128)} %get-tuple-element.34), calls=%async_computation | async-start | bytes 3145728 | tf_op jit(solution)/shard_map/all_to_all | solution.py:563
  102.3 8.5 %collective-permute-start.4 = (f32[3,72,128]{2,1,0:T(8,128)S(1)}, f32[3,72,128]{2,1,0:T(8,128)S(1)}, u32[]{:S(2)}, u32[]{:S(2)}) collective-permute-start(f32[3,72,128]{2,1,0:T(8,128)S(1)} %get-tuple-element.39), channel_id=1, source_target_pairs={{0,1},{1,2},{2,3},{3,4},{4,5},{5,6},{6,7},{7,8},{8,9},{9,10},{10,1... | collective-permute-start | bytes 331784 | tf_op jit(solution)/shard_map/ppermute | solution.py:572
  103.1 7.6 %collective-permute-start.5 = (f32[3,72,128]{2,1,0:T(8,128)S(1)}, f32[3,72,128]{2,1,0:T(8,128)S(1)}, u32[]{:S(2)}, u32[]{:S(2)}) collective-permute-start(f32[3,72,128]{2,1,0:T(8,128)S(1)} %get-tuple-element.40), channel_id=1, source_target_pairs={{1,0},{2,1},{3,2},{4,3},{5,4},{6,5},{7,6},{8,7},{9,8},{10,9},{11,1... | collective-permute-start | bytes 331784 | tf_op jit(solution)/shard_map/ppermute | solution.py:573
  108.0 4.5 %collective-permute-start.6 = (f32[3,72,128]{2,1,0:T(8,128)S(1)}, f32[3,72,128]{2,1,0:T(8,128)S(1)}, u32[]{:S(2)}, u32[]{:S(2)}) collective-permute-start(f32[3,72,128]{2,1,0:T(8,128)S(1)} %get-tuple-element.41), channel_id=1, source_target_pairs={{0,32},{32,64},{64,96},{96,0},{1,33},{33,65},{65,97},{97,1},{2,34}... | collective-permute-start | bytes 331784 | tf_op jit(solution)/shard_map/ppermute | solution.py:570
  110.7 5.7 %collective-permute-start.7 = (f32[3,72,128]{2,1,0:T(8,128)S(1)}, f32[3,72,128]{2,1,0:T(8,128)S(1)}, u32[]{:S(2)}, u32[]{:S(2)}) collective-permute-start(f32[3,72,128]{2,1,0:T(8,128)S(1)} %get-tuple-element.42), channel_id=1, source_target_pairs={{32,0},{64,32},{96,64},{0,96},{33,1},{65,33},{97,65},{1,97},{34,2}... | collective-permute-start | bytes 331784 | tf_op jit(solution)/shard_map/ppermute | solution.py:571

commit v6 on v5

--- a/solution.py
+++ b/solution.py
@@ -15,6 +15,7 @@
 BLOCK = 15
 VMEM_LIMIT = 52 * 2**20
 PACK_LIMIT = 58 * 2**20
+SMALL_LIMIT = 48 * 2**20
 ADD_LIMIT = 49 * 2**20
 
 
@@ -85,7 +86,7 @@
 
 
 PACK = (16, 8192)
-ADD = (17, 4096)
+ADD = (17, 8192)
 
 
 def whole_part(value, divisor):
@@ -220,86 +221,68 @@
     return jnp.concatenate([high, high, matrix - high], axis=1).astype(bf16)
 
 
-def step_kernel(
-    lat_ref,
-    field,
-    field_west,
-    field_east,
-    clon,
-    clon_before,
-    clat,
-    west_col,
-    east_col,
-    clon_col,
-    south,
-    north,
-    clat_south,
-    weights,
-    *refs,
-    lat_size,
-    second,
-):
+def step_kernel(*refs, names, lat_size):
+    ref = dict(zip(names, refs))
+    second = "total" in ref
+    field, clon, clat, out = ref["field"], ref["clon"], ref["clat"], ref["out"]
     species, block, levels, rows = field.shape
     lane = lax.broadcasted_iota(jnp.int32, (levels, rows), 1)
     first, last = lane == 0, lane == rows - 1
-    lat = lat_ref[0]
-    below = jnp.where(jnp.logical_and(first, lat == 0), 0.0, 1.0)
-    inside = jnp.where(jnp.logical_and(last, lat == lat_size - 1), 0.0, 1.0)
-    w = weights[...]
     here = pl.program_id(0)
     at_start, at_end = here == 0, here == pl.num_programs(0) - 1
     start = here * block
-    turn = lax.rem(rows - 2 * start, rows)
-    even = lane % 2 == 0
-
-    def turned(a, b):
-        return pltpu.roll(jnp.where(even, a, b), turn, 1)
-
-    halos = [turned(south[s], north[s]) for s in range(species)]
-    courant_south = pltpu.roll(clat_south[0], turn, 1)
+    w = ref["weights"][...]
     waiting = []
 
     def back(v, i):
-        return pltpu.roll(v, rows - 2 * i, 1) if i else v
+        return pltpu.roll(v, (rows - 2 * i) % rows, 1) if i else v
 
     if second:
-        total, table, out, flux = refs
-        t = table[...]
-        akl = t.shape[1] // 4
+        lat = ref["lat"][0]
+        below = jnp.where(jnp.logical_and(first, lat == 0), 0.0, 1.0)
+        inside = jnp.where(jnp.logical_and(last, lat == lat_size - 1), 0.0, 1.0)
+        turn = lax.rem(rows - 2 * start, rows)
+        even = lane % 2 == 0
+        ends = jnp.logical_or(first, last)
+        halos = [
+            pltpu.roll(jnp.where(even, ref["south"][s], ref["north"][s]), turn, 1) for s in range(species)
+        ]
+        left_out = [pltpu.roll(ref["lanes"][s], turn, 1) for s in range(species)]
+        courant_south = pltpu.roll(ref["clat_south"][0], turn, 1)
+        t = ref["table"][...]
+        cols = pl.num_programs(0) * block
         wanted = []
         made = {}
 
         def make(ready):
             forcing = jnp.dot(t, jnp.concatenate([p for _, _, p in ready], axis=1), preferred_element_type=f32)
-            for k, (key, v, _) in enumerate(ready):
-                made[key] = v + forcing[:, k * rows : (k + 1) * rows]
-
-        def want(s, i, v, x):
-            wanted.append(((s, i), v, spread(total, s * cols + x, rows, akl)))
-            if len(wanted) == 2:
-                make(wanted)
-                wanted.clear()
-
-        cols = pl.num_programs(0) * block
+            for k, ((s, i), v, _) in enumerate(ready):
+                v = v + forcing[:, k * rows : (k + 1) * rows] + jnp.where(ends, back(left_out[s], i), 0.0)
+                if i == 0:
+                    v = v + jnp.where(at_start, ref["column_start"][s], 0.0)
+                if i == block - 1:
+                    v = v + jnp.where(at_end, ref["column_end"][s], 0.0)
+                made[s, i] = v
+
         for i in range(-1, block + 1):
+            x = jnp.clip(start + i, 0, cols - 1)
             for s in range(species):
-                if i < 0:
-                    want(s, i, field_west[s, 0], jnp.maximum(start - 1, 0))
-                elif i == block:
-                    want(s, i, field_east[s, 0], jnp.minimum(start + block, cols - 1))
-                else:
-                    want(s, i, field[s, i], start + i)
+                v = ref["field_west"][s, 0] if i < 0 else ref["field_east"][s, 0] if i == block else field[s, i]
+                wanted.append(((s, i), v, spread(ref["total"], s * cols + x, rows, t.shape[1] // 4)))
+                if len(wanted) == 2:
+                    make(wanted)
+                    wanted.clear()
         if wanted:
             make(wanted)
 
         def at_column(s, i):
             return made[s, i]
     else:
-        out, up, down, west, east = refs
+        below, inside = jnp.where(first, 0.0, 1.0), jnp.where(last, 0.0, 1.0)
         finished = [[None] * block for _ in range(species)]
 
         def at_column(s, i):
-            return field_west[s, 0] if i < 0 else field_east[s, 0] if i == block else field[s, i]
+            return ref["field_west"][s, 0] if i < 0 else ref["field_east"][s, 0] if i == block else field[s, i]
 
     def mix(ready):
         mixed = jnp.dot(
@@ -309,37 +292,46 @@
             m = mixed[:, k * rows : (k + 1) * rows]
             out[s, i] = m
             if second:
-                flux[s, pl.ds(start + i, 1), :] = at_column(s, i)[0:1] + m[0:1]
+                ref["flux"][s, pl.ds(start + i, 1), :] = at_column(s, i)[0:1] + m[0:1]
             else:
                 finished[s][i] = m
 
     for i in range(block):
         cl, cw = clon[i], clat[i]
-        cl_west = clon[i - 1] if i else jnp.where(at_start, clon_col[0], clon_before[0])
+        cl_west = clon[i - 1] if i else ref["clon_before"][0]
+        if i == 0 and second:
+            cl_west = jnp.where(at_start, ref["clon_col"][0], cl_west)
         e = jnp.maximum(cl, 0.0) + kappa_mix
         w_ = kappa_mix - jnp.minimum(cl_west, 0.0)
+        if not second and i == 0:
+            w_ = jnp.where(at_start, 0.0, w_)
+        if not second and i == block - 1:
+            e = jnp.where(at_end, 0.0, e)
         n = (jnp.maximum(cw, 0.0) + kappa_mix) * inside
-        cs = jnp.where(first, back(courant_south, i), pltpu.roll(cw, 1, 1))
+        cs = pltpu.roll(cw, 1, 1)
+        if second:
+            cs = jnp.where(first, back(courant_south, i), cs)
         s_ = (kappa_mix - jnp.minimum(cs, 0.0)) * below
         centre = 1.0 - (e + w_ + n + s_)
         for s in range(species):
             v, v_w, v_e = at_column(s, i), at_column(s, i - 1), at_column(s, i + 1)
-            if i == 0:
-                v_w = jnp.where(at_start, west_col[s], v_w)
-            if i == block - 1:
-                v_e = jnp.where(at_end, east_col[s], v_e)
-            halo = back(halos[s], i)
-            v_n = jnp.where(last, halo, pltpu.roll(v, rows - 1, 1))
-            v_s = jnp.where(first, halo, pltpu.roll(v, 1, 1))
+            v_n, v_s = pltpu.roll(v, rows - 1, 1), pltpu.roll(v, 1, 1)
+            if second:
+                if i == 0:
+                    v_w = jnp.where(at_start, ref["west_col"][s], v_w)
+                if i == block - 1:
+                    v_e = jnp.where(at_end, ref["east_col"][s], v_e)
+                halo = back(halos[s], i)
+                v_n, v_s = jnp.where(last, halo, v_n), jnp.where(first, halo, v_s)
             h = centre * v + e * v_e + w_ * v_w + n * v_n + s_ * v_s
-            high, low = split(h)
-            waiting.append((s, i, jnp.concatenate([high, low, high], axis=0).astype(bf16)))
+            waiting.append((s, i, mix_parts(h)))
             if len(waiting) == 2:
                 mix(waiting)
                 waiting.clear()
     if waiting:
         mix(waiting)
     if not second:
+        up, down, west, east = ref["up"], ref["down"], ref["west"], ref["east"]
 
         @pl.when(at_start)
         def _():
@@ -358,6 +350,92 @@
             down[s] = edge_lanes(finished[s], down[s], start, False)
 
 
+def mix_parts(h):
+    high, low = split(h)
+    return jnp.concatenate([high, low, high], axis=0).astype(bf16)
+
+
+def left_out_kernel(
+    lat_ref,
+    up_own,
+    down_own,
+    west_own,
+    east_own,
+    south,
+    north,
+    west,
+    east,
+    weights,
+    up_in,
+    down_in,
+    west_in,
+    east_in,
+    up,
+    down,
+    west_out,
+    east_out,
+    lanes,
+    column_start,
+    column_end,
+    *,
+    cols,
+    lat_size,
+):
+    species, levels, rows = up_in.shape
+    lane = lax.broadcasted_iota(jnp.int32, (levels, rows), 1)
+    even = lane % 2 == 0
+    ends = jnp.logical_or(lane == 0, lane == rows - 1)
+    lat = lat_ref[0]
+    below = jnp.where(lat == 0, 0.0, 1.0)
+    inside = jnp.where(lat == lat_size - 1, 0.0, 1.0)
+    far = 2 * (cols - 1)
+
+    def later(v):
+        return pltpu.roll(v, 1, 1)
+
+    def sooner(v):
+        return pltpu.roll(v, rows - 1, 1)
+
+    n = (jnp.maximum(sooner(up_own[species]), 0.0) + kappa_mix) * inside
+    s_ = (kappa_mix - jnp.minimum(south[species], 0.0)) * below
+    w_ = kappa_mix - jnp.minimum(west[species], 0.0)
+    e = jnp.maximum(west_own[species], 0.0) + kappa_mix
+    w = weights[...]
+    for s in range(species):
+        rim = jnp.where(even, s_ * (south[s] - later(down_own[s])), n * (north[s] - sooner(up_own[s])))
+        terms = [rim, w_ * (west[s] - east_own[s]), e * (east[s] - west_own[s])]
+        mixed = jnp.dot(w, jnp.concatenate([mix_parts(h) for h in terms], axis=1), preferred_element_type=f32)
+        c, c_start, c_end = [mixed[:, k * rows : (k + 1) * rows] for k in range(3)]
+        lanes[s], column_start[s], column_end[s] = c, c_start, c_end
+        up[s] = (
+            up_in[s]
+            + jnp.where(even, later(c), 0.0)
+            + jnp.where(lane == 0, later(c_start), 0.0)
+            + jnp.where(lane == far, pltpu.roll(c_end, far + 1, 1), 0.0)
+        )
+        down[s] = (
+            down_in[s]
+            + jnp.where(even, 0.0, sooner(c))
+            + jnp.where(lane == rows - 1, sooner(c_start), 0.0)
+            + jnp.where(lane == far - 1, pltpu.roll(c_end, far - 1, 1), 0.0)
+        )
+        west_out[s] = west_in[s] + c_end + jnp.where(ends, pltpu.roll(c, rows - far, 1), 0.0)
+        east_out[s] = east_in[s] + c_start + jnp.where(ends, c, 0.0)
+
+
+def left_out(lat, own, halo, weights, edges, cols, lat_size):
+    shape = jax.ShapeDtypeStruct(edges[0].shape, f32)
+    vmem = pl.BlockSpec(memory_space=pltpu.VMEM)
+    return pl.pallas_call(
+        functools.partial(left_out_kernel, cols=cols, lat_size=lat_size),
+        out_shape=(shape,) * 7,
+        in_specs=[pl.BlockSpec(memory_space=pltpu.SMEM)] + [vmem] * 13,
+        out_specs=(vmem,) * 7,
+        compiler_params=pltpu.CompilerParams(vmem_limit_bytes=SMALL_LIMIT),
+        cost_estimate=pl.CostEstimate(flops=shape.size * 3000, bytes_accessed=shape.size * 100, transcendentals=0),
+    )(lat, *own, *halo, weights, *edges)
+
+
 def spread(total, sx, rows, akl):
     pair = total[
         pl.ds(pl.multiple_of((sx >> 1) * 2 * akl, 8), 2 * akl),
@@ -366,60 +444,50 @@
     return jnp.concatenate(split(pair), axis=0).astype(bf16)
 
 
-def step(lat, field, clon, clat, halo, weights, lat_size, total=None, table=None):
+def step(field, clon, clat, weights, lat_size, more=None):
     species, cols, levels, rows = field.shape
     columns = pl.BlockSpec((species, BLOCK, levels, rows), lambda i: (0, i, 0, 0))
     courant = pl.BlockSpec((BLOCK, levels, rows), lambda i: (i, 0, 0))
     whole = lambda shape: pl.BlockSpec(shape, lambda i: (0,) * len(shape))
     part = lambda at: pl.BlockSpec((1, levels, rows), lambda i: (at, 0, 0))
-    west, east, clon_west, south, north, clat_south = halo
-    three = whole((species, levels, rows))
-    second = total is not None
-    more = (total, table) if second else ()
-    shapes = [(species, cols, rows)] if second else [(species, levels, rows)] * 4
+    three = (species, levels, rows)
+    given = {
+        "field": (field, columns),
+        "field_west": (
+            field,
+            pl.BlockSpec((species, 1, levels, rows), lambda i: (0, jnp.maximum(i * BLOCK - 1, 0), 0, 0)),
+        ),
+        "field_east": (
+            field,
+            pl.BlockSpec((species, 1, levels, rows), lambda i: (0, jnp.minimum(i * BLOCK + BLOCK, cols - 1), 0, 0)),
+        ),
+        "clon": (clon, courant),
+        "clon_before": (clon, pl.BlockSpec((1, levels, rows), lambda i: (jnp.maximum(i * BLOCK - 1, 0), 0, 0))),
+        "clat": (clat, courant),
+        "weights": (weights, whole(weights.shape)),
+    }
+    if more is None:
+        made = dict(up=three, down=three, west=three, east=three)
+    else:
+        made = dict(flux=(species, cols, rows))
+        for name, value in more.items():
+            spec = whole(value.shape)
+            if name == "lat":
+                spec = pl.BlockSpec(memory_space=pltpu.SMEM)
+            elif name in ("clon_col", "clat_south"):
+                spec = part(species)
+            given[name] = (value, spec)
     return pl.pallas_call(
-        functools.partial(step_kernel, lat_size=lat_size, second=second),
-        out_shape=[pltpu.HBM(field.shape, f32)] + [jax.ShapeDtypeStruct(shape, f32) for shape in shapes],
+        functools.partial(step_kernel, names=(*given, "out", *made), lat_size=lat_size),
+        out_shape=[pltpu.HBM(field.shape, f32)] + [jax.ShapeDtypeStruct(shape, f32) for shape in made.values()],
         grid=(cols // BLOCK,),
-        in_specs=[
-            pl.BlockSpec(memory_space=pltpu.SMEM),
-            columns,
-            pl.BlockSpec((species, 1, levels, rows), lambda i: (0, jnp.maximum(i * BLOCK - 1, 0), 0, 0)),
-            pl.BlockSpec((species, 1, levels, rows), lambda i: (0, jnp.minimum(i * BLOCK + BLOCK, cols - 1), 0, 0)),
-            courant,
-            pl.BlockSpec((1, levels, rows), lambda i: (jnp.maximum(i * BLOCK - 1, 0), 0, 0)),
-            courant,
-            three,
-            three,
-            part(species),
-            three,
-            three,
-            part(species),
-            whole(weights.shape),
-            *[whole(m.shape) for m in more],
-        ],
-        out_specs=[columns] + [whole(shape) for shape in shapes],
+        in_specs=[spec for _, spec in given.values()],
+        out_specs=[columns] + [whole(shape) for shape in made.values()],
         compiler_params=pltpu.CompilerParams(vmem_limit_bytes=VMEM_LIMIT),
         cost_estimate=pl.CostEstimate(
             flops=field.size * levels * 6, bytes_accessed=field.size * 12, transcendentals=0
         ),
-    )(
-        lat,
-        field,
-        field,
-        field,
-        clon,
-        clon,
-        clat,
-        west,
-        east,
-        clon_west,
-        south,
-        north,
-        clat_south,
-        weights,
-        *more,
-    )
+    )(*[value for value, _ in given.values()])
 
 
 def add_kernel(
@@ -553,26 +621,40 @@
     clat = courant_lat.transpose(1, 0, 2)
     lat = lax.axis_index("lat").reshape(1)
 
-    sent, up, down, west, east = pack(sounding_dest, sounding_values, sounding_target, field, clon, clat, n_tiles)
-    south = lax.ppermute(up, "lat", north_way)
-    north = lax.ppermute(down, "lat", south_way)
-    west = lax.ppermute(west, "lon", east_way)
-    east = lax.ppermute(east, "lon", west_way)
-    sent, south, north, west, east = lax.optimization_barrier((sent, south, north, west, east))
-    clat_south, clon_west = south, west
+    sent, *own = pack(sounding_dest, sounding_values, sounding_target, field, clon, clat, n_tiles)
     got = lax.all_to_all(sent, ("lat", "lon"), split_axis=0, concat_axis=0, tiled=True)
 
+    def exchange(up, down, west, east):
+        return (
+            lax.ppermute(up, "lat", north_way),
+            lax.ppermute(down, "lat", south_way),
+            lax.ppermute(west, "lon", east_way),
+            lax.ppermute(east, "lon", west_way),
+        )
+
+    halo = exchange(*own)
     weights = mix_weights(vertical_mix)
     table = (jnp.arange(levels, dtype=jnp.int32)[:, None] == level_index[None, :]).astype(bf16)
     table = jnp.concatenate([table] * 4, axis=1)
-    plain, *own_edges = step(lat, field, clon, clat, (west, east, clon_west, south, north, clat_south), weights, lat_size)
-    total, up, down, west, east = add_soundings(got, own_edges, table, cols)
-    south = lax.ppermute(up, "lat", north_way)
-    north = lax.ppermute(down, "lat", south_way)
-    west = lax.ppermute(west, "lon", east_way)
-    east = lax.ppermute(east, "lon", west_way)
-    halo = (west, east, clon_west, south, north, clat_south)
-    out, flux = step(lat, plain, clon, clat, halo, weights, lat_size, total, table)
+    plain, *edges = step(field, clon, clat, weights, lat_size)
+    total, *edges = add_soundings(got, edges, table, cols)
+    *edges, lanes, column_start, column_end = left_out(lat, own, halo, weights, edges, cols, lat_size)
+    south, north, west, east = exchange(*edges)
+    more = dict(
+        lat=lat,
+        south=south,
+        north=north,
+        west_col=west,
+        east_col=east,
+        clon_col=halo[2],
+        clat_south=halo[0],
+        total=total,
+        table=table,
+        lanes=lanes,
+        column_start=column_start,
+        column_end=column_end,
+    )
+    out, flux = step(plain, clon, clat, weights, lat_size, more)
     return out.transpose(0, 2, 1, 3), flux
 
 

time: 127 us -> 115 us (0.906)
  the two profiles are of different devices: /device:TPU:1 before, /device:TPU:30 now
where the time goes in v6:
time: 115 us
  Pallas kernels  76.2 us (66%)
  starting transfers between devices  26.8 us (23%)
  waiting for transfers between devices  10.7 us (9%)
    pallas_call x1, Pallas kernels, add_soundings(): pl.pallas_call(functools.partial(add_kernel, cols=cols), out_shape=(jax.S...  32.6 us
    pallas_call x2, Pallas kernels, step(): pl.pallas_call(functools.partial(step_kernel, names=(*given, 'out', *made...  22 us
    pallas_call x1, Pallas kernels, pack(): pl.pallas_call(pack_kernel, out_shape=tuple((jax.ShapeDtypeStruct(shape,...  21.1 us
    all_to_all x1, starting transfers between devices, on_device(): lax.all_to_all(sent, ('lat', 'lon'), split_axis=0, concat_axis=0, tiled=T...  10.2 us
    ppermute x2, starting transfers between devices, exchange(): lax.ppermute(west, 'lon', east_way)  9.14 us
    ppermute x2, waiting for transfers between devices, exchange(): lax.ppermute(east, 'lon', west_way)  6.64 us
    ppermute x2, starting transfers between devices, exchange(): lax.ppermute(down, 'lat', south_way)  6.57 us
    ppermute x2, waiting for transfers between devices, exchange(): lax.ppermute(west, 'lon', east_way)  2.32 us
  transfers between devices with their start and end apart: 9, of which 3 were waited for; matrix products, arithmetic and copies ran while one was open for 0% of the time, Pallas kernels for 37%

profile of v6, /device:TPU:30, one launch (start us, length us, event | category | flops | bytes accessed | tf_op | source)
XLA Modules:
  0.0 114.9 jit_solution(701219114118461384)
XLA Ops:
  0.6 21.1 %shard_map.96 = (f32[128,24,128]{2,1,0:T(8,128)}, f32[4,72,128]{2,1,0:T(8,128)}, f32[3,72,128]{2,1,0:T(8,128)}, f32[4,72,128]{2,1,0:T(8,128)}, f32[3,72,128]{2,1,0:T(8,128)}) custom-call(s32[1,8192]{1,0:T(1,128)} %bitcast.23, f32[20,8192]{1,0:T(8,128)} %values.1, s32[1,8192]{1,0:T(1,128)} %bitcast.24, f32[3,45,72,128]{3,2,1,0:T(8,128)} %bitcast.10, ...), custom_call_target="tpu_custom_call" | custom-call | flops 12884901888 | bytes 7270400 | tf_op jit(solution)/shard_map/pallas_call | solution.py:192
  21.7 0.0 copy-start.2
  21.8 0.0 copy-start.3
  21.8 0.0 copy-start
  21.8 0.0 copy-start.1
  21.8 0.0 copy-start.4
  21.8 10.2 %all-to-all-start = ((f32[128,24,128]{2,1,0:T(8,128)}), f32[128,24,128]{2,1,0:T(8,128)S(1)}, u32[]{:S(2)}, u32[]{:S(2)}) async-start(f32[128,24,128]{2,1,0:T(8,128)} %get-tuple-element.31), calls=%async_computation | async-start | bytes 3145728 | tf_op jit(solution)/shard_map/all_to_all | solution.py:625
  32.0 0.0 copy-done.2
  32.0 3.3 %collective-permute-start.1 = (f32[3,72,128]{2,1,0:T(8,128)S(1)}, f32[3,72,128]{2,1,0:T(8,128)S(1)}, u32[]{:S(2)}, u32[]{:S(2)}) collective-permute-start(f32[3,72,128]{2,1,0:T(8,128)S(1)} %copy-done.2), channel_id=1, source_target_pairs={{32,0},{64,32},{96,64},{0,96},{33,1},{65,33},{97,65},{1,97},{34,2}... | collective-permute-start | bytes 331784 | tf_op jit(solution)/shard_map/ppermute | solution.py:630
  35.4 0.0 copy-done.3
  35.4 0.8 collective-permute-start.3
  36.2 0.0 copy-done
  36.2 0.0 collective-permute-start
  36.2 0.0 copy-done.1
  36.2 5.7 %collective-permute-start.2 = (f32[4,72,128]{2,1,0:T(8,128)S(1)}, f32[4,72,128]{2,1,0:T(8,128)S(1)}, u32[]{:S(2)}, u32[]{:S(2)}) collective-permute-start(f32[4,72,128]{2,1,0:T(8,128)S(1)} %copy-done.1), channel_id=1, source_target_pairs={{0,1},{1,2},{2,3},{3,4},{4,5},{5,6},{6,7},{7,8},{8,9},{9,10},{10,1... | collective-permute-start | bytes 442376 | tf_op jit(solution)/shard_map/ppermute | solution.py:631
  41.9 0.0 copy-done.4
  41.9 0.1 copy.10
  42.0 0.1 pad_maximum_fusion.refs_6_.weights
  42.1 0.0 copy-start.5
  42.1 10.3 %shard_map.95 = (f32[3,45,72,128]{3,2,1,0:T(8,128)}, f32[3,72,128]{2,1,0:T(8,128)S(1)}, f32[3,72,128]{2,1,0:T(8,128)S(1)}, f32[3,72,128]{2,1,0:T(8,128)S(1)}, f32[3,72,128]{2,1,0:T(8,128)S(1)}) custom-call(f32[3,45,72,128]{3,2,1,0:T(8,128)} %bitcast.11, f32[3,45,72,128]{3,2,1,0:T(8,128)} %bitcast.12, f32[3,45,72,128]{3,2,1,0:T(8,128)} %bitcast.13, ...), custom_call_target="tpu_custom_call" | custom-call | flops 537477120 | bytes 14929920 | tf_op jit(solution)/shard_map/pallas_call | solution.py:480
  52.4 0.0 copy-done.5
  52.4 0.1 add_convert_fusion.table.refs_15_
  52.5 1.7 %all-to-all-done.got_at = f32[128,24,128]{2,1,0:T(8,128)S(1)} async-done(((f32[128,24,128]{2,1,0:T(8,128)}), f32[128,24,128]{2,1,0:T(8,128)S(1)}, u32[]{:S(2)}, u32[]{:S(2)}) %all-to-all-start) | async-done | bytes 1572896 | tf_op jit(solution)/shard_map/all_to_all | solution.py:625
  54.3 32.6 %shard_map.97 = (f32[2720,256]{1,0:T(8,128)}, f32[3,72,128]{2,1,0:T(8,128)S(1)}, f32[3,72,128]{2,1,0:T(8,128)S(1)}, f32[3,72,128]{2,1,0:T(8,128)S(1)}, f32[3,72,128]{2,1,0:T(8,128)S(1)}) custom-call(f32[128,24,128]{2,1,0:T(8,128)S(1)} %all-to-all-done.got_at, f32[3,72,128]{2,1,0:T(8,128)S(1)} %get-tuple-element.32.plain_up, ...), custom_call_target="tpu_custom_call" | custom-call | flops 22817013760 | bytes 1572864 | tf_op jit(solution)/shard_map/pallas_call | solution.py:580
  86.9 0.0 collective-permute-done.1.north
  86.9 0.0 collective-permute-done.3.east
  86.9 0.0 collective-permute-done.south.refs_13_
  86.9 0.0 collective-permute-done.2.west.refs_12_
  87.0 0.5 shard_map.98
  87.4 0.1 collective-permute-start.4
  87.5 3.2 %collective-permute-start.5 = (f32[3,72,128]{2,1,0:T(8,128)S(1)}, f32[3,72,128]{2,1,0:T(8,128)S(1)}, u32[]{:S(2)}, u32[]{:S(2)}) collective-permute-start(f32[3,72,128]{2,1,0:T(8,128)S(1)} %get-tuple-element.41), channel_id=1, source_target_pairs={{32,0},{64,32},{96,64},{0,96},{33,1},{65,33},{97,65},{1,97},{34,2}... | collective-permute-start | bytes 331784 | tf_op jit(solution)/shard_map/ppermute | solution.py:630
  90.8 3.4 %collective-permute-start.6 = (f32[3,72,128]{2,1,0:T(8,128)S(1)}, f32[3,72,128]{2,1,0:T(8,128)S(1)}, u32[]{:S(2)}, u32[]{:S(2)}) collective-permute-start(f32[3,72,128]{2,1,0:T(8,128)S(1)} %get-tuple-element.42), channel_id=1, source_target_pairs={{0,1},{1,2},{2,3},{3,4},{4,5},{5,6},{6,7},{7,8},{8,9},{9,10},{10,1... | collective-permute-start | bytes 331784 | tf_op jit(solution)/shard_map/ppermute | solution.py:631
  94.2 0.0 collective-permute-start.7
  94.2 0.0 collective-permute-done.4.refs_8_
  94.2 0.0 collective-permute-done.5.refs_9_
  94.2 2.3 %collective-permute-done.6.refs_10_ = f32[3,72,128]{2,1,0:T(8,128)S(1)} collective-permute-done((f32[3,72,128]{2,1,0:T(8,128)S(1)}, f32[3,72,128]{2,1,0:T(8,128)S(1)}, u32[]{:S(2)}, u32[]{:S(2)}) %collective-permute-start.6) | collective-permute-done | bytes 110624 | tf_op jit(solution)/shard_map/ppermute | solution.py:631
  96.5 6.6 %collective-permute-done.7.refs_11_ = f32[3,72,128]{2,1,0:T(8,128)S(1)} collective-permute-done((f32[3,72,128]{2,1,0:T(8,128)S(1)}, f32[3,72,128]{2,1,0:T(8,128)S(1)}, u32[]{:S(2)}, u32[]{:S(2)}) %collective-permute-start.7) | collective-permute-done | bytes 110624 | tf_op jit(solution)/shard_map/ppermute | solution.py:632
  103.2 11.7 %shard_map.99 = (f32[3,45,72,128]{3,2,1,0:T(8,128)}, f32[3,45,128]{2,1,0:T(8,128)}) custom-call(f32[3,45,72,128]{3,2,1,0:T(8,128)} %get-tuple-element.26.refs_0_.refs_1_.refs_2_, f32[3,45,72,128]{3,2,1,0:T(8,128)} %get-tuple-element.26.refs_0_.refs_1_.refs_2_, f32[3,45,72,128]{3,2,1,0:T(8,128)} %get-tuple-element.26.refs_0_.refs_1_.refs_2_, ...), custom_call_target="tpu_custom_call" | custom-call | flops 537477120 | bytes 14929920 | tf_op jit(solution)/shard_map/pallas_call | solution.py:480
  (2 shorter events, 0.0 us)
Async XLA Ops:
  21.7 10.3 %copy-start.2 = (f32[3,72,128]{2,1,0:T(8,128)S(1)}, f32[3,72,128]{2,1,0:T(8,128)}, u32[]{:S(2)}) copy-start(f32[3,72,128]{2,1,0:T(8,128)} %get-tuple-element.28.down_own) | copy-start | bytes 331780
  21.8 13.6 %copy-start.3 = (f32[3,72,128]{2,1,0:T(8,128)S(1)}, f32[3,72,128]{2,1,0:T(8,128)}, u32[]{:S(2)}) copy-start(f32[3,72,128]{2,1,0:T(8,128)} %get-tuple-element.30.east_own) | copy-start | bytes 331780
  21.8 14.4 %copy-start = (f32[4,72,128]{2,1,0:T(8,128)S(1)}, f32[4,72,128]{2,1,0:T(8,128)}, u32[]{:S(2)}) copy-start(f32[4,72,128]{2,1,0:T(8,128)} %get-tuple-element.27.up_own) | copy-start | bytes 442372
  21.8 14.4 %copy-start.1 = (f32[4,72,128]{2,1,0:T(8,128)S(1)}, f32[4,72,128]{2,1,0:T(8,128)}, u32[]{:S(2)}) copy-start(f32[4,72,128]{2,1,0:T(8,128)} %get-tuple-element.29.west_own) | copy-start | bytes 442372
  21.8 20.1 %copy-start.4 = (f32[72,72]{1,0:T(8,128)S(1)}, f32[72,72]{1,0:T(8,128)}, u32[]{:S(2)}) copy-start(f32[72,72]{1,0:T(8,128)} %param.11) | copy-start | bytes 62212
  21.8 32.5 %all-to-all-start = ((f32[128,24,128]{2,1,0:T(8,128)}), f32[128,24,128]{2,1,0:T(8,128)S(1)}, u32[]{:S(2)}, u32[]{:S(2)}) async-start(f32[128,24,128]{2,1,0:T(8,128)} %get-tuple-element.31), calls=%async_computation | async-start | bytes 3145728 | tf_op jit(solution)/shard_map/all_to_all | solution.py:625
  32.0 54.9 %collective-permute-start.1 = (f32[3,72,128]{2,1,0:T(8,128)S(1)}, f32[3,72,128]{2,1,0:T(8,128)S(1)}, u32[]{:S(2)}, u32[]{:S(2)}) collective-permute-start(f32[3,72,128]{2,1,0:T(8,128)S(1)} %copy-done.2), channel_id=1, source_target_pairs={{32,0},{64,32},{96,64},{0,96},{33,1},{65,33},{97,65},{1,97},{34,2}... | collective-permute-start | bytes 331784 | tf_op jit(solution)/shard_map/ppermute | solution.py:630
  35.4 51.5 %collective-permute-start.3 = (f32[3,72,128]{2,1,0:T(8,128)S(1)}, f32[3,72,128]{2,1,0:T(8,128)S(1)}, u32[]{:S(2)}, u32[]{:S(2)}) collective-permute-start(f32[3,72,128]{2,1,0:T(8,128)S(1)} %copy-done.3), channel_id=1, source_target_pairs={{1,0},{2,1},{3,2},{4,3},{5,4},{6,5},{7,6},{8,7},{9,8},{10,9},{11,1... | collective-permute-start | bytes 331784 | tf_op jit(solution)/shard_map/ppermute | solution.py:632
  36.2 50.8 %collective-permute-start = (f32[4,72,128]{2,1,0:T(8,128)S(1)}, f32[4,72,128]{2,1,0:T(8,128)S(1)}, u32[]{:S(2)}, u32[]{:S(2)}) collective-permute-start(f32[4,72,128]{2,1,0:T(8,128)S(1)} %copy-done), channel_id=1, source_target_pairs={{0,32},{32,64},{64,96},{96,0},{1,33},{33,65},{65,97},{97,1},{2,34}... | collective-permute-start | bytes 442376 | tf_op jit(solution)/shard_map/ppermute | solution.py:629
  36.2 50.8 %collective-permute-start.2 = (f32[4,72,128]{2,1,0:T(8,128)S(1)}, f32[4,72,128]{2,1,0:T(8,128)S(1)}, u32[]{:S(2)}, u32[]{:S(2)}) collective-permute-start(f32[4,72,128]{2,1,0:T(8,128)S(1)} %copy-done.1), channel_id=1, source_target_pairs={{0,1},{1,2},{2,3},{3,4},{4,5},{5,6},{6,7},{7,8},{8,9},{9,10},{10,1... | collective-permute-start | bytes 442376 | tf_op jit(solution)/shard_map/ppermute | solution.py:631
  42.1 10.3 %copy-start.5 = (s32[20]{0:T(128)S(1)}, s32[20]{0:T(128)}, u32[]{:S(2)}) copy-start(s32[20]{0:T(128)} %param.15) | copy-start | bytes 244
  87.4 6.8 %collective-permute-start.4 = (f32[3,72,128]{2,1,0:T(8,128)S(1)}, f32[3,72,128]{2,1,0:T(8,128)S(1)}, u32[]{:S(2)}, u32[]{:S(2)}) collective-permute-start(f32[3,72,128]{2,1,0:T(8,128)S(1)} %get-tuple-element.40), channel_id=1, source_target_pairs={{0,32},{32,64},{64,96},{96,0},{1,33},{33,65},{65,97},{97,1},{2,34}... | collective-permute-start | bytes 331784 | tf_op jit(solution)/shard_map/ppermute | solution.py:629
  87.5 6.7 %collective-permute-start.5 = (f32[3,72,128]{2,1,0:T(8,128)S(1)}, f32[3,72,128]{2,1,0:T(8,128)S(1)}, u32[]{:S(2)}, u32[]{:S(2)}) collective-permute-start(f32[3,72,128]{2,1,0:T(8,128)S(1)} %get-tuple-element.41), channel_id=1, source_target_pairs={{32,0},{64,32},{96,64},{0,96},{33,1},{65,33},{97,65},{1,97},{34,2}... | collective-permute-start | bytes 331784 | tf_op jit(solution)/shard_map/ppermute | solution.py:630
  90.8 5.8 %collective-permute-start.6 = (f32[3,72,128]{2,1,0:T(8,128)S(1)}, f32[3,72,128]{2,1,0:T(8,128)S(1)}, u32[]{:S(2)}, u32[]{:S(2)}) collective-permute-start(f32[3,72,128]{2,1,0:T(8,128)S(1)} %get-tuple-element.42), channel_id=1, source_target_pairs={{0,1},{1,2},{2,3},{3,4},{4,5},{5,6},{6,7},{7,8},{8,9},{9,10},{10,1... | collective-permute-start | bytes 331784 | tf_op jit(solution)/shard_map/ppermute | solution.py:631
  94.2 9.0 %collective-permute-start.7 = (f32[3,72,128]{2,1,0:T(8,128)S(1)}, f32[3,72,128]{2,1,0:T(8,128)S(1)}, u32[]{:S(2)}, u32[]{:S(2)}) collective-permute-start(f32[3,72,128]{2,1,0:T(8,128)S(1)} %get-tuple-element.43), channel_id=1, source_target_pairs={{1,0},{2,1},{3,2},{4,3},{5,4},{6,5},{7,6},{8,7},{9,8},{10,9},{11,1... | collective-permute-start | bytes 331784 | tf_op jit(solution)/shard_map/ppermute | solution.py:632

commit v7 on v6

--- a/solution.py
+++ b/solution.py
@@ -10,6 +10,7 @@
 kappa_mix = 0.05
 LANES = 128
 WIDE = 256
+TILE = 16
 f32 = jnp.float32
 bf16 = jnp.bfloat16
 BLOCK = 15
@@ -28,46 +29,48 @@
     return lax.dot_general(a, b, (((1,), (1,)), ((), ())), preferred_element_type=f32)
 
 
-def onehot_product(parts, group, spot, total, count, step, together, depth, beside=None):
-    rows, length = parts.shape
-    chunks = length // depth
+def onehot_product(parts, keys, tiles, spot, total, groups, step, together, depth, begin, end, onto=False, beside=None):
+    rows = parts.shape[0]
+    chunks = (end - begin) // depth
 
     def chunk(g, c):
-        at = pl.ds(pl.multiple_of(c * depth, depth), depth)
-        held, key = parts[:, at], group[:, at]
-        left = jnp.concatenate(
-            [
-                jnp.where(key == ((g * together + i) * step).astype(f32).astype(bf16), held, jnp.zeros_like(held))
-                for i in range(together)
-            ],
-            axis=0,
-        )
-        return nt_dot(left, spot[:, at])
+        at = pl.ds(pl.multiple_of(begin + c * depth, LANES), depth)
+        key = [k[:, at] for k in keys]
+        held = [parts[TILE * q : TILE * (q + 1), at] for q in range(len(tiles))]
+        none = jnp.zeros_like(held[0])
+        left = []
+        for i in range(together):
+            hit = {}
+            for kind in tiles:
+                if kind not in hit:
+                    which, offset = kind
+                    number = jnp.asarray((g * together + i) * step + offset, jnp.int32).astype(f32).astype(bf16)
+                    hit[kind] = key[which] == number
+            left += [jnp.where(hit[kind], part, none) for kind, part in zip(tiles, held)]
+        return nt_dot(jnp.concatenate(left, axis=0), spot[:, at])
 
     def of_group(g, carry):
         to = pl.ds(pl.multiple_of(g * (together * rows), together * rows), together * rows)
         if beside is not None:
             beside(g)
-        if chunks == 1:
+        if not onto:
             total[to, :] = chunk(g, 0)
+
+        def of_chunk(c, carry):
+            total[to, :] += chunk(g, c)
             return carry
 
-        def of_chunk(c, carry):
-            product = chunk(g, c)
-
-            @pl.when(c == 0)
-            def _():
-                total[to, :] = product
-
-            @pl.when(c > 0)
-            def _():
-                total[to, :] += product
-
-            return carry
-
-        return lax.fori_loop(0, chunks, of_chunk, carry)
-
-    lax.fori_loop(0, count // together, of_group, 0)
+        return lax.fori_loop(0 if onto else 1, chunks, of_chunk, carry)
+
+    lax.fori_loop(groups[0] // together, groups[1] // together, of_group, 0)
+
+
+def mark(spot, at, row):
+    row = jnp.broadcast_to(row.astype(f32), (TILE, row.shape[1])).astype(bf16)
+    base = lax.broadcasted_iota(jnp.int32, row.shape, 0).astype(f32).astype(bf16)
+    one, none = jnp.ones_like(row), jnp.zeros_like(row)
+    for q in range(WIDE // TILE):
+        spot[TILE * q : TILE * (q + 1), at] = jnp.where(row - jnp.asarray(TILE * q, bf16) == base, one, none)
 
 
 def edge_lanes(columns, kept, first, up, share=None):
@@ -86,11 +89,15 @@
 
 
 PACK = (16, 8192)
-ADD = (17, 8192)
+ADD = (17, 6144)
 
 
 def whole_part(value, divisor):
     return ((value.astype(f32) + 0.5) * (1.0 / divisor)).astype(jnp.int32)
+
+
+def half_segment(columns):
+    return -(-columns // 4) // 2 * 2 * WIDE
 
 
 def pack_kernel(
@@ -129,23 +136,26 @@
     upper = (
         lax.broadcasted_iota(jnp.int32, square, 0) < lax.broadcasted_iota(jnp.int32, square, 1)
     ).astype(f32).astype(bf16)
-    iota_w = lax.broadcasted_iota(jnp.int32, square, 0)
+
+    halfway = half_segment(species * cols)
 
     def rank(at, base):
         d = dest[:, at]
-        hot = iota_t == d
-        hot_f = jnp.where(hot, 1.0, 0.0)
-        earlier = jnp.dot(hot_f.astype(bf16), upper, preferred_element_type=f32) + base
-        own = jnp.sum(jnp.where(hot, earlier, 0.0), axis=0, keepdims=True).astype(jnp.int32)
-        low = own + (d & 1) * LANES
-        spot[:, at] = jnp.where(iota_w == low, 1.0, 0.0).astype(bf16)
-        group[:, at] = jnp.broadcast_to((d >> 1).astype(f32), (2 * held, WIDE)).astype(bf16)
         t = target[:, at]
         cell = whole_part(t, species)
         row_of = whole_part(cell, cols)
         segment = ((t - cell * species) * cols + cell - row_of * cols) * rows + row_of
+        upper_half = segment >= halfway
+        hot = iota_t == d
+        hot_f = jnp.where(hot, jnp.where(upper_half, 256.0, 1.0), 0.0)
+        earlier = jnp.dot(hot_f.astype(bf16), upper, preferred_element_type=f32) + base
+        own = jnp.sum(jnp.where(hot, earlier, 0.0), axis=0, keepdims=True).astype(jnp.int32)
+        slot = jnp.where(upper_half, LANES - 1 - (own >> 8), own & 255)
+        low = slot + (d & 1) * LANES
+        mark(spot, at, low)
+        group[:, at] = jnp.broadcast_to((d >> 1).astype(f32), (TILE, WIDE)).astype(bf16)
         row = jnp.concatenate(
-            [values[:, at], segment.astype(f32), jnp.zeros((held - levels - 1, WIDE), f32)], axis=0
+            [values[:, at], (segment + 1).astype(f32), jnp.zeros((held - levels - 1, WIDE), f32)], axis=0
         )
         parts[:, at] = jnp.concatenate(split(row), axis=0).astype(bf16)
         return base + jnp.sum(hot_f, axis=1, keepdims=True)
@@ -169,7 +179,10 @@
             if s < species:
                 down[s] = edge_lanes(columns, down[s], first, False, new)
 
-    onehot_product(parts, group, spot, total, n_tiles // 2, 1, *PACK, beside=take_edges)
+    tiles = ((0, 0),) * (2 * held // TILE)
+    onehot_product(
+        parts, [group], tiles, spot, total, (0, n_tiles // 2), 1, *PACK, 0, length, beside=take_edges
+    )
 
     def put(g, carry):
         for i in range(4):
@@ -198,7 +211,7 @@
         out_specs=(vmem,) * 5,
         scratch_shapes=(
             pltpu.VMEM((2 * held, length), bf16),
-            pltpu.VMEM((2 * held, length), bf16),
+            pltpu.VMEM((TILE, length), bf16),
             pltpu.VMEM((WIDE, length), bf16),
             pltpu.VMEM((n_tiles // 2 * 2 * held, WIDE), f32),
             pltpu.VMEM(field.shape, f32),
@@ -505,6 +518,7 @@
     got,
     parts,
     group,
+    middle,
     spot,
     sem_got,
     *,
@@ -521,26 +535,66 @@
     ]
     for copy in came:
         copy.start()
-    iota_w = lax.broadcasted_iota(jnp.int32, (WIDE, WIDE), 0)
-    second = (lax.broadcasted_iota(jnp.int32, (4 * akl, WIDE), 0) >= 2 * akl).astype(f32)
+    second = (lax.broadcasted_iota(jnp.int32, (TILE, WIDE), 0) >= TILE // 2).astype(f32)
+    quarter_of = lax.broadcasted_iota(jnp.int32, (held, slots), 1) // (slots // 4)
+    length = sources * slots
+    halfway = half_segment(species * cols)
+
+    def put(row, at):
+        wide = row.shape[1]
+        at = pl.ds(pl.multiple_of(at, LANES), wide)
+        segment = row[akl : akl + 1].astype(jnp.int32) - 1
+        mark(spot, at, segment & (WIDE - 1))
+        pair = jnp.broadcast_to((segment >> 8).astype(f32), (TILE, wide))
+        group[:, at] = pair.astype(bf16)
+        middle[:, at] = (pair - second[:, :wide]).astype(bf16)
+        high, low = split(row[:akl])
+        both = jnp.concatenate([high, low], axis=0)
+        parts[:, at] = jnp.concatenate([both, both], axis=0).astype(bf16)
+        return segment
 
     def prepare(g, carry):
-        for i in range(2):
-            b = 2 * g + i
-            row = jnp.concatenate([got[2 * b], got[2 * b + 1]], axis=1)
-            at = pl.ds(pl.multiple_of(b * WIDE, WIDE), WIDE)
-            segment = row[akl : akl + 1].astype(jnp.int32)
-            spot[:, at] = jnp.where(iota_w == (segment & (WIDE - 1)), 1.0, 0.0).astype(bf16)
-            group[:, at] = ((segment >> 8).astype(f32) - second).astype(bf16)
-            high, low = split(row[:akl])
-            both = jnp.concatenate([high, low], axis=0)
-            parts[:, at] = jnp.concatenate([both, both], axis=0).astype(bf16)
-        return carry
-
+        highest, lowest = carry
+        fours = []
+        for b in range(2):
+            turned = [got[8 * g + 4 * b + k] for k in range(4)]
+            turned = [pltpu.roll(v, k * (slots // 4), 1) if k else v for k, v in enumerate(turned)]
+            rows_of = []
+            for q in range(4):
+                row = turned[0]
+                for k in range(1, 4):
+                    row = jnp.where(quarter_of == (q + k) % 4, turned[k], row)
+                rows_of.append(row)
+            fours.append(rows_of)
+        row = [jnp.concatenate([fours[0][q], fours[1][q]], axis=1) for q in range(4)]
+        segment = put(row[0], g * WIDE)
+        highest = jnp.maximum(highest, segment)
+        put(row[1], length // 4 + 2 * g * WIDE)
+        put(row[2], length // 4 + (2 * g + 1) * WIDE)
+        segment = put(row[3], 3 * (length // 4) + g * WIDE)
+        lowest = jnp.minimum(lowest, jnp.where(segment < 0, 2 * halfway, segment))
+        return highest, lowest
+
+    carry = (jnp.full((1, WIDE), -1, jnp.int32), jnp.full((1, WIDE), 2 * halfway, jnp.int32))
     for q, copy in enumerate(came):
         copy.wait()
-        lax.fori_loop(q * quarter // 4, (q + 1) * quarter // 4, prepare, 0)
-    onehot_product(parts, group, spot, total, total.shape[0] // (4 * akl), 2, *ADD)
+        carry = lax.fori_loop(q * quarter // 8, (q + 1) * quarter // 8, prepare, carry)
+    highest, lowest = jnp.max(carry[0]), jnp.min(carry[1])
+
+    tiles = ((0, 0), (0, 0), (1, 0), (0, 1), (0, 1))
+    groups = total.shape[0] // (4 * akl)
+    lower, higher = (0, groups // 2), (groups // 2, groups)
+    add = functools.partial(onehot_product, parts, [group, middle], tiles, spot, total)
+    add(lower, 2, *ADD, 0, 3 * (length // 4))
+    add(higher, 2, *ADD, length // 4, length)
+
+    @pl.when(highest >= halfway)
+    def _():
+        add(higher, 2, ADD[0], length // 8, 0, length // 4, onto=True)
+
+    @pl.when(lowest < halfway)
+    def _():
+        add(lower, 2, ADD[0], length // 8, 3 * (length // 4), length, onto=True)
 
     t = table[...]
 
@@ -585,7 +639,8 @@
         scratch_shapes=(
             pltpu.VMEM(got.shape, f32),
             pltpu.VMEM((4 * akl, length), bf16),
-            pltpu.VMEM((4 * akl, length), bf16),
+            pltpu.VMEM((TILE, length), bf16),
+            pltpu.VMEM((TILE, length), bf16),
             pltpu.VMEM((WIDE, length), bf16),
             pltpu.SemaphoreType.DMA((4,)),
         ),

time: 115 us -> 108 us (0.939)
  Pallas kernels: 76.2 us -> 68.7 us
    pallas_call x1, Pallas kernels: 32.6 us -> 26.2 us  [add_soundings(): pl.pallas_call(functools.partial(add_kernel, cols=cols), out_shape=(jax.S...]
  transfers between devices with their start and end apart: 9 -> 9, of which waited for: 3 -> 3; matrix products, arithmetic and copies ran while one was open for 0% -> 0% of each run, Pallas kernels for 37% -> 34%
where the time goes in v7:
time: 108 us; the launch traced here: 107 us
  Pallas kernels  68.7 us (64%)
  starting transfers between devices  26.6 us (25%)
  waiting for transfers between devices  10.9 us (10%)
    pallas_call x1, Pallas kernels, add_soundings(): pl.pallas_call(functools.partial(add_kernel, cols=cols), out_shape=(jax.S...  26.2 us
    pallas_call x2, Pallas kernels, step(): pl.pallas_call(functools.partial(step_kernel, names=(*given, 'out', *made...  22 us
    pallas_call x1, Pallas kernels, pack(): pl.pallas_call(pack_kernel, out_shape=tuple((jax.ShapeDtypeStruct(shape,...  20.1 us
    all_to_all x1, starting transfers between devices, on_device(): lax.all_to_all(sent, ('lat', 'lon'), split_axis=0, concat_axis=0, tiled=T...  10.2 us
    ppermute x2, starting transfers between devices, exchange(): lax.ppermute(west, 'lon', east_way)  8.97 us
    ppermute x2, waiting for transfers between devices, exchange(): lax.ppermute(east, 'lon', west_way)  6.64 us
    ppermute x2, starting transfers between devices, exchange(): lax.ppermute(down, 'lat', south_way)  6.57 us
    ppermute x2, waiting for transfers between devices, exchange(): lax.ppermute(west, 'lon', east_way)  2.32 us
  transfers between devices with their start and end apart: 9, of which 3 were waited for; matrix products, arithmetic and copies ran while one was open for 0% of the time, Pallas kernels for 34%

profile of v7, /device:TPU:30, one launch (start us, length us, event | category | flops | bytes accessed | tf_op | source)
XLA Modules:
  0.0 107.4 jit_solution(17421334600774728995)
XLA Ops:
  0.6 20.1 %shard_map.96 = (f32[128,24,128]{2,1,0:T(8,128)}, f32[4,72,128]{2,1,0:T(8,128)}, f32[3,72,128]{2,1,0:T(8,128)}, f32[4,72,128]{2,1,0:T(8,128)}, f32[3,72,128]{2,1,0:T(8,128)}) custom-call(s32[1,8192]{1,0:T(1,128)} %bitcast.23, f32[20,8192]{1,0:T(8,128)} %values.1, s32[1,8192]{1,0:T(1,128)} %bitcast.24, f32[3,45,72,128]{3,2,1,0:T(8,128)} %bitcast.10, ...), custom_call_target="tpu_custom_call" | custom-call | flops 12884901888 | bytes 7270400 | tf_op jit(solution)/shard_map/pallas_call | solution.py:205
  20.7 0.0 copy-start.2
  20.7 0.0 copy-start.3
  20.7 0.0 copy-start
  20.7 0.0 copy-start.1
  20.7 0.0 copy-start.4
  20.8 10.2 %all-to-all-start = ((f32[128,24,128]{2,1,0:T(8,128)}), f32[128,24,128]{2,1,0:T(8,128)S(1)}, u32[]{:S(2)}, u32[]{:S(2)}) async-start(f32[128,24,128]{2,1,0:T(8,128)} %get-tuple-element.31), calls=%async_computation | async-start | bytes 3145728 | tf_op jit(solution)/shard_map/all_to_all | solution.py:680
  31.0 0.0 copy-done.2
  31.0 3.3 %collective-permute-start.1 = (f32[3,72,128]{2,1,0:T(8,128)S(1)}, f32[3,72,128]{2,1,0:T(8,128)S(1)}, u32[]{:S(2)}, u32[]{:S(2)}) collective-permute-start(f32[3,72,128]{2,1,0:T(8,128)S(1)} %copy-done.2), channel_id=1, source_target_pairs={{32,0},{64,32},{96,64},{0,96},{33,1},{65,33},{97,65},{1,97},{34,2}... | collective-permute-start | bytes 331784 | tf_op jit(solution)/shard_map/ppermute | solution.py:685
  34.3 0.0 copy-done.3
  34.4 0.8 collective-permute-start.3
  35.1 0.0 copy-done
  35.1 0.0 collective-permute-start
  35.1 0.0 copy-done.1
  35.2 5.5 %collective-permute-start.2 = (f32[4,72,128]{2,1,0:T(8,128)S(1)}, f32[4,72,128]{2,1,0:T(8,128)S(1)}, u32[]{:S(2)}, u32[]{:S(2)}) collective-permute-start(f32[4,72,128]{2,1,0:T(8,128)S(1)} %copy-done.1), channel_id=1, source_target_pairs={{0,1},{1,2},{2,3},{3,4},{4,5},{5,6},{6,7},{7,8},{8,9},{9,10},{10,1... | collective-permute-start | bytes 442376 | tf_op jit(solution)/shard_map/ppermute | solution.py:686
  40.7 0.0 copy-done.4
  40.7 0.1 copy.10
  40.8 0.1 pad_maximum_fusion.refs_6_.weights
  40.9 0.0 copy-start.5
  40.9 10.3 %shard_map.95 = (f32[3,45,72,128]{3,2,1,0:T(8,128)}, f32[3,72,128]{2,1,0:T(8,128)S(1)}, f32[3,72,128]{2,1,0:T(8,128)S(1)}, f32[3,72,128]{2,1,0:T(8,128)S(1)}, f32[3,72,128]{2,1,0:T(8,128)S(1)}) custom-call(f32[3,45,72,128]{3,2,1,0:T(8,128)} %bitcast.11, f32[3,45,72,128]{3,2,1,0:T(8,128)} %bitcast.12, f32[3,45,72,128]{3,2,1,0:T(8,128)} %bitcast.13, ...), custom_call_target="tpu_custom_call" | custom-call | flops 537477120 | bytes 14929920 | tf_op jit(solution)/shard_map/pallas_call | solution.py:493
  51.2 0.0 copy-done.5
  51.2 0.1 add_convert_fusion.table.refs_15_
  51.3 2.0 %all-to-all-done.got_at = f32[128,24,128]{2,1,0:T(8,128)S(1)} async-done(((f32[128,24,128]{2,1,0:T(8,128)}), f32[128,24,128]{2,1,0:T(8,128)S(1)}, u32[]{:S(2)}, u32[]{:S(2)}) %all-to-all-start) | async-done | bytes 1572896 | tf_op jit(solution)/shard_map/all_to_all | solution.py:680
  53.2 26.2 %shard_map.97 = (f32[2720,256]{1,0:T(8,128)}, f32[3,72,128]{2,1,0:T(8,128)S(1)}, f32[3,72,128]{2,1,0:T(8,128)S(1)}, f32[3,72,128]{2,1,0:T(8,128)S(1)}, f32[3,72,128]{2,1,0:T(8,128)S(1)}) custom-call(f32[128,24,128]{2,1,0:T(8,128)S(1)} %all-to-all-done.got_at, f32[3,72,128]{2,1,0:T(8,128)S(1)} %get-tuple-element.32.plain_up, ...), custom_call_target="tpu_custom_call" | custom-call | flops 22817013760 | bytes 1572864 | tf_op jit(solution)/shard_map/pallas_call | solution.py:634
  79.5 0.0 collective-permute-done.1.north
  79.5 0.0 collective-permute-done.3.east
  79.5 0.0 collective-permute-done.south.refs_13_
  79.5 0.0 collective-permute-done.2.west.refs_12_
  79.5 0.5 shard_map.98
  80.0 0.1 collective-permute-start.4
  80.1 3.2 %collective-permute-start.5 = (f32[3,72,128]{2,1,0:T(8,128)S(1)}, f32[3,72,128]{2,1,0:T(8,128)S(1)}, u32[]{:S(2)}, u32[]{:S(2)}) collective-permute-start(f32[3,72,128]{2,1,0:T(8,128)S(1)} %get-tuple-element.41), channel_id=1, source_target_pairs={{32,0},{64,32},{96,64},{0,96},{33,1},{65,33},{97,65},{1,97},{34,2}... | collective-permute-start | bytes 331784 | tf_op jit(solution)/shard_map/ppermute | solution.py:685
  83.3 3.4 %collective-permute-start.6 = (f32[3,72,128]{2,1,0:T(8,128)S(1)}, f32[3,72,128]{2,1,0:T(8,128)S(1)}, u32[]{:S(2)}, u32[]{:S(2)}) collective-permute-start(f32[3,72,128]{2,1,0:T(8,128)S(1)} %get-tuple-element.42), channel_id=1, source_target_pairs={{0,1},{1,2},{2,3},{3,4},{4,5},{5,6},{6,7},{7,8},{8,9},{9,10},{10,1... | collective-permute-start | bytes 331784 | tf_op jit(solution)/shard_map/ppermute | solution.py:686
  86.8 0.0 collective-permute-start.7
  86.8 0.0 collective-permute-done.4.refs_8_
  86.8 0.0 collective-permute-done.5.refs_9_
  86.8 2.3 %collective-permute-done.6.refs_10_ = f32[3,72,128]{2,1,0:T(8,128)S(1)} collective-permute-done((f32[3,72,128]{2,1,0:T(8,128)S(1)}, f32[3,72,128]{2,1,0:T(8,128)S(1)}, u32[]{:S(2)}, u32[]{:S(2)}) %collective-permute-start.6) | collective-permute-done | bytes 110624 | tf_op jit(solution)/shard_map/ppermute | solution.py:686
  89.1 6.6 %collective-permute-done.7.refs_11_ = f32[3,72,128]{2,1,0:T(8,128)S(1)} collective-permute-done((f32[3,72,128]{2,1,0:T(8,128)S(1)}, f32[3,72,128]{2,1,0:T(8,128)S(1)}, u32[]{:S(2)}, u32[]{:S(2)}) %collective-permute-start.7) | collective-permute-done | bytes 110624 | tf_op jit(solution)/shard_map/ppermute | solution.py:687
  95.7 11.7 %shard_map.99 = (f32[3,45,72,128]{3,2,1,0:T(8,128)}, f32[3,45,128]{2,1,0:T(8,128)}) custom-call(f32[3,45,72,128]{3,2,1,0:T(8,128)} %get-tuple-element.26.refs_0_.refs_1_.refs_2_, f32[3,45,72,128]{3,2,1,0:T(8,128)} %get-tuple-element.26.refs_0_.refs_1_.refs_2_, f32[3,45,72,128]{3,2,1,0:T(8,128)} %get-tuple-element.26.refs_0_.refs_1_.refs_2_, ...), custom_call_target="tpu_custom_call" | custom-call | flops 537477120 | bytes 14929920 | tf_op jit(solution)/shard_map/pallas_call | solution.py:493
  (2 shorter events, 0.0 us)
Async XLA Ops:
  20.7 10.3 %copy-start.2 = (f32[3,72,128]{2,1,0:T(8,128)S(1)}, f32[3,72,128]{2,1,0:T(8,128)}, u32[]{:S(2)}) copy-start(f32[3,72,128]{2,1,0:T(8,128)} %get-tuple-element.28.down_own) | copy-start | bytes 331780
  20.7 13.6 %copy-start.3 = (f32[3,72,128]{2,1,0:T(8,128)S(1)}, f32[3,72,128]{2,1,0:T(8,128)}, u32[]{:S(2)}) copy-start(f32[3,72,128]{2,1,0:T(8,128)} %get-tuple-element.30.east_own) | copy-start | bytes 331780
  20.7 14.4 %copy-start = (f32[4,72,128]{2,1,0:T(8,128)S(1)}, f32[4,72,128]{2,1,0:T(8,128)}, u32[]{:S(2)}) copy-start(f32[4,72,128]{2,1,0:T(8,128)} %get-tuple-element.27.up_own) | copy-start | bytes 442372
  20.7 14.4 %copy-start.1 = (f32[4,72,128]{2,1,0:T(8,128)S(1)}, f32[4,72,128]{2,1,0:T(8,128)}, u32[]{:S(2)}) copy-start(f32[4,72,128]{2,1,0:T(8,128)} %get-tuple-element.29.west_own) | copy-start | bytes 442372
  20.7 19.9 %copy-start.4 = (f32[72,72]{1,0:T(8,128)S(1)}, f32[72,72]{1,0:T(8,128)}, u32[]{:S(2)}) copy-start(f32[72,72]{1,0:T(8,128)} %param.11) | copy-start | bytes 62212
  20.8 32.5 %all-to-all-start = ((f32[128,24,128]{2,1,0:T(8,128)}), f32[128,24,128]{2,1,0:T(8,128)S(1)}, u32[]{:S(2)}, u32[]{:S(2)}) async-start(f32[128,24,128]{2,1,0:T(8,128)} %get-tuple-element.31), calls=%async_computation | async-start | bytes 3145728 | tf_op jit(solution)/shard_map/all_to_all | solution.py:680
  31.0 48.5 %collective-permute-start.1 = (f32[3,72,128]{2,1,0:T(8,128)S(1)}, f32[3,72,128]{2,1,0:T(8,128)S(1)}, u32[]{:S(2)}, u32[]{:S(2)}) collective-permute-start(f32[3,72,128]{2,1,0:T(8,128)S(1)} %copy-done.2), channel_id=1, source_target_pairs={{32,0},{64,32},{96,64},{0,96},{33,1},{65,33},{97,65},{1,97},{34,2}... | collective-permute-start | bytes 331784 | tf_op jit(solution)/shard_map/ppermute | solution.py:685
  34.4 45.1 %collective-permute-start.3 = (f32[3,72,128]{2,1,0:T(8,128)S(1)}, f32[3,72,128]{2,1,0:T(8,128)S(1)}, u32[]{:S(2)}, u32[]{:S(2)}) collective-permute-start(f32[3,72,128]{2,1,0:T(8,128)S(1)} %copy-done.3), channel_id=1, source_target_pairs={{1,0},{2,1},{3,2},{4,3},{5,4},{6,5},{7,6},{8,7},{9,8},{10,9},{11,1... | collective-permute-start | bytes 331784 | tf_op jit(solution)/shard_map/ppermute | solution.py:687
  35.1 44.4 %collective-permute-start = (f32[4,72,128]{2,1,0:T(8,128)S(1)}, f32[4,72,128]{2,1,0:T(8,128)S(1)}, u32[]{:S(2)}, u32[]{:S(2)}) collective-permute-start(f32[4,72,128]{2,1,0:T(8,128)S(1)} %copy-done), channel_id=1, source_target_pairs={{0,32},{32,64},{64,96},{96,0},{1,33},{33,65},{65,97},{97,1},{2,34}... | collective-permute-start | bytes 442376 | tf_op jit(solution)/shard_map/ppermute | solution.py:684
  35.2 44.4 %collective-permute-start.2 = (f32[4,72,128]{2,1,0:T(8,128)S(1)}, f32[4,72,128]{2,1,0:T(8,128)S(1)}, u32[]{:S(2)}, u32[]{:S(2)}) collective-permute-start(f32[4,72,128]{2,1,0:T(8,128)S(1)} %copy-done.1), channel_id=1, source_target_pairs={{0,1},{1,2},{2,3},{3,4},{4,5},{5,6},{6,7},{7,8},{8,9},{9,10},{10,1... | collective-permute-start | bytes 442376 | tf_op jit(solution)/shard_map/ppermute | solution.py:686
  40.9 10.3 %copy-start.5 = (s32[20]{0:T(128)S(1)}, s32[20]{0:T(128)}, u32[]{:S(2)}) copy-start(s32[20]{0:T(128)} %param.15) | copy-start | bytes 244
  80.0 6.8 %collective-permute-start.4 = (f32[3,72,128]{2,1,0:T(8,128)S(1)}, f32[3,72,128]{2,1,0:T(8,128)S(1)}, u32[]{:S(2)}, u32[]{:S(2)}) collective-permute-start(f32[3,72,128]{2,1,0:T(8,128)S(1)} %get-tuple-element.40), channel_id=1, source_target_pairs={{0,32},{32,64},{64,96},{96,0},{1,33},{33,65},{65,97},{97,1},{2,34}... | collective-permute-start | bytes 331784 | tf_op jit(solution)/shard_map/ppermute | solution.py:684
  80.1 6.7 %collective-permute-start.5 = (f32[3,72,128]{2,1,0:T(8,128)S(1)}, f32[3,72,128]{2,1,0:T(8,128)S(1)}, u32[]{:S(2)}, u32[]{:S(2)}) collective-permute-start(f32[3,72,128]{2,1,0:T(8,128)S(1)} %get-tuple-element.41), channel_id=1, source_target_pairs={{32,0},{64,32},{96,64},{0,96},{33,1},{65,33},{97,65},{1,97},{34,2}... | collective-permute-start | bytes 331784 | tf_op jit(solution)/shard_map/ppermute | solution.py:685
  83.3 5.8 %collective-permute-start.6 = (f32[3,72,128]{2,1,0:T(8,128)S(1)}, f32[3,72,128]{2,1,0:T(8,128)S(1)}, u32[]{:S(2)}, u32[]{:S(2)}) collective-permute-start(f32[3,72,128]{2,1,0:T(8,128)S(1)} %get-tuple-element.42), channel_id=1, source_target_pairs={{0,1},{1,2},{2,3},{3,4},{4,5},{5,6},{6,7},{7,8},{8,9},{9,10},{10,1... | collective-permute-start | bytes 331784 | tf_op jit(solution)/shard_map/ppermute | solution.py:686
  86.8 9.0 %collective-permute-start.7 = (f32[3,72,128]{2,1,0:T(8,128)S(1)}, f32[3,72,128]{2,1,0:T(8,128)S(1)}, u32[]{:S(2)}, u32[]{:S(2)}) collective-permute-start(f32[3,72,128]{2,1,0:T(8,128)S(1)} %get-tuple-element.43), channel_id=1, source_target_pairs={{1,0},{2,1},{3,2},{4,3},{5,4},{6,5},{7,6},{8,7},{9,8},{10,9},{11,1... | collective-permute-start | bytes 331784 | tf_op jit(solution)/shard_map/ppermute | solution.py:687

commit v8 on v7

--- a/solution.py
+++ b/solution.py
@@ -89,7 +89,6 @@
 
 
 PACK = (16, 8192)
-ADD = (17, 6144)
 
 
 def whole_part(value, divisor):
@@ -520,6 +519,11 @@
     group,
     middle,
     spot,
+    parts_b,
+    group_b,
+    middle_b,
+    spot_b,
+    bounds,
     sem_got,
     *,
     cols,
@@ -537,27 +541,28 @@
         copy.start()
     second = (lax.broadcasted_iota(jnp.int32, (TILE, WIDE), 0) >= TILE // 2).astype(f32)
     quarter_of = lax.broadcasted_iota(jnp.int32, (held, slots), 1) // (slots // 4)
-    length = sources * slots
+    length = sources * slots // 2
+    outer = length // 4
     halfway = half_segment(species * cols)
-
-    def put(row, at):
-        wide = row.shape[1]
-        at = pl.ds(pl.multiple_of(at, LANES), wide)
+    halves = ((parts, group, middle, spot), (parts_b, group_b, middle_b, spot_b))
+
+    def put(to, row, at):
+        to_parts, to_group, to_middle, to_spot = to
+        at = pl.ds(at if isinstance(at, int) else pl.multiple_of(at, LANES), WIDE)
         segment = row[akl : akl + 1].astype(jnp.int32) - 1
-        mark(spot, at, segment & (WIDE - 1))
-        pair = jnp.broadcast_to((segment >> 8).astype(f32), (TILE, wide))
-        group[:, at] = pair.astype(bf16)
-        middle[:, at] = (pair - second[:, :wide]).astype(bf16)
+        mark(to_spot, at, segment & (WIDE - 1))
+        pair = jnp.broadcast_to((segment >> 8).astype(f32), (TILE, WIDE))
+        to_group[:, at] = pair.astype(bf16)
+        to_middle[:, at] = (pair - second).astype(bf16)
         high, low = split(row[:akl])
         both = jnp.concatenate([high, low], axis=0)
-        parts[:, at] = jnp.concatenate([both, both], axis=0).astype(bf16)
+        to_parts[:, at] = jnp.concatenate([both, both], axis=0).astype(bf16)
         return segment
 
-    def prepare(g, carry):
-        highest, lowest = carry
+    def prepare(half, g):
         fours = []
         for b in range(2):
-            turned = [got[8 * g + 4 * b + k] for k in range(4)]
+            turned = [got[half * (sources // 2) + 8 * g + 4 * b + k] for k in range(4)]
             turned = [pltpu.roll(v, k * (slots // 4), 1) if k else v for k, v in enumerate(turned)]
             rows_of = []
             for q in range(4):
@@ -567,34 +572,58 @@
                 rows_of.append(row)
             fours.append(rows_of)
         row = [jnp.concatenate([fours[0][q], fours[1][q]], axis=1) for q in range(4)]
-        segment = put(row[0], g * WIDE)
-        highest = jnp.maximum(highest, segment)
-        put(row[1], length // 4 + 2 * g * WIDE)
-        put(row[2], length // 4 + (2 * g + 1) * WIDE)
-        segment = put(row[3], 3 * (length // 4) + g * WIDE)
-        lowest = jnp.minimum(lowest, jnp.where(segment < 0, 2 * halfway, segment))
-        return highest, lowest
-
-    carry = (jnp.full((1, WIDE), -1, jnp.int32), jnp.full((1, WIDE), 2 * halfway, jnp.int32))
+        to = halves[half]
+        segment = put(to, row[0], g * WIDE)
+        bounds[0:1] = jnp.maximum(bounds[0:1], segment)
+        put(to, row[1], outer + 2 * g * WIDE)
+        put(to, row[2], outer + (2 * g + 1) * WIDE)
+        segment = put(to, row[3], 3 * outer + g * WIDE)
+        bounds[1:2] = jnp.minimum(bounds[1:2], jnp.where(segment < 0, 2 * halfway, segment))
+
+    def prepare_one(g, carry):
+        prepare(0, g)
+        return carry
+
+    bounds[0:1] = jnp.full((1, WIDE), -1, jnp.int32)
+    bounds[1:2] = jnp.full((1, WIDE), 2 * halfway, jnp.int32)
+    steps = sources // 16
     for q, copy in enumerate(came):
         copy.wait()
-        carry = lax.fori_loop(q * quarter // 8, (q + 1) * quarter // 8, prepare, carry)
-    highest, lowest = jnp.max(carry[0]), jnp.min(carry[1])
+        if q < 2:
+            lax.fori_loop(q * steps // 2, (q + 1) * steps // 2, prepare_one, 0)
 
     tiles = ((0, 0), (0, 0), (1, 0), (0, 1), (0, 1))
     groups = total.shape[0] // (4 * akl)
     lower, higher = (0, groups // 2), (groups // 2, groups)
-    add = functools.partial(onehot_product, parts, [group, middle], tiles, spot, total)
-    add(lower, 2, *ADD, 0, 3 * (length // 4))
-    add(higher, 2, *ADD, length // 4, length)
+
+    def add(half, of, depth, begin, end, **how):
+        held_parts, held_group, held_middle, held_spot = halves[half]
+        onehot_product(
+            held_parts, [held_group, held_middle], tiles, held_spot, total, of, 2, groups // 2, depth, begin, end, **how
+        )
+
+    def beside(steps_now):
+        def run(_):
+            for g in steps_now:
+                prepare(1, g)
+
+        return run
+
+    add(0, lower, 3 * outer, 0, 3 * outer, beside=beside(range(steps // 2)))
+    add(0, higher, 3 * outer, outer, length, beside=beside(range(steps // 2, steps)))
+    add(1, lower, 3 * outer, 0, 3 * outer, onto=True)
+    add(1, higher, 3 * outer, outer, length, onto=True)
+    highest, lowest = jnp.max(bounds[0:1]), jnp.min(bounds[1:2])
 
     @pl.when(highest >= halfway)
     def _():
-        add(higher, 2, ADD[0], length // 8, 0, length // 4, onto=True)
+        for half in range(2):
+            add(half, higher, outer, 0, outer, onto=True)
 
     @pl.when(lowest < halfway)
     def _():
-        add(lower, 2, ADD[0], length // 8, 3 * (length // 4), length, onto=True)
+        for half in range(2):
+            add(half, lower, outer, 3 * outer, length, onto=True)
 
     t = table[...]
 
@@ -629,6 +658,7 @@
     akl = table.shape[1] // 4
     length = sources * slots
     pairs = -(-species * cols // 4)
+    halves = [pltpu.VMEM((rows_held, length // 2), bf16) for rows_held in (4 * akl, TILE, TILE, WIDE)]
     edge = jax.ShapeDtypeStruct((species, levels, rows), f32)
     vmem, hbm = pl.BlockSpec(memory_space=pltpu.VMEM), pl.BlockSpec(memory_space=pl.ANY)
     return pl.pallas_call(
@@ -638,10 +668,9 @@
         out_specs=(vmem,) * 5,
         scratch_shapes=(
             pltpu.VMEM(got.shape, f32),
-            pltpu.VMEM((4 * akl, length), bf16),
-            pltpu.VMEM((TILE, length), bf16),
-            pltpu.VMEM((TILE, length), bf16),
-            pltpu.VMEM((WIDE, length), bf16),
+            *halves,
+            *halves,
+            pltpu.VMEM((2, WIDE), jnp.int32),
             pltpu.SemaphoreType.DMA((4,)),
         ),
         compiler_params=pltpu.CompilerParams(vmem_limit_bytes=ADD_LIMIT),

time: 108 us -> 106 us (0.981)
  Pallas kernels: 68.7 us -> 67.4 us
    pallas_call x1, Pallas kernels: 26.2 us -> 24.9 us  [add_soundings(): pl.pallas_call(functools.partial(add_kernel, cols=cols), out_shape=(jax.S...]
  transfers between devices with their start and end apart: 9 -> 9, of which waited for: 3 -> 3; matrix products, arithmetic and copies ran while one was open for 0% -> 0% of each run, Pallas kernels for 34% -> 33%
where the time goes in v8:
time: 106 us
  Pallas kernels  67.4 us (64%)
  starting transfers between devices  26.6 us (25%)
  waiting for transfers between devices  10.9 us (10%)
    pallas_call x1, Pallas kernels, add_soundings(): pl.pallas_call(functools.partial(add_kernel, cols=cols), out_shape=(jax.S...  24.9 us
    pallas_call x2, Pallas kernels, step(): pl.pallas_call(functools.partial(step_kernel, names=(*given, 'out', *made...  22 us
    pallas_call x1, Pallas kernels, pack(): pl.pallas_call(pack_kernel, out_shape=tuple((jax.ShapeDtypeStruct(shape,...  20.1 us
    all_to_all x1, starting transfers between devices, on_device(): lax.all_to_all(sent, ('lat', 'lon'), split_axis=0, concat_axis=0, tiled=T...  10.2 us
    ppermute x2, starting transfers between devices, exchange(): lax.ppermute(west, 'lon', east_way)  8.97 us
    ppermute x2, waiting for transfers between devices, exchange(): lax.ppermute(east, 'lon', west_way)  6.64 us
    ppermute x2, starting transfers between devices, exchange(): lax.ppermute(down, 'lat', south_way)  6.57 us
    ppermute x2, waiting for transfers between devices, exchange(): lax.ppermute(west, 'lon', east_way)  2.32 us
  transfers between devices with their start and end apart: 9, of which 3 were waited for; matrix products, arithmetic and copies ran while one was open for 0% of the time, Pallas kernels for 33%

profile of v8, /device:TPU:30, one launch (start us, length us, event | category | flops | bytes accessed | tf_op | source)
XLA Modules:
  0.0 106.1 jit_solution(7871554468604867442)
XLA Ops:
  0.6 20.1 %shard_map.96 = (f32[128,24,128]{2,1,0:T(8,128)}, f32[4,72,128]{2,1,0:T(8,128)}, f32[3,72,128]{2,1,0:T(8,128)}, f32[4,72,128]{2,1,0:T(8,128)}, f32[3,72,128]{2,1,0:T(8,128)}) custom-call(s32[1,8192]{1,0:T(1,128)} %bitcast.23, f32[20,8192]{1,0:T(8,128)} %values.1, s32[1,8192]{1,0:T(1,128)} %bitcast.24, f32[3,45,72,128]{3,2,1,0:T(8,128)} %bitcast.10, ...), custom_call_target="tpu_custom_call" | custom-call | flops 12884901888 | bytes 7270400 | tf_op jit(solution)/shard_map/pallas_call | solution.py:204
  20.7 0.0 copy-start.2
  20.7 0.0 copy-start.3
  20.7 0.0 copy-start
  20.7 0.0 copy-start.1
  20.7 0.0 copy-start.4
  20.8 10.2 %all-to-all-start = ((f32[128,24,128]{2,1,0:T(8,128)}), f32[128,24,128]{2,1,0:T(8,128)S(1)}, u32[]{:S(2)}, u32[]{:S(2)}) async-start(f32[128,24,128]{2,1,0:T(8,128)} %get-tuple-element.31), calls=%async_computation | async-start | bytes 3145728 | tf_op jit(solution)/shard_map/all_to_all | solution.py:709
  31.0 0.0 copy-done.2
  31.0 3.3 %collective-permute-start.1 = (f32[3,72,128]{2,1,0:T(8,128)S(1)}, f32[3,72,128]{2,1,0:T(8,128)S(1)}, u32[]{:S(2)}, u32[]{:S(2)}) collective-permute-start(f32[3,72,128]{2,1,0:T(8,128)S(1)} %copy-done.2), channel_id=1, source_target_pairs={{32,0},{64,32},{96,64},{0,96},{33,1},{65,33},{97,65},{1,97},{34,2}... | collective-permute-start | bytes 331784 | tf_op jit(solution)/shard_map/ppermute | solution.py:714
  34.3 0.0 copy-done.3
  34.4 0.8 collective-permute-start.3
  35.1 0.0 copy-done
  35.1 0.0 collective-permute-start
  35.1 0.0 copy-done.1
  35.2 5.5 %collective-permute-start.2 = (f32[4,72,128]{2,1,0:T(8,128)S(1)}, f32[4,72,128]{2,1,0:T(8,128)S(1)}, u32[]{:S(2)}, u32[]{:S(2)}) collective-permute-start(f32[4,72,128]{2,1,0:T(8,128)S(1)} %copy-done.1), channel_id=1, source_target_pairs={{0,1},{1,2},{2,3},{3,4},{4,5},{5,6},{6,7},{7,8},{8,9},{9,10},{10,1... | collective-permute-start | bytes 442376 | tf_op jit(solution)/shard_map/ppermute | solution.py:715
  40.7 0.0 copy-done.4
  40.7 0.1 copy.10
  40.8 0.1 pad_maximum_fusion.refs_6_.weights
  40.9 0.0 copy-start.5
  40.9 10.3 %shard_map.95 = (f32[3,45,72,128]{3,2,1,0:T(8,128)}, f32[3,72,128]{2,1,0:T(8,128)S(1)}, f32[3,72,128]{2,1,0:T(8,128)S(1)}, f32[3,72,128]{2,1,0:T(8,128)S(1)}, f32[3,72,128]{2,1,0:T(8,128)S(1)}) custom-call(f32[3,45,72,128]{3,2,1,0:T(8,128)} %bitcast.11, f32[3,45,72,128]{3,2,1,0:T(8,128)} %bitcast.12, f32[3,45,72,128]{3,2,1,0:T(8,128)} %bitcast.13, ...), custom_call_target="tpu_custom_call" | custom-call | flops 537477120 | bytes 14929920 | tf_op jit(solution)/shard_map/pallas_call | solution.py:492
  51.2 0.0 copy-done.5
  51.2 0.1 add_convert_fusion.table.refs_15_
  51.3 2.0 %all-to-all-done.got_at = f32[128,24,128]{2,1,0:T(8,128)S(1)} async-done(((f32[128,24,128]{2,1,0:T(8,128)}), f32[128,24,128]{2,1,0:T(8,128)S(1)}, u32[]{:S(2)}, u32[]{:S(2)}) %all-to-all-start) | async-done | bytes 1572896 | tf_op jit(solution)/shard_map/all_to_all | solution.py:709
  53.2 24.9 %shard_map.97 = (f32[2720,256]{1,0:T(8,128)}, f32[3,72,128]{2,1,0:T(8,128)S(1)}, f32[3,72,128]{2,1,0:T(8,128)S(1)}, f32[3,72,128]{2,1,0:T(8,128)S(1)}, f32[3,72,128]{2,1,0:T(8,128)S(1)}) custom-call(f32[128,24,128]{2,1,0:T(8,128)S(1)} %all-to-all-done.got_at, f32[3,72,128]{2,1,0:T(8,128)S(1)} %get-tuple-element.32.plain_up, ...), custom_call_target="tpu_custom_call" | custom-call | flops 22817013760 | bytes 1572864 | tf_op jit(solution)/shard_map/pallas_call | solution.py:664
  78.1 0.0 collective-permute-done.1.north
  78.1 0.0 collective-permute-done.3.east
  78.1 0.0 collective-permute-done.south.refs_13_
  78.2 0.0 collective-permute-done.2.west.refs_12_
  78.2 0.5 shard_map.98
  78.6 0.1 collective-permute-start.4
  78.7 3.2 %collective-permute-start.5 = (f32[3,72,128]{2,1,0:T(8,128)S(1)}, f32[3,72,128]{2,1,0:T(8,128)S(1)}, u32[]{:S(2)}, u32[]{:S(2)}) collective-permute-start(f32[3,72,128]{2,1,0:T(8,128)S(1)} %get-tuple-element.41), channel_id=1, source_target_pairs={{32,0},{64,32},{96,64},{0,96},{33,1},{65,33},{97,65},{1,97},{34,2}... | collective-permute-start | bytes 331784 | tf_op jit(solution)/shard_map/ppermute | solution.py:714
  82.0 3.4 %collective-permute-start.6 = (f32[3,72,128]{2,1,0:T(8,128)S(1)}, f32[3,72,128]{2,1,0:T(8,128)S(1)}, u32[]{:S(2)}, u32[]{:S(2)}) collective-permute-start(f32[3,72,128]{2,1,0:T(8,128)S(1)} %get-tuple-element.42), channel_id=1, source_target_pairs={{0,1},{1,2},{2,3},{3,4},{4,5},{5,6},{6,7},{7,8},{8,9},{9,10},{10,1... | collective-permute-start | bytes 331784 | tf_op jit(solution)/shard_map/ppermute | solution.py:715
  85.4 0.0 collective-permute-start.7
  85.4 0.0 collective-permute-done.4.refs_8_
  85.4 0.0 collective-permute-done.5.refs_9_
  85.4 2.3 %collective-permute-done.6.refs_10_ = f32[3,72,128]{2,1,0:T(8,128)S(1)} collective-permute-done((f32[3,72,128]{2,1,0:T(8,128)S(1)}, f32[3,72,128]{2,1,0:T(8,128)S(1)}, u32[]{:S(2)}, u32[]{:S(2)}) %collective-permute-start.6) | collective-permute-done | bytes 110624 | tf_op jit(solution)/shard_map/ppermute | solution.py:715
  87.7 6.6 %collective-permute-done.7.refs_11_ = f32[3,72,128]{2,1,0:T(8,128)S(1)} collective-permute-done((f32[3,72,128]{2,1,0:T(8,128)S(1)}, f32[3,72,128]{2,1,0:T(8,128)S(1)}, u32[]{:S(2)}, u32[]{:S(2)}) %collective-permute-start.7) | collective-permute-done | bytes 110624 | tf_op jit(solution)/shard_map/ppermute | solution.py:716
  94.4 11.7 %shard_map.99 = (f32[3,45,72,128]{3,2,1,0:T(8,128)}, f32[3,45,128]{2,1,0:T(8,128)}) custom-call(f32[3,45,72,128]{3,2,1,0:T(8,128)} %get-tuple-element.26.refs_0_.refs_1_.refs_2_, f32[3,45,72,128]{3,2,1,0:T(8,128)} %get-tuple-element.26.refs_0_.refs_1_.refs_2_, f32[3,45,72,128]{3,2,1,0:T(8,128)} %get-tuple-element.26.refs_0_.refs_1_.refs_2_, ...), custom_call_target="tpu_custom_call" | custom-call | flops 537477120 | bytes 14929920 | tf_op jit(solution)/shard_map/pallas_call | solution.py:492
  (2 shorter events, 0.0 us)
Async XLA Ops:
  20.7 10.3 %copy-start.2 = (f32[3,72,128]{2,1,0:T(8,128)S(1)}, f32[3,72,128]{2,1,0:T(8,128)}, u32[]{:S(2)}) copy-start(f32[3,72,128]{2,1,0:T(8,128)} %get-tuple-element.28.down_own) | copy-start | bytes 331780
  20.7 13.6 %copy-start.3 = (f32[3,72,128]{2,1,0:T(8,128)S(1)}, f32[3,72,128]{2,1,0:T(8,128)}, u32[]{:S(2)}) copy-start(f32[3,72,128]{2,1,0:T(8,128)} %get-tuple-element.30.east_own) | copy-start | bytes 331780
  20.7 14.4 %copy-start = (f32[4,72,128]{2,1,0:T(8,128)S(1)}, f32[4,72,128]{2,1,0:T(8,128)}, u32[]{:S(2)}) copy-start(f32[4,72,128]{2,1,0:T(8,128)} %get-tuple-element.27.up_own) | copy-start | bytes 442372
  20.7 14.4 %copy-start.1 = (f32[4,72,128]{2,1,0:T(8,128)S(1)}, f32[4,72,128]{2,1,0:T(8,128)}, u32[]{:S(2)}) copy-start(f32[4,72,128]{2,1,0:T(8,128)} %get-tuple-element.29.west_own) | copy-start | bytes 442372
  20.7 19.9 %copy-start.4 = (f32[72,72]{1,0:T(8,128)S(1)}, f32[72,72]{1,0:T(8,128)}, u32[]{:S(2)}) copy-start(f32[72,72]{1,0:T(8,128)} %param.11) | copy-start | bytes 62212
  20.8 32.5 %all-to-all-start = ((f32[128,24,128]{2,1,0:T(8,128)}), f32[128,24,128]{2,1,0:T(8,128)S(1)}, u32[]{:S(2)}, u32[]{:S(2)}) async-start(f32[128,24,128]{2,1,0:T(8,128)} %get-tuple-element.31), calls=%async_computation | async-start | bytes 3145728 | tf_op jit(solution)/shard_map/all_to_all | solution.py:709
  31.0 47.1 %collective-permute-start.1 = (f32[3,72,128]{2,1,0:T(8,128)S(1)}, f32[3,72,128]{2,1,0:T(8,128)S(1)}, u32[]{:S(2)}, u32[]{:S(2)}) collective-permute-start(f32[3,72,128]{2,1,0:T(8,128)S(1)} %copy-done.2), channel_id=1, source_target_pairs={{32,0},{64,32},{96,64},{0,96},{33,1},{65,33},{97,65},{1,97},{34,2}... | collective-permute-start | bytes 331784 | tf_op jit(solution)/shard_map/ppermute | solution.py:714
  34.4 43.8 %collective-permute-start.3 = (f32[3,72,128]{2,1,0:T(8,128)S(1)}, f32[3,72,128]{2,1,0:T(8,128)S(1)}, u32[]{:S(2)}, u32[]{:S(2)}) collective-permute-start(f32[3,72,128]{2,1,0:T(8,128)S(1)} %copy-done.3), channel_id=1, source_target_pairs={{1,0},{2,1},{3,2},{4,3},{5,4},{6,5},{7,6},{8,7},{9,8},{10,9},{11,1... | collective-permute-start | bytes 331784 | tf_op jit(solution)/shard_map/ppermute | solution.py:716
  35.1 43.0 %collective-permute-start = (f32[4,72,128]{2,1,0:T(8,128)S(1)}, f32[4,72,128]{2,1,0:T(8,128)S(1)}, u32[]{:S(2)}, u32[]{:S(2)}) collective-permute-start(f32[4,72,128]{2,1,0:T(8,128)S(1)} %copy-done), channel_id=1, source_target_pairs={{0,32},{32,64},{64,96},{96,0},{1,33},{33,65},{65,97},{97,1},{2,34}... | collective-permute-start | bytes 442376 | tf_op jit(solution)/shard_map/ppermute | solution.py:713
  35.2 43.0 %collective-permute-start.2 = (f32[4,72,128]{2,1,0:T(8,128)S(1)}, f32[4,72,128]{2,1,0:T(8,128)S(1)}, u32[]{:S(2)}, u32[]{:S(2)}) collective-permute-start(f32[4,72,128]{2,1,0:T(8,128)S(1)} %copy-done.1), channel_id=1, source_target_pairs={{0,1},{1,2},{2,3},{3,4},{4,5},{5,6},{6,7},{7,8},{8,9},{9,10},{10,1... | collective-permute-start | bytes 442376 | tf_op jit(solution)/shard_map/ppermute | solution.py:715
  40.9 10.3 %copy-start.5 = (s32[20]{0:T(128)S(1)}, s32[20]{0:T(128)}, u32[]{:S(2)}) copy-start(s32[20]{0:T(128)} %param.15) | copy-start | bytes 244
  78.6 6.8 %collective-permute-start.4 = (f32[3,72,128]{2,1,0:T(8,128)S(1)}, f32[3,72,128]{2,1,0:T(8,128)S(1)}, u32[]{:S(2)}, u32[]{:S(2)}) collective-permute-start(f32[3,72,128]{2,1,0:T(8,128)S(1)} %get-tuple-element.40), channel_id=1, source_target_pairs={{0,32},{32,64},{64,96},{96,0},{1,33},{33,65},{65,97},{97,1},{2,34}... | collective-permute-start | bytes 331784 | tf_op jit(solution)/shard_map/ppermute | solution.py:713
  78.7 6.7 %collective-permute-start.5 = (f32[3,72,128]{2,1,0:T(8,128)S(1)}, f32[3,72,128]{2,1,0:T(8,128)S(1)}, u32[]{:S(2)}, u32[]{:S(2)}) collective-permute-start(f32[3,72,128]{2,1,0:T(8,128)S(1)} %get-tuple-element.41), channel_id=1, source_target_pairs={{32,0},{64,32},{96,64},{0,96},{33,1},{65,33},{97,65},{1,97},{34,2}... | collective-permute-start | bytes 331784 | tf_op jit(solution)/shard_map/ppermute | solution.py:714
  82.0 5.8 %collective-permute-start.6 = (f32[3,72,128]{2,1,0:T(8,128)S(1)}, f32[3,72,128]{2,1,0:T(8,128)S(1)}, u32[]{:S(2)}, u32[]{:S(2)}) collective-permute-start(f32[3,72,128]{2,1,0:T(8,128)S(1)} %get-tuple-element.42), channel_id=1, source_target_pairs={{0,1},{1,2},{2,3},{3,4},{4,5},{5,6},{6,7},{7,8},{8,9},{9,10},{10,1... | collective-permute-start | bytes 331784 | tf_op jit(solution)/shard_map/ppermute | solution.py:715
  85.4 9.0 %collective-permute-start.7 = (f32[3,72,128]{2,1,0:T(8,128)S(1)}, f32[3,72,128]{2,1,0:T(8,128)S(1)}, u32[]{:S(2)}, u32[]{:S(2)}) collective-permute-start(f32[3,72,128]{2,1,0:T(8,128)S(1)} %get-tuple-element.43), channel_id=1, source_target_pairs={{1,0},{2,1},{3,2},{4,3},{5,4},{6,5},{7,6},{8,7},{9,8},{10,9},{11,1... | collective-permute-start | bytes 331784 | tf_op jit(solution)/shard_map/ppermute | solution.py:716

commit v9 on v8

--- a/solution.py
+++ b/solution.py
@@ -73,6 +73,28 @@
         spot[TILE * q : TILE * (q + 1), at] = jnp.where(row - jnp.asarray(TILE * q, bf16) == base, one, none)
 
 
+def turn(v, by):
+    return pltpu.roll(v, by % v.shape[1], 1)
+
+
+def is_even(shape):
+    return lax.broadcasted_iota(jnp.int32, shape, 1) % 2 == 0
+
+
+def interleave(values, to, first_even):
+    even = is_even(values[0].shape)
+    mine = even if first_even else jnp.logical_not(even)
+    for k in range(0, len(values), 2):
+        both = values[k]
+        if k + 1 < len(values):
+            both = jnp.where(mine, both, turn(values[k + 1], 1 if first_even else -1))
+        to[k // 2] = both
+
+
+def apart(held, s, first_even):
+    return held[s // 2] if s % 2 == 0 else turn(held[s // 2], -1 if first_even else 1)
+
+
 def edge_lanes(columns, kept, first, up, share=None):
     rows = kept.shape[1]
     lane = lax.broadcasted_iota(jnp.int32, kept.shape, 1)
@@ -107,8 +129,8 @@
     clon_at,
     clat_at,
     out,
-    up,
-    down,
+    up_sent,
+    down_sent,
     west,
     east,
     parts,
@@ -117,6 +139,8 @@
     total,
     field,
     clat,
+    up,
+    down,
     sems,
 ):
     n_tiles, held, _ = out.shape
@@ -182,6 +206,8 @@
     onehot_product(
         parts, [group], tiles, spot, total, (0, n_tiles // 2), 1, *PACK, 0, length, beside=take_edges
     )
+    interleave([up[s] for s in range(species + 1)], up_sent, True)
+    interleave([down[s] for s in range(species)], down_sent, False)
 
     def put(g, carry):
         for i in range(4):
@@ -200,11 +226,12 @@
     species, cols, depth, rows = field.shape
     held = -(-(levels + 1) // 8) * 8
     four, three = (species + 1, depth, rows), (species, depth, rows)
+    up, down = ((species + 2) // 2, depth, rows), ((species + 1) // 2, depth, rows)
     vmem, hbm = pl.BlockSpec(memory_space=pltpu.VMEM), pl.BlockSpec(memory_space=pl.ANY)
     return pl.pallas_call(
         pack_kernel,
         out_shape=tuple(
-            jax.ShapeDtypeStruct(shape, f32) for shape in ((n_tiles, held, LANES), four, three, four, three)
+            jax.ShapeDtypeStruct(shape, f32) for shape in ((n_tiles, held, LANES), up, down, four, three)
         ),
         in_specs=[vmem, vmem, vmem, hbm, hbm, hbm],
         out_specs=(vmem,) * 5,
@@ -215,6 +242,8 @@
             pltpu.VMEM((n_tiles // 2 * 2 * held, WIDE), f32),
             pltpu.VMEM(field.shape, f32),
             pltpu.VMEM(clat.shape, f32),
+            pltpu.VMEM(four, f32),
+            pltpu.VMEM(three, f32),
             pltpu.SemaphoreType.DMA((3 + 2 * species,)),
         ),
         compiler_params=pltpu.CompilerParams(vmem_limit_bytes=PACK_LIMIT),
@@ -253,14 +282,17 @@
         lat = ref["lat"][0]
         below = jnp.where(jnp.logical_and(first, lat == 0), 0.0, 1.0)
         inside = jnp.where(jnp.logical_and(last, lat == lat_size - 1), 0.0, 1.0)
-        turn = lax.rem(rows - 2 * start, rows)
+        back_to_start = lax.rem(rows - 2 * start, rows)
         even = lane % 2 == 0
         ends = jnp.logical_or(first, last)
         halos = [
-            pltpu.roll(jnp.where(even, ref["south"][s], ref["north"][s]), turn, 1) for s in range(species)
+            pltpu.roll(
+                jnp.where(even, apart(ref["south"], s, True), apart(ref["north"], s, False)), back_to_start, 1
+            )
+            for s in range(species)
         ]
-        left_out = [pltpu.roll(ref["lanes"][s], turn, 1) for s in range(species)]
-        courant_south = pltpu.roll(ref["clat_south"][0], turn, 1)
+        left_out = [pltpu.roll(ref["lanes"][s], back_to_start, 1) for s in range(species)]
+        courant_south = pltpu.roll(apart(ref["clat_south"], species, True), back_to_start, 1)
         t = ref["table"][...]
         cols = pl.num_programs(0) * block
         wanted = []
@@ -408,24 +440,27 @@
     def sooner(v):
         return pltpu.roll(v, rows - 1, 1)
 
-    n = (jnp.maximum(sooner(up_own[species]), 0.0) + kappa_mix) * inside
-    s_ = (kappa_mix - jnp.minimum(south[species], 0.0)) * below
+    ups, downs = [], []
+    n = (jnp.maximum(sooner(apart(up_own, species, True)), 0.0) + kappa_mix) * inside
+    s_ = (kappa_mix - jnp.minimum(apart(south, species, True), 0.0)) * below
     w_ = kappa_mix - jnp.minimum(west[species], 0.0)
     e = jnp.maximum(west_own[species], 0.0) + kappa_mix
     w = weights[...]
     for s in range(species):
-        rim = jnp.where(even, s_ * (south[s] - later(down_own[s])), n * (north[s] - sooner(up_own[s])))
+        from_south = s_ * (apart(south, s, True) - later(apart(down_own, s, False)))
+        from_north = n * (apart(north, s, False) - sooner(apart(up_own, s, True)))
+        rim = jnp.where(even, from_south, from_north)
         terms = [rim, w_ * (west[s] - east_own[s]), e * (east[s] - west_own[s])]
         mixed = jnp.dot(w, jnp.concatenate([mix_parts(h) for h in terms], axis=1), preferred_element_type=f32)
         c, c_start, c_end = [mixed[:, k * rows : (k + 1) * rows] for k in range(3)]
         lanes[s], column_start[s], column_end[s] = c, c_start, c_end
-        up[s] = (
+        ups.append(
             up_in[s]
             + jnp.where(even, later(c), 0.0)
             + jnp.where(lane == 0, later(c_start), 0.0)
             + jnp.where(lane == far, pltpu.roll(c_end, far + 1, 1), 0.0)
         )
-        down[s] = (
+        downs.append(
             down_in[s]
             + jnp.where(even, 0.0, sooner(c))
             + jnp.where(lane == rows - 1, sooner(c_start), 0.0)
@@ -433,6 +468,8 @@
         )
         west_out[s] = west_in[s] + c_end + jnp.where(ends, pltpu.roll(c, rows - far, 1), 0.0)
         east_out[s] = east_in[s] + c_start + jnp.where(ends, c, 0.0)
+    interleave(ups, up, True)
+    interleave(downs, down, False)
 
 
 def left_out(lat, own, halo, weights, edges, cols, lat_size):
@@ -440,7 +477,7 @@
     vmem = pl.BlockSpec(memory_space=pltpu.VMEM)
     return pl.pallas_call(
         functools.partial(left_out_kernel, cols=cols, lat_size=lat_size),
-        out_shape=(shape,) * 7,
+        out_shape=(jax.ShapeDtypeStruct(((len(edges[0]) + 1) // 2, *shape.shape[1:]), f32),) * 2 + (shape,) * 5,
         in_specs=[pl.BlockSpec(memory_space=pltpu.SMEM)] + [vmem] * 13,
         out_specs=(vmem,) * 7,
         compiler_params=pltpu.CompilerParams(vmem_limit_bytes=SMALL_LIMIT),
@@ -486,7 +523,7 @@
             spec = whole(value.shape)
             if name == "lat":
                 spec = pl.BlockSpec(memory_space=pltpu.SMEM)
-            elif name in ("clon_col", "clat_south"):
+            elif name == "clon_col":
                 spec = part(species)
             given[name] = (value, spec)
     return pl.pallas_call(

time: 106 us -> 108 us (1.019)
  the two profiles are of different devices: /device:TPU:30 before, /device:TPU:1 now
where the time goes in v9:
time: 108 us
  Pallas kernels  67.7 us (63%)
  starting transfers between devices  28.7 us (27%)
  waiting for transfers between devices  10 us (9%)
    pallas_call x1, Pallas kernels, add_soundings(): pl.pallas_call(functools.partial(add_kernel, cols=cols), out_shape=(jax.S...  24.9 us
    pallas_call x2, Pallas kernels, step(): pl.pallas_call(functools.partial(step_kernel, names=(*given, 'out', *made...  22.2 us
    pallas_call x1, Pallas kernels, pack(): pl.pallas_call(pack_kernel, out_shape=tuple((jax.ShapeDtypeStruct(shape,...  20.1 us
    all_to_all x1, starting transfers between devices, on_device(): lax.all_to_all(sent, ('lat', 'lon'), split_axis=0, concat_axis=0, tiled=T...  11.5 us
    ppermute x2, starting transfers between devices, exchange(): lax.ppermute(east, 'lon', west_way)  10.2 us
    ppermute x2, starting transfers between devices, exchange(): lax.ppermute(up, 'lat', north_way)  6.37 us
    all_to_all x1, waiting for transfers between devices, on_device(): lax.all_to_all(sent, ('lat', 'lon'), split_axis=0, concat_axis=0, tiled=T...  4.7 us
    ppermute x2, waiting for transfers between devices, exchange(): lax.ppermute(down, 'lat', south_way)  3.88 us
  transfers between devices with their start and end apart: 9, of which 3 were waited for; matrix products, arithmetic and copies ran while one was open for 0% of the time, Pallas kernels for 33%

profile of v9, /device:TPU:1, one launch (start us, length us, event | category | flops | bytes accessed | tf_op | source)
XLA Modules:
  0.0 107.5 jit_solution(11505062791861628446)
XLA Ops:
  0.6 20.1 %shard_map.96 = (f32[128,24,128]{2,1,0:T(8,128)}, f32[2,72,128]{2,1,0:T(8,128)}, f32[2,72,128]{2,1,0:T(8,128)}, f32[4,72,128]{2,1,0:T(8,128)}, f32[3,72,128]{2,1,0:T(8,128)}) custom-call(s32[1,8192]{1,0:T(1,128)} %bitcast.23, f32[20,8192]{1,0:T(8,128)} %values.1, s32[1,8192]{1,0:T(1,128)} %bitcast.24, f32[3,45,72,128]{3,2,1,0:T(8,128)} %bitcast.10, ...), custom_call_target="tpu_custom_call" | custom-call | flops 12884901888 | bytes 7270400 | tf_op jit(solution)/shard_map/pallas_call | solution.py:231
  20.7 0.0 copy-start.2
  20.7 0.0 copy-start.3
  20.7 0.0 copy-start.1
  20.7 0.0 copy-start
  20.7 0.0 copy-start.4
  20.8 11.5 %all-to-all-start = ((f32[128,24,128]{2,1,0:T(8,128)}), f32[128,24,128]{2,1,0:T(8,128)S(1)}, u32[]{:S(2)}, u32[]{:S(2)}) async-start(f32[128,24,128]{2,1,0:T(8,128)} %get-tuple-element.31), calls=%async_computation | async-start | bytes 3145728 | tf_op jit(solution)/shard_map/all_to_all | solution.py:746
  32.3 0.0 copy-done.2
  32.3 3.6 %collective-permute-start = (f32[2,72,128]{2,1,0:T(8,128)S(1)}, f32[2,72,128]{2,1,0:T(8,128)S(1)}, u32[]{:S(2)}, u32[]{:S(2)}) collective-permute-start(f32[2,72,128]{2,1,0:T(8,128)S(1)} %copy-done.2), channel_id=1, source_target_pairs={{0,32},{32,64},{64,96},{96,0},{1,33},{33,65},{65,97},{97,1},{2,34}... | collective-permute-start | bytes 221192 | tf_op jit(solution)/shard_map/ppermute | solution.py:750
  35.9 0.0 copy-done.3
  35.9 0.0 collective-permute-start.1
  35.9 0.0 copy-done.1
  35.9 5.1 %collective-permute-start.3 = (f32[3,72,128]{2,1,0:T(8,128)S(1)}, f32[3,72,128]{2,1,0:T(8,128)S(1)}, u32[]{:S(2)}, u32[]{:S(2)}) collective-permute-start(f32[3,72,128]{2,1,0:T(8,128)S(1)} %copy-done.1), channel_id=1, source_target_pairs={{1,0},{2,1},{3,2},{4,3},{5,4},{6,5},{7,6},{8,7},{9,8},{10,9},{11,1... | collective-permute-start | bytes 331784 | tf_op jit(solution)/shard_map/ppermute | solution.py:753
  41.0 0.0 copy-done
  41.0 0.0 collective-permute-start.2
  41.0 0.0 copy-done.4
  41.0 0.1 copy.10
  41.1 0.1 pad_maximum_fusion.refs_6_.weights
  41.2 0.0 copy-start.5
  41.2 10.2 %shard_map.95 = (f32[3,45,72,128]{3,2,1,0:T(8,128)}, f32[3,72,128]{2,1,0:T(8,128)S(1)}, f32[3,72,128]{2,1,0:T(8,128)S(1)}, f32[3,72,128]{2,1,0:T(8,128)S(1)}, f32[3,72,128]{2,1,0:T(8,128)S(1)}) custom-call(f32[3,45,72,128]{3,2,1,0:T(8,128)} %bitcast.11, f32[3,45,72,128]{3,2,1,0:T(8,128)} %bitcast.12, f32[3,45,72,128]{3,2,1,0:T(8,128)} %bitcast.13, ...), custom_call_target="tpu_custom_call" | custom-call | flops 537477120 | bytes 14929920 | tf_op jit(solution)/shard_map/pallas_call | solution.py:529
  51.4 0.0 copy-done.5
  51.5 0.1 add_convert_fusion.table.refs_15_
  51.6 4.7 %all-to-all-done.got_at = f32[128,24,128]{2,1,0:T(8,128)S(1)} async-done(((f32[128,24,128]{2,1,0:T(8,128)}), f32[128,24,128]{2,1,0:T(8,128)S(1)}, u32[]{:S(2)}, u32[]{:S(2)}) %all-to-all-start) | async-done | bytes 1572896 | tf_op jit(solution)/shard_map/all_to_all | solution.py:746
  56.3 24.9 %shard_map.97 = (f32[2720,256]{1,0:T(8,128)}, f32[3,72,128]{2,1,0:T(8,128)S(1)}, f32[3,72,128]{2,1,0:T(8,128)S(1)}, f32[3,72,128]{2,1,0:T(8,128)S(1)}, f32[3,72,128]{2,1,0:T(8,128)S(1)}) custom-call(f32[128,24,128]{2,1,0:T(8,128)S(1)} %all-to-all-done.got_at, f32[3,72,128]{2,1,0:T(8,128)S(1)} %get-tuple-element.32.plain_up, ...), custom_call_target="tpu_custom_call" | custom-call | flops 22817013760 | bytes 1572864 | tf_op jit(solution)/shard_map/pallas_call | solution.py:701
  81.1 0.0 collective-permute-done.south.refs_13_
  81.2 0.0 collective-permute-done.1.north
  81.2 0.0 collective-permute-done.3.east
  81.2 0.0 collective-permute-done.2.west.refs_12_
  81.2 0.6 shard_map.98
  81.7 0.6 collective-permute-start.6
  82.4 5.1 %collective-permute-start.7 = (f32[3,72,128]{2,1,0:T(8,128)S(1)}, f32[3,72,128]{2,1,0:T(8,128)S(1)}, u32[]{:S(2)}, u32[]{:S(2)}) collective-permute-start(f32[3,72,128]{2,1,0:T(8,128)S(1)} %get-tuple-element.43), channel_id=1, source_target_pairs={{1,0},{2,1},{3,2},{4,3},{5,4},{6,5},{7,6},{8,7},{9,8},{10,9},{11,1... | collective-permute-start | bytes 331784 | tf_op jit(solution)/shard_map/ppermute | solution.py:753
  87.5 2.8 %collective-permute-start.4 = (f32[2,72,128]{2,1,0:T(8,128)S(1)}, f32[2,72,128]{2,1,0:T(8,128)S(1)}, u32[]{:S(2)}, u32[]{:S(2)}) collective-permute-start(f32[2,72,128]{2,1,0:T(8,128)S(1)} %get-tuple-element.40), channel_id=1, source_target_pairs={{0,32},{32,64},{64,96},{96,0},{1,33},{33,65},{65,97},{97,1},{2,34}... | collective-permute-start | bytes 221192 | tf_op jit(solution)/shard_map/ppermute | solution.py:750
  90.3 0.0 collective-permute-start.5
  90.3 1.4 %collective-permute-done.4.refs_8_ = f32[2,72,128]{2,1,0:T(8,128)S(1)} collective-permute-done((f32[2,72,128]{2,1,0:T(8,128)S(1)}, f32[2,72,128]{2,1,0:T(8,128)S(1)}, u32[]{:S(2)}, u32[]{:S(2)}) %collective-permute-start.4) | collective-permute-done | bytes 73760 | tf_op jit(solution)/shard_map/ppermute | solution.py:750
  91.7 3.9 %collective-permute-done.5.refs_9_ = f32[2,72,128]{2,1,0:T(8,128)S(1)} collective-permute-done((f32[2,72,128]{2,1,0:T(8,128)S(1)}, f32[2,72,128]{2,1,0:T(8,128)S(1)}, u32[]{:S(2)}, u32[]{:S(2)}) %collective-permute-start.5) | collective-permute-done | bytes 73760 | tf_op jit(solution)/shard_map/ppermute | solution.py:751
  95.6 0.0 collective-permute-done.6.refs_10_
  95.6 0.0 collective-permute-done.7.refs_11_
  95.6 12.0 %shard_map.99 = (f32[3,45,72,128]{3,2,1,0:T(8,128)}, f32[3,45,128]{2,1,0:T(8,128)}) custom-call(f32[3,45,72,128]{3,2,1,0:T(8,128)} %get-tuple-element.26.refs_0_.refs_1_.refs_2_, f32[3,45,72,128]{3,2,1,0:T(8,128)} %get-tuple-element.26.refs_0_.refs_1_.refs_2_, f32[3,45,72,128]{3,2,1,0:T(8,128)} %get-tuple-element.26.refs_0_.refs_1_.refs_2_, ...), custom_call_target="tpu_custom_call" | custom-call | flops 537477120 | bytes 14929920 | tf_op jit(solution)/shard_map/pallas_call | solution.py:529
  (2 shorter events, 0.0 us)
Async XLA Ops:
  20.7 11.6 %copy-start.2 = (f32[2,72,128]{2,1,0:T(8,128)S(1)}, f32[2,72,128]{2,1,0:T(8,128)}, u32[]{:S(2)}) copy-start(f32[2,72,128]{2,1,0:T(8,128)} %get-tuple-element.27.up_own) | copy-start | bytes 221188
  20.7 15.2 %copy-start.3 = (f32[2,72,128]{2,1,0:T(8,128)S(1)}, f32[2,72,128]{2,1,0:T(8,128)}, u32[]{:S(2)}) copy-start(f32[2,72,128]{2,1,0:T(8,128)} %get-tuple-element.28.down_own) | copy-start | bytes 221188
  20.7 15.2 %copy-start.1 = (f32[3,72,128]{2,1,0:T(8,128)S(1)}, f32[3,72,128]{2,1,0:T(8,128)}, u32[]{:S(2)}) copy-start(f32[3,72,128]{2,1,0:T(8,128)} %get-tuple-element.30.east_own) | copy-start | bytes 331780
  20.7 20.2 %copy-start = (f32[4,72,128]{2,1,0:T(8,128)S(1)}, f32[4,72,128]{2,1,0:T(8,128)}, u32[]{:S(2)}) copy-start(f32[4,72,128]{2,1,0:T(8,128)} %get-tuple-element.29.west_own) | copy-start | bytes 442372
  20.7 20.2 %copy-start.4 = (f32[72,72]{1,0:T(8,128)S(1)}, f32[72,72]{1,0:T(8,128)}, u32[]{:S(2)}) copy-start(f32[72,72]{1,0:T(8,128)} %param.11) | copy-start | bytes 62212
  20.8 35.5 %all-to-all-start = ((f32[128,24,128]{2,1,0:T(8,128)}), f32[128,24,128]{2,1,0:T(8,128)S(1)}, u32[]{:S(2)}, u32[]{:S(2)}) async-start(f32[128,24,128]{2,1,0:T(8,128)} %get-tuple-element.31), calls=%async_computation | async-start | bytes 3145728 | tf_op jit(solution)/shard_map/all_to_all | solution.py:746
  32.3 48.9 %collective-permute-start = (f32[2,72,128]{2,1,0:T(8,128)S(1)}, f32[2,72,128]{2,1,0:T(8,128)S(1)}, u32[]{:S(2)}, u32[]{:S(2)}) collective-permute-start(f32[2,72,128]{2,1,0:T(8,128)S(1)} %copy-done.2), channel_id=1, source_target_pairs={{0,32},{32,64},{64,96},{96,0},{1,33},{33,65},{65,97},{97,1},{2,34}... | collective-permute-start | bytes 221192 | tf_op jit(solution)/shard_map/ppermute | solution.py:750
  35.9 45.3 %collective-permute-start.1 = (f32[2,72,128]{2,1,0:T(8,128)S(1)}, f32[2,72,128]{2,1,0:T(8,128)S(1)}, u32[]{:S(2)}, u32[]{:S(2)}) collective-permute-start(f32[2,72,128]{2,1,0:T(8,128)S(1)} %copy-done.3), channel_id=1, source_target_pairs={{32,0},{64,32},{96,64},{0,96},{33,1},{65,33},{97,65},{1,97},{34,2}... | collective-permute-start | bytes 221192 | tf_op jit(solution)/shard_map/ppermute | solution.py:751
  35.9 45.3 %collective-permute-start.3 = (f32[3,72,128]{2,1,0:T(8,128)S(1)}, f32[3,72,128]{2,1,0:T(8,128)S(1)}, u32[]{:S(2)}, u32[]{:S(2)}) collective-permute-start(f32[3,72,128]{2,1,0:T(8,128)S(1)} %copy-done.1), channel_id=1, source_target_pairs={{1,0},{2,1},{3,2},{4,3},{5,4},{6,5},{7,6},{8,7},{9,8},{10,9},{11,1... | collective-permute-start | bytes 331784 | tf_op jit(solution)/shard_map/ppermute | solution.py:753
  41.0 40.2 %collective-permute-start.2 = (f32[4,72,128]{2,1,0:T(8,128)S(1)}, f32[4,72,128]{2,1,0:T(8,128)S(1)}, u32[]{:S(2)}, u32[]{:S(2)}) collective-permute-start(f32[4,72,128]{2,1,0:T(8,128)S(1)} %copy-done), channel_id=1, source_target_pairs={{0,1},{1,2},{2,3},{3,4},{4,5},{5,6},{6,7},{7,8},{8,9},{9,10},{10,1... | collective-permute-start | bytes 442376 | tf_op jit(solution)/shard_map/ppermute | solution.py:752
  41.2 10.3 %copy-start.5 = (s32[20]{0:T(128)S(1)}, s32[20]{0:T(128)}, u32[]{:S(2)}) copy-start(s32[20]{0:T(128)} %param.15) | copy-start | bytes 244
  81.7 13.8 %collective-permute-start.6 = (f32[3,72,128]{2,1,0:T(8,128)S(1)}, f32[3,72,128]{2,1,0:T(8,128)S(1)}, u32[]{:S(2)}, u32[]{:S(2)}) collective-permute-start(f32[3,72,128]{2,1,0:T(8,128)S(1)} %get-tuple-element.42), channel_id=1, source_target_pairs={{0,1},{1,2},{2,3},{3,4},{4,5},{5,6},{6,7},{7,8},{8,9},{9,10},{10,1... | collective-permute-start | bytes 331784 | tf_op jit(solution)/shard_map/ppermute | solution.py:752
  82.4 13.2 %collective-permute-start.7 = (f32[3,72,128]{2,1,0:T(8,128)S(1)}, f32[3,72,128]{2,1,0:T(8,128)S(1)}, u32[]{:S(2)}, u32[]{:S(2)}) collective-permute-start(f32[3,72,128]{2,1,0:T(8,128)S(1)} %get-tuple-element.43), channel_id=1, source_target_pairs={{1,0},{2,1},{3,2},{4,3},{5,4},{6,5},{7,6},{8,7},{9,8},{10,9},{11,1... | collective-permute-start | bytes 331784 | tf_op jit(solution)/shard_map/ppermute | solution.py:753
  87.5 4.2 %collective-permute-start.4 = (f32[2,72,128]{2,1,0:T(8,128)S(1)}, f32[2,72,128]{2,1,0:T(8,128)S(1)}, u32[]{:S(2)}, u32[]{:S(2)}) collective-permute-start(f32[2,72,128]{2,1,0:T(8,128)S(1)} %get-tuple-element.40), channel_id=1, source_target_pairs={{0,32},{32,64},{64,96},{96,0},{1,33},{33,65},{65,97},{97,1},{2,34}... | collective-permute-start | bytes 221192 | tf_op jit(solution)/shard_map/ppermute | solution.py:750
  90.3 5.3 %collective-permute-start.5 = (f32[2,72,128]{2,1,0:T(8,128)S(1)}, f32[2,72,128]{2,1,0:T(8,128)S(1)}, u32[]{:S(2)}, u32[]{:S(2)}) collective-permute-start(f32[2,72,128]{2,1,0:T(8,128)S(1)} %get-tuple-element.41), channel_id=1, source_target_pairs={{32,0},{64,32},{96,64},{0,96},{33,1},{65,33},{97,65},{1,97},{34,2}... | collective-permute-start | bytes 221192 | tf_op jit(solution)/shard_map/ppermute | solution.py:751

commit v10 on v8

--- a/solution.py
+++ b/solution.py
@@ -281,7 +281,7 @@
             for s in range(species):
                 v = ref["field_west"][s, 0] if i < 0 else ref["field_east"][s, 0] if i == block else field[s, i]
                 wanted.append(((s, i), v, spread(ref["total"], s * cols + x, rows, t.shape[1] // 4)))
-                if len(wanted) == 2:
+                if len(wanted) == 3:
                     make(wanted)
                     wanted.clear()
         if wanted:
@@ -337,7 +337,7 @@
                 v_n, v_s = jnp.where(last, halo, v_n), jnp.where(first, halo, v_s)
             h = centre * v + e * v_e + w_ * v_w + n * v_n + s_ * v_s
             waiting.append((s, i, mix_parts(h)))
-            if len(waiting) == 2:
+            if len(waiting) == 3:
                 mix(waiting)
                 waiting.clear()
     if waiting:

time: 106 us -> 106 us (level)
  no operation moved by 1% of the time
where the time goes in v10:
time: 106 us
  Pallas kernels  67.5 us (64%)
  starting transfers between devices  26.6 us (25%)
  waiting for transfers between devices  11 us (10%)
    pallas_call x1, Pallas kernels, add_soundings(): pl.pallas_call(functools.partial(add_kernel, cols=cols), out_shape=(jax.S...  24.9 us
    pallas_call x2, Pallas kernels, step(): pl.pallas_call(functools.partial(step_kernel, names=(*given, 'out', *made...  22.1 us
    pallas_call x1, Pallas kernels, pack(): pl.pallas_call(pack_kernel, out_shape=tuple((jax.ShapeDtypeStruct(shape,...  20.1 us
    all_to_all x1, starting transfers between devices, on_device(): lax.all_to_all(sent, ('lat', 'lon'), split_axis=0, concat_axis=0, tiled=T...  10.2 us
    ppermute x2, starting transfers between devices, exchange(): lax.ppermute(west, 'lon', east_way)  8.97 us
    ppermute x2, waiting for transfers between devices, exchange(): lax.ppermute(east, 'lon', west_way)  6.64 us
    ppermute x2, starting transfers between devices, exchange(): lax.ppermute(down, 'lat', south_way)  6.57 us
    ppermute x2, waiting for transfers between devices, exchange(): lax.ppermute(west, 'lon', east_way)  2.32 us
  transfers between devices with their start and end apart: 9, of which 3 were waited for; matrix products, arithmetic and copies ran while one was open for 0% of the time, Pallas kernels for 33%

profile of v10, /device:TPU:30, one launch (start us, length us, event | category | flops | bytes accessed | tf_op | source)
XLA Modules:
  0.0 106.2 jit_solution(12136015976717995600)
XLA Ops:
  0.6 20.1 %shard_map.96 = (f32[128,24,128]{2,1,0:T(8,128)}, f32[4,72,128]{2,1,0:T(8,128)}, f32[3,72,128]{2,1,0:T(8,128)}, f32[4,72,128]{2,1,0:T(8,128)}, f32[3,72,128]{2,1,0:T(8,128)}) custom-call(s32[1,8192]{1,0:T(1,128)} %bitcast.23, f32[20,8192]{1,0:T(8,128)} %values.1, s32[1,8192]{1,0:T(1,128)} %bitcast.24, f32[3,45,72,128]{3,2,1,0:T(8,128)} %bitcast.10, ...), custom_call_target="tpu_custom_call" | custom-call | flops 12884901888 | bytes 7270400 | tf_op jit(solution)/shard_map/pallas_call | solution.py:204
  20.7 0.0 copy-start.2
  20.7 0.0 copy-start.3
  20.7 0.0 copy-start
  20.7 0.0 copy-start.1
  20.7 0.0 copy-start.4
  20.8 10.2 %all-to-all-start = ((f32[128,24,128]{2,1,0:T(8,128)}), f32[128,24,128]{2,1,0:T(8,128)S(1)}, u32[]{:S(2)}, u32[]{:S(2)}) async-start(f32[128,24,128]{2,1,0:T(8,128)} %get-tuple-element.31), calls=%async_computation | async-start | bytes 3145728 | tf_op jit(solution)/shard_map/all_to_all | solution.py:709
  31.0 0.0 copy-done.2
  31.0 3.3 %collective-permute-start.1 = (f32[3,72,128]{2,1,0:T(8,128)S(1)}, f32[3,72,128]{2,1,0:T(8,128)S(1)}, u32[]{:S(2)}, u32[]{:S(2)}) collective-permute-start(f32[3,72,128]{2,1,0:T(8,128)S(1)} %copy-done.2), channel_id=1, source_target_pairs={{32,0},{64,32},{96,64},{0,96},{33,1},{65,33},{97,65},{1,97},{34,2}... | collective-permute-start | bytes 331784 | tf_op jit(solution)/shard_map/ppermute | solution.py:714
  34.3 0.0 copy-done.3
  34.4 0.8 collective-permute-start.3
  35.1 0.0 copy-done
  35.1 0.0 collective-permute-start
  35.1 0.0 copy-done.1
  35.2 5.5 %collective-permute-start.2 = (f32[4,72,128]{2,1,0:T(8,128)S(1)}, f32[4,72,128]{2,1,0:T(8,128)S(1)}, u32[]{:S(2)}, u32[]{:S(2)}) collective-permute-start(f32[4,72,128]{2,1,0:T(8,128)S(1)} %copy-done.1), channel_id=1, source_target_pairs={{0,1},{1,2},{2,3},{3,4},{4,5},{5,6},{6,7},{7,8},{8,9},{9,10},{10,1... | collective-permute-start | bytes 442376 | tf_op jit(solution)/shard_map/ppermute | solution.py:715
  40.7 0.0 copy-done.4
  40.7 0.1 copy.10
  40.8 0.1 pad_maximum_fusion.refs_6_.weights
  40.9 0.0 copy-start.5
  40.9 10.2 %shard_map.95 = (f32[3,45,72,128]{3,2,1,0:T(8,128)}, f32[3,72,128]{2,1,0:T(8,128)S(1)}, f32[3,72,128]{2,1,0:T(8,128)S(1)}, f32[3,72,128]{2,1,0:T(8,128)S(1)}, f32[3,72,128]{2,1,0:T(8,128)S(1)}) custom-call(f32[3,45,72,128]{3,2,1,0:T(8,128)} %bitcast.11, f32[3,45,72,128]{3,2,1,0:T(8,128)} %bitcast.12, f32[3,45,72,128]{3,2,1,0:T(8,128)} %bitcast.13, ...), custom_call_target="tpu_custom_call" | custom-call | flops 537477120 | bytes 14929920 | tf_op jit(solution)/shard_map/pallas_call | solution.py:492
  51.1 0.0 copy-done.5
  51.1 0.1 add_convert_fusion.table.refs_15_
  51.2 2.0 %all-to-all-done.got_at = f32[128,24,128]{2,1,0:T(8,128)S(1)} async-done(((f32[128,24,128]{2,1,0:T(8,128)}), f32[128,24,128]{2,1,0:T(8,128)S(1)}, u32[]{:S(2)}, u32[]{:S(2)}) %all-to-all-start) | async-done | bytes 1572896 | tf_op jit(solution)/shard_map/all_to_all | solution.py:709
  53.2 24.9 %shard_map.97 = (f32[2720,256]{1,0:T(8,128)}, f32[3,72,128]{2,1,0:T(8,128)S(1)}, f32[3,72,128]{2,1,0:T(8,128)S(1)}, f32[3,72,128]{2,1,0:T(8,128)S(1)}, f32[3,72,128]{2,1,0:T(8,128)S(1)}) custom-call(f32[128,24,128]{2,1,0:T(8,128)S(1)} %all-to-all-done.got_at, f32[3,72,128]{2,1,0:T(8,128)S(1)} %get-tuple-element.32.plain_up, ...), custom_call_target="tpu_custom_call" | custom-call | flops 22817013760 | bytes 1572864 | tf_op jit(solution)/shard_map/pallas_call | solution.py:664
  78.1 0.0 collective-permute-done.1.north
  78.1 0.0 collective-permute-done.3.east
  78.1 0.0 collective-permute-done.south.refs_13_
  78.2 0.0 collective-permute-done.2.west.refs_12_
  78.2 0.5 shard_map.98
  78.6 0.1 collective-permute-start.4
  78.7 3.2 %collective-permute-start.5 = (f32[3,72,128]{2,1,0:T(8,128)S(1)}, f32[3,72,128]{2,1,0:T(8,128)S(1)}, u32[]{:S(2)}, u32[]{:S(2)}) collective-permute-start(f32[3,72,128]{2,1,0:T(8,128)S(1)} %get-tuple-element.41), channel_id=1, source_target_pairs={{32,0},{64,32},{96,64},{0,96},{33,1},{65,33},{97,65},{1,97},{34,2}... | collective-permute-start | bytes 331784 | tf_op jit(solution)/shard_map/ppermute | solution.py:714
  82.0 3.4 %collective-permute-start.6 = (f32[3,72,128]{2,1,0:T(8,128)S(1)}, f32[3,72,128]{2,1,0:T(8,128)S(1)}, u32[]{:S(2)}, u32[]{:S(2)}) collective-permute-start(f32[3,72,128]{2,1,0:T(8,128)S(1)} %get-tuple-element.42), channel_id=1, source_target_pairs={{0,1},{1,2},{2,3},{3,4},{4,5},{5,6},{6,7},{7,8},{8,9},{9,10},{10,1... | collective-permute-start | bytes 331784 | tf_op jit(solution)/shard_map/ppermute | solution.py:715
  85.4 0.0 collective-permute-start.7
  85.4 0.0 collective-permute-done.4.refs_8_
  85.4 0.0 collective-permute-done.5.refs_9_
  85.4 2.3 %collective-permute-done.6.refs_10_ = f32[3,72,128]{2,1,0:T(8,128)S(1)} collective-permute-done((f32[3,72,128]{2,1,0:T(8,128)S(1)}, f32[3,72,128]{2,1,0:T(8,128)S(1)}, u32[]{:S(2)}, u32[]{:S(2)}) %collective-permute-start.6) | collective-permute-done | bytes 110624 | tf_op jit(solution)/shard_map/ppermute | solution.py:715
  87.7 6.6 %collective-permute-done.7.refs_11_ = f32[3,72,128]{2,1,0:T(8,128)S(1)} collective-permute-done((f32[3,72,128]{2,1,0:T(8,128)S(1)}, f32[3,72,128]{2,1,0:T(8,128)S(1)}, u32[]{:S(2)}, u32[]{:S(2)}) %collective-permute-start.7) | collective-permute-done | bytes 110624 | tf_op jit(solution)/shard_map/ppermute | solution.py:716
  94.4 11.8 %shard_map.99 = (f32[3,45,72,128]{3,2,1,0:T(8,128)}, f32[3,45,128]{2,1,0:T(8,128)}) custom-call(f32[3,45,72,128]{3,2,1,0:T(8,128)} %get-tuple-element.26.refs_0_.refs_1_.refs_2_, f32[3,45,72,128]{3,2,1,0:T(8,128)} %get-tuple-element.26.refs_0_.refs_1_.refs_2_, f32[3,45,72,128]{3,2,1,0:T(8,128)} %get-tuple-element.26.refs_0_.refs_1_.refs_2_, ...), custom_call_target="tpu_custom_call" | custom-call | flops 537477120 | bytes 14929920 | tf_op jit(solution)/shard_map/pallas_call | solution.py:492
  (2 shorter events, 0.0 us)
Async XLA Ops:
  20.7 10.3 %copy-start.2 = (f32[3,72,128]{2,1,0:T(8,128)S(1)}, f32[3,72,128]{2,1,0:T(8,128)}, u32[]{:S(2)}) copy-start(f32[3,72,128]{2,1,0:T(8,128)} %get-tuple-element.28.down_own) | copy-start | bytes 331780
  20.7 13.6 %copy-start.3 = (f32[3,72,128]{2,1,0:T(8,128)S(1)}, f32[3,72,128]{2,1,0:T(8,128)}, u32[]{:S(2)}) copy-start(f32[3,72,128]{2,1,0:T(8,128)} %get-tuple-element.30.east_own) | copy-start | bytes 331780
  20.7 14.4 %copy-start = (f32[4,72,128]{2,1,0:T(8,128)S(1)}, f32[4,72,128]{2,1,0:T(8,128)}, u32[]{:S(2)}) copy-start(f32[4,72,128]{2,1,0:T(8,128)} %get-tuple-element.27.up_own) | copy-start | bytes 442372
  20.7 14.4 %copy-start.1 = (f32[4,72,128]{2,1,0:T(8,128)S(1)}, f32[4,72,128]{2,1,0:T(8,128)}, u32[]{:S(2)}) copy-start(f32[4,72,128]{2,1,0:T(8,128)} %get-tuple-element.29.west_own) | copy-start | bytes 442372
  20.7 19.9 %copy-start.4 = (f32[72,72]{1,0:T(8,128)S(1)}, f32[72,72]{1,0:T(8,128)}, u32[]{:S(2)}) copy-start(f32[72,72]{1,0:T(8,128)} %param.11) | copy-start | bytes 62212
  20.8 32.5 %all-to-all-start = ((f32[128,24,128]{2,1,0:T(8,128)}), f32[128,24,128]{2,1,0:T(8,128)S(1)}, u32[]{:S(2)}, u32[]{:S(2)}) async-start(f32[128,24,128]{2,1,0:T(8,128)} %get-tuple-element.31), calls=%async_computation | async-start | bytes 3145728 | tf_op jit(solution)/shard_map/all_to_all | solution.py:709
  31.0 47.1 %collective-permute-start.1 = (f32[3,72,128]{2,1,0:T(8,128)S(1)}, f32[3,72,128]{2,1,0:T(8,128)S(1)}, u32[]{:S(2)}, u32[]{:S(2)}) collective-permute-start(f32[3,72,128]{2,1,0:T(8,128)S(1)} %copy-done.2), channel_id=1, source_target_pairs={{32,0},{64,32},{96,64},{0,96},{33,1},{65,33},{97,65},{1,97},{34,2}... | collective-permute-start | bytes 331784 | tf_op jit(solution)/shard_map/ppermute | solution.py:714
  34.4 43.8 %collective-permute-start.3 = (f32[3,72,128]{2,1,0:T(8,128)S(1)}, f32[3,72,128]{2,1,0:T(8,128)S(1)}, u32[]{:S(2)}, u32[]{:S(2)}) collective-permute-start(f32[3,72,128]{2,1,0:T(8,128)S(1)} %copy-done.3), channel_id=1, source_target_pairs={{1,0},{2,1},{3,2},{4,3},{5,4},{6,5},{7,6},{8,7},{9,8},{10,9},{11,1... | collective-permute-start | bytes 331784 | tf_op jit(solution)/shard_map/ppermute | solution.py:716
  35.1 43.0 %collective-permute-start = (f32[4,72,128]{2,1,0:T(8,128)S(1)}, f32[4,72,128]{2,1,0:T(8,128)S(1)}, u32[]{:S(2)}, u32[]{:S(2)}) collective-permute-start(f32[4,72,128]{2,1,0:T(8,128)S(1)} %copy-done), channel_id=1, source_target_pairs={{0,32},{32,64},{64,96},{96,0},{1,33},{33,65},{65,97},{97,1},{2,34}... | collective-permute-start | bytes 442376 | tf_op jit(solution)/shard_map/ppermute | solution.py:713
  35.2 43.0 %collective-permute-start.2 = (f32[4,72,128]{2,1,0:T(8,128)S(1)}, f32[4,72,128]{2,1,0:T(8,128)S(1)}, u32[]{:S(2)}, u32[]{:S(2)}) collective-permute-start(f32[4,72,128]{2,1,0:T(8,128)S(1)} %copy-done.1), channel_id=1, source_target_pairs={{0,1},{1,2},{2,3},{3,4},{4,5},{5,6},{6,7},{7,8},{8,9},{9,10},{10,1... | collective-permute-start | bytes 442376 | tf_op jit(solution)/shard_map/ppermute | solution.py:715
  40.9 10.2 %copy-start.5 = (s32[20]{0:T(128)S(1)}, s32[20]{0:T(128)}, u32[]{:S(2)}) copy-start(s32[20]{0:T(128)} %param.15) | copy-start | bytes 244
  78.6 6.8 %collective-permute-start.4 = (f32[3,72,128]{2,1,0:T(8,128)S(1)}, f32[3,72,128]{2,1,0:T(8,128)S(1)}, u32[]{:S(2)}, u32[]{:S(2)}) collective-permute-start(f32[3,72,128]{2,1,0:T(8,128)S(1)} %get-tuple-element.40), channel_id=1, source_target_pairs={{0,32},{32,64},{64,96},{96,0},{1,33},{33,65},{65,97},{97,1},{2,34}... | collective-permute-start | bytes 331784 | tf_op jit(solution)/shard_map/ppermute | solution.py:713
  78.7 6.7 %collective-permute-start.5 = (f32[3,72,128]{2,1,0:T(8,128)S(1)}, f32[3,72,128]{2,1,0:T(8,128)S(1)}, u32[]{:S(2)}, u32[]{:S(2)}) collective-permute-start(f32[3,72,128]{2,1,0:T(8,128)S(1)} %get-tuple-element.41), channel_id=1, source_target_pairs={{32,0},{64,32},{96,64},{0,96},{33,1},{65,33},{97,65},{1,97},{34,2}... | collective-permute-start | bytes 331784 | tf_op jit(solution)/shard_map/ppermute | solution.py:714
  82.0 5.8 %collective-permute-start.6 = (f32[3,72,128]{2,1,0:T(8,128)S(1)}, f32[3,72,128]{2,1,0:T(8,128)S(1)}, u32[]{:S(2)}, u32[]{:S(2)}) collective-permute-start(f32[3,72,128]{2,1,0:T(8,128)S(1)} %get-tuple-element.42), channel_id=1, source_target_pairs={{0,1},{1,2},{2,3},{3,4},{4,5},{5,6},{6,7},{7,8},{8,9},{9,10},{10,1... | collective-permute-start | bytes 331784 | tf_op jit(solution)/shard_map/ppermute | solution.py:715
  85.4 9.0 %collective-permute-start.7 = (f32[3,72,128]{2,1,0:T(8,128)S(1)}, f32[3,72,128]{2,1,0:T(8,128)S(1)}, u32[]{:S(2)}, u32[]{:S(2)}) collective-permute-start(f32[3,72,128]{2,1,0:T(8,128)S(1)} %get-tuple-element.43), channel_id=1, source_target_pairs={{1,0},{2,1},{3,2},{4,3},{5,4},{6,5},{7,6},{8,7},{9,8},{10,9},{11,1... | collective-permute-start | bytes 331784 | tf_op jit(solution)/shard_map/ppermute | solution.py:716
